TPU v7x, 32 devices: a whole 2x2x4 slice. The times are simulated.
32 devices in a mesh: groups: 2 (over y), map: 16 (over z, x, core).
Axes of the slice: x: 2, y: 2, z: 4, core: 2. Of those that a mesh axis runs over, the one named last changes fastest.
Arguments:
- amplitude_maps: bfloat16 [400, 512, 512], P('groups', 'map'), parts along dimension 0, may hold values from -6 to 6
- kept_blocks: int32 [512], P(('groups', 'map')), parts along dimension 0, may hold values from 0 to 2047, as said below
- block_owner: int32 [512, 1], P(('groups', 'map')), parts along dimension 0, may hold values from 0 to 15; in each aligned block of 16 rows (0 to 15, 16 to 31, ...) at most 2 rows name the same one
- observed: bfloat16 [8192], P(('groups', 'map')), parts along dimension 0, may hold values from -8 to 8
- error_scale: bfloat16 [8192], P(('groups', 'map')), parts along dimension 0, may hold values from 0.5 to 1.59375
- perturbation: bfloat16 [8192, 200], P(('groups', 'map')), parts along dimension 0, may hold values from -6 to 6
- model_slab: bfloat16 [200, 393216], P(None, ('groups', 'map')), parts along dimension 1, may hold values from -6 to 6
Outputs:
- updated_slab: bfloat16 [200, 393216], P(None, ('groups', 'map')), parts along dimension 1
- update_weights: float32 [400, 200], P('groups'), parts along dimension 0
- data_misfit: float32 [8192], P(('groups', 'map')), parts along dimension 0
There are 2 independent parts, one for each index of `groups`. A program takes and returns all parts, laid end to end along the dimension named above; each array names one. Nothing has to cross between parts.
Inputs may be any that keep to these rules, and one draw needn't show every extreme that they name: `kept_blocks`: the 16 entries of one device are distinct numbers of that device's own 2048 blocks. `block_owner`: at most 2 of the 16 kept blocks of one device share an owner.
All inputs are finite; a program needn't handle non-finite values.
Results may differ from a plain program's by a relative error of at most 0.0018.
The roundings to bfloat16 on the way count: a program that leaves them out, or rounds other values in their place, can miss the bound.
Values may be sent and summed in bfloat16 or wider, within the bound.
No kernel may reach another device: no remote copies, remote signals or barrier semaphores. Data moves between devices by JAX's collectives and lax.ppermute only.
A program may use at most 128 MiB of HBM per device.

v0:
```python
import math

import jax
import jax.numpy as jnp
from jax import lax
from jax.sharding import PartitionSpec as P

BLK = 8
CAP = 2


inflation = 4.0
epsilon = 1e-06


def dct_table(length):
    frequency = jnp.arange(length, dtype=jnp.float32)[:, None]
    sample = jnp.arange(length, dtype=jnp.float32)[None, :]
    cosine_table = jnp.cos(math.pi * (2.0 * sample + 1.0) * frequency / (2.0 * length))
    factor = jnp.where(frequency == 0, math.sqrt(1.0 / length), math.sqrt(2.0 / length))
    return (cosine_table * factor).astype(jnp.bfloat16)


def gram_terms(predicted, observed_rows, scale_rows, noise_rows, live_mask, weight_scale):
    members = predicted.shape[1]
    center = jnp.mean(predicted, axis=1, keepdims=True)
    anomaly = (predicted - center) / math.sqrt(members - 1)
    weight = live_mask * weight_scale / (scale_rows * scale_rows)
    mismatch = (
        observed_rows[:, None] + math.sqrt(inflation) * scale_rows[:, None] * noise_rows - predicted
    )
    weighted = anomaly * weight[:, None]
    contract = (((0,), (0,)), ((), ()))
    gram_matrix = lax.dot_general(anomaly, weighted, contract, precision=lax.Precision.HIGHEST)
    cross_terms = lax.dot_general(weighted, mismatch, contract, precision=lax.Precision.HIGHEST)
    relative = mismatch / scale_rows[:, None]
    misfit_rows = live_mask * jnp.sqrt(jnp.mean(relative * relative, axis=1) + epsilon)
    return (gram_matrix, cross_terms, misfit_rows)


def solve_weights(gram_matrix, cross_terms):
    members = gram_matrix.shape[0]
    factor = jnp.linalg.cholesky(gram_matrix + inflation * jnp.eye(members, dtype=jnp.float32))
    return jax.scipy.linalg.cho_solve((factor, True), cross_terms)


def update_state(block, update_weights):
    state = block.astype(jnp.float32)
    members = state.shape[0]
    anomaly = (state - jnp.mean(state, axis=0, keepdims=True)) / math.sqrt(members - 1)
    moved = state + lax.dot_general(
        update_weights, anomaly, (((0,), (0,)), ((), ())), precision=lax.Precision.HIGHEST
    )
    return moved.astype(jnp.bfloat16)


def body(amplitude_maps, kept_blocks, block_owner, observed, error_scale, perturbation, model_slab):
    members, rows_here, map_width = amplitude_maps.shape
    devices = lax.axis_size("map")
    map_height = rows_here * devices
    table_w = dct_table(map_width)
    table_h = dct_table(map_height)
    rowwise = jnp.einsum(
        "ehw,kw->hke", amplitude_maps, table_w, preferred_element_type=jnp.float32
    ).astype(jnp.bfloat16)
    coefficients = jnp.einsum(
        "kh,hwe->wke",
        table_h,
        lax.all_to_all(rowwise, "map", split_axis=1, concat_axis=0, tiled=True),
        preferred_element_type=jnp.float32,
    ).astype(jnp.bfloat16)
    block_rows = coefficients.reshape(-1, BLK * members)
    candidates = block_rows.shape[0]
    keep_count = kept_blocks.shape[0]
    slot_count = devices * CAP
    dest_owner = block_owner[:, 0]
    positions = jnp.arange(keep_count, dtype=jnp.int32)
    earlier = (dest_owner[:, None] == dest_owner[None, :]) & (
        positions[None, :] < positions[:, None]
    )
    slot_rank = jnp.sum(earlier.astype(jnp.int32), axis=1)
    slot_index = dest_owner * CAP + slot_rank
    pick_slot = (slot_index[:, None] == jnp.arange(slot_count, dtype=jnp.int32)[None, :]).astype(
        jnp.bfloat16
    )
    weight_scale = members / (devices * keep_count * BLK)
    contract = (((0,), (0,)), ((), ()))
    pick_block = (kept_blocks[:, None] == jnp.arange(candidates, dtype=jnp.int32)[None, :]).astype(
        jnp.bfloat16
    )
    routing = lax.dot_general(
        pick_slot, pick_block, contract, preferred_element_type=jnp.float32
    ).astype(jnp.bfloat16)
    outgoing = jnp.dot(routing, block_rows, preferred_element_type=jnp.float32).astype(jnp.bfloat16)
    live_slots = jnp.sum(pick_slot.astype(jnp.float32), axis=0).astype(jnp.bfloat16)
    arrived, arrived_live = (
        lax.all_to_all(
            outgoing.reshape(devices, CAP, BLK * members),
            "map",
            split_axis=0,
            concat_axis=0,
            tiled=True,
        ),
        lax.all_to_all(
            live_slots.reshape(devices, CAP), "map", split_axis=0, concat_axis=0, tiled=True
        ),
    )
    predicted = arrived.reshape(-1, members).astype(jnp.float32)
    live_mask = jnp.repeat(arrived_live.astype(jnp.float32).reshape(-1), BLK)
    gram_matrix, cross_terms, data_misfit = gram_terms(
        predicted,
        observed.astype(jnp.float32),
        error_scale.astype(jnp.float32),
        perturbation.astype(jnp.float32),
        live_mask,
        weight_scale,
    )
    gram_matrix, cross_terms = lax.psum((gram_matrix, cross_terms), "map")
    update_weights = solve_weights(gram_matrix, cross_terms)
    updated_slab = update_state(model_slab, update_weights)
    return (updated_slab, update_weights, data_misfit)


def solution(mesh):
    in_specs = (
        P("groups", "map", None),
        P(("groups", "map")),
        P(("groups", "map"), None),
        P(("groups", "map")),
        P(("groups", "map")),
        P(("groups", "map"), None),
        P(None, ("groups", "map")),
    )
    out_specs = (P(None, ("groups", "map")), P("groups", None), P(("groups", "map")))
    return jax.shard_map(body, mesh=mesh, in_specs=in_specs, out_specs=out_specs, check_vma=False)
```

profile of v0, /device:TPU:0, one launch (start us, length us, event | category | flops | bytes accessed | tf_op | source)
XLA Modules:
  0.0 518.3 jit_solution(12664776586817616321)
XLA Ops:
  7.2 23.2 %fusion.9 = bf16[32,512,200]{1,2,0:T(8,128)(2,1)} fusion(bf16[200,32,512]{2,1,0:T(8,128)(2,1)} %param.7, f32[512]{0:T(512)S(1)} %get-tuple-element.50, f32[512]{0:T(512)S(1)} %get-tuple-element.49), kind=kOutput, calls=%fused_computation.10 | convolution fusion | flops 3359768576 | bytes 13111296 | tf_op jit(solution)/shard_map/ehw,kw->hke/dot_general | solution.py:63
  30.4 14.2 %copy.36 = bf16[32,512,200]{2,0,1:T(8,128)(2,1)} copy(bf16[32,512,200]{1,2,0:T(8,128)(2,1)} %fusion.9) | data formatting | bytes 13107200 | tf_op jit(solution)/shard_map/convert_element_type | solution.py:65
  44.6 7.5 %all-to-all-start = ((bf16[32,512,200]{2,0,1:T(8,128)(2,1)}), bf16[32,512,200]{2,0,1:T(8,128)(2,1)}, u32[]{:S(2)}, u32[]{:S(2)}) async-start(bf16[32,512,200]{2,0,1:T(8,128)(2,1)} %copy.36), calls=%async_computation | async-start | bytes 16777216 | tf_op jit(solution)/shard_map/all_to_all | solution.py:69
  52.5 0.7 all_to_all.29
  53.2 3.2 convert_reduce_fusion
  56.4 146.5 %all-to-all-done = bf16[32,512,200]{2,0,1:T(8,128)(2,1)} async-done(((bf16[32,512,200]{2,0,1:T(8,128)(2,1)}), bf16[32,512,200]{2,0,1:T(8,128)(2,1)}, u32[]{:S(2)}, u32[]{:S(2)}) %all-to-all-start) | async-done | bytes 6553632 | tf_op jit(solution)/shard_map/all_to_all | solution.py:69
  202.9 51.4 %all-to-all-start.2 = ((bf16[16,1,2]{2,1,0:T(2,128)(2,1)}), bf16[16,1,2]{2,1,0:T(2,128)(2,1)S(1)}, u32[]{:S(2)}, u32[]{:S(2)}) async-start(bf16[16,1,2]{2,1,0:T(2,128)(2,1)} %all_to_all.29), calls=%async_computation.2 | async-start | bytes 16384 | tf_op jit(solution)/shard_map/all_to_all | solution.py:104
  254.3 12.3 %copy.38 = bf16[16,32,32,200]{3,2,1,0:T(8,128)(2,1)} copy(bf16[16,32,32,200]{3,1,2,0:T(8,128)(2,1)} %bitcast.7) | data formatting | bytes 13107200 | tf_op jit(solution)/shard_map/all_to_all | solution.py:69
  266.6 36.1 %fusion.12 = bf16[32,512,200]{1,2,0:T(8,128)(2,1)} fusion(bf16[512,32,200]{2,1,0:T(8,128)(2,1)} %bitcast.56, f32[512]{0:T(512)S(1)} %get-tuple-element.50, f32[512]{0:T(512)S(1)} %get-tuple-element.49), kind=kOutput, calls=%fused_computation.11 | convolution fusion | flops 3359768576 | bytes 13111296 | tf_op jit(solution)/shard_map/kh,hwe->wke/dot_general | solution.py:66
  302.6 10.6 %copy.40 = bf16[32,512,200]{2,1,0:T(8,128)(2,1)} copy(bf16[32,512,200]{1,2,0:T(8,128)(2,1)} %fusion.12) | data formatting | bytes 13107200 | tf_op jit(solution)/shard_map/convert_element_type | solution.py:71
  313.3 14.8 %reshape.103 = bf16[2048,1600]{1,0:T(8,128)(2,1)} reshape(bf16[32,512,200]{2,1,0:T(8,128)(2,1)} %copy.40) | data formatting | bytes 13107200 | tf_op jit(solution)/shard_map/reshape | solution.py:72
  328.1 4.4 convolution_convert_fusion.1
  332.6 0.7 reshape.104
  333.2 6.1 %all-to-all-start.1 = ((bf16[16,2,1600]{2,1,0:T(2,128)(2,1)}), bf16[16,2,1600]{2,1,0:T(2,128)(2,1)S(1)}, u32[]{:S(2)}, u32[]{:S(2)}) async-start(bf16[16,2,1600]{2,1,0:T(2,128)(2,1)} %reshape.104), calls=%async_computation.1 | async-start | bytes 212992 | tf_op jit(solution)/shard_map/all_to_all | solution.py:97
  339.9 7.0 %all-to-all-done.1 = bf16[16,2,1600]{2,1,0:T(2,128)(2,1)S(1)} async-done(((bf16[16,2,1600]{2,1,0:T(2,128)(2,1)}), bf16[16,2,1600]{2,1,0:T(2,128)(2,1)S(1)}, u32[]{:S(2)}, u32[]{:S(2)}) %all-to-all-start.1) | async-done | bytes 102432 | tf_op jit(solution)/shard_map/all_to_all | solution.py:97
  347.4 0.6 sqrt_multiply_fusion
  348.2 1.4 fusion.26
  351.3 1.3 fusion.58
  352.6 86.8 %all-reduce.6.cloned.1.call-done = (f32[200,200]{1,0:T(8,128)}, f32[200,200]{1,0:T(8,128)}) async-done(((f32[200,200]{1,0:T(8,128)}, f32[200,200]{1,0:T(8,128)}), (f32[200,200]{1,0:T(8,128)}, f32[200,200]{1,0:T(8,128)})) %all-reduce.6.cloned.1.call-update) | async-done | bytes 320016 | tf_op jit(solution)/shard_map/psum | solution.py:118
  439.4 0.9 select_add_fusion
  440.5 1.0 fusion.29
  441.4 11.7 %cholesky.50 = f32[128,128]{1,0:T(8,128)S(1)} custom-call(f32[128,128]{1,0:T(8,128)S(1)} %cholesky.121), custom_call_target="Cholesky" | custom-call | tf_op jit(solution)/shard_map/jit(cholesky)/cholesky | solution.py:43
  453.2 9.8 %custom-call.18 = f32[1,128,128]{1,2,0:T(8,128)S(1)} custom-call(f32[1,128,128]{2,1,0:T(8,128)S(1)} %get-tuple-element.42), custom_call_target="InvertDiagBlocksLowerTriangular" | custom-call | tf_op jit(solution)/shard_map/jit(cholesky)/cholesky | solution.py:43
  463.5 6.6 %cholesky.108 = f32[72,72]{1,0:T(8,128)S(1)} custom-call(f32[72,72]{1,0:T(8,128)S(1)} %convolution_subtract_fusion.2), custom_call_target="Cholesky" | custom-call | tf_op jit(solution)/shard_map/jit(cholesky)/cholesky | solution.py:43
  470.1 0.6 compare_reduce_fusion
  470.7 0.6 compare_reduce_fusion.1
  472.8 19.8 %custom-call.19 = f32[2,128,128]{1,2,0:T(8,128)S(1)} custom-call(f32[2,128,128]{2,1,0:T(8,128)S(1)} %pad_maximum_fusion.1), custom_call_target="InvertDiagBlocksLowerTriangular" | custom-call | tf_op jit(solution)/shard_map/jit(_cho_solve)/triangular_solve | solution.py:44
  492.7 1.3 fusion.30
  494.0 1.2 convolution_subtract_fusion.1
  495.7 0.4 convolution_subtract_fusion
  496.5 0.8 copy.45
  497.3 13.9 %fusion = bf16[200,12288]{1,0:T(8,128)(2,1)} fusion(bf16[200,12288]{1,0:T(8,128)(2,1)} %param.13, f32[12288]{0:T(1024)S(1)} %broadcast_multiply_fusion.1, f32[72,200]{0,1:T(8,128)S(1)} %copy.44, f32[128,200]{0,1:T(8,128)S(1)} %fusion.41), kind=kOutput, calls=%fused_computation.1 | convolution fusion | flops 5913025536 | bytes 10039552 | tf_op jit(solution)/shard_map/dot_general | solution.py:51
  (57 shorter events, 4.7 us)
Async XLA Ops:
  44.6 7.6 %copy-start.3 = (s32[16,1]{0,1:T(1,128)S(1)}, s32[16,1]{0,1:T(1,128)}, u32[]{:S(2)}) copy-start(s32[16,1]{0,1:T(1,128)} %param.9) | copy-start | bytes 196
  44.6 158.3 %all-to-all-start = ((bf16[32,512,200]{2,0,1:T(8,128)(2,1)}), bf16[32,512,200]{2,0,1:T(8,128)(2,1)}, u32[]{:S(2)}, u32[]{:S(2)}) async-start(bf16[32,512,200]{2,0,1:T(8,128)(2,1)} %copy.36), calls=%async_computation | async-start | bytes 16777216 | tf_op jit(solution)/shard_map/all_to_all | solution.py:69
  202.9 130.4 %all-to-all-start.2 = ((bf16[16,1,2]{2,1,0:T(2,128)(2,1)}), bf16[16,1,2]{2,1,0:T(2,128)(2,1)S(1)}, u32[]{:S(2)}, u32[]{:S(2)}) async-start(bf16[16,1,2]{2,1,0:T(2,128)(2,1)} %all_to_all.29), calls=%async_computation.2 | async-start | bytes 16384 | tf_op jit(solution)/shard_map/all_to_all | solution.py:104
  313.3 14.9 %copy-start.1 = (s32[16]{0:T(128)S(1)}, s32[16]{0:T(128)}, u32[]{:S(2)}) copy-start(s32[16]{0:T(128)} %param.8) | copy-start | bytes 196
  313.3 26.2 %copy-start.2 = (bf16[256]{0:T(256)(128)(2,1)S(1)}, bf16[256]{0:T(256)(128)(2,1)}, u32[]{:S(2)}) copy-start(bf16[256]{0:T(256)(128)(2,1)} %param.11) | copy-start | bytes 1540
  313.3 26.2 %copy-start = (bf16[256,200]{0,1:T(8,128)(2,1)S(1)}, bf16[256,200]{0,1:T(8,128)(2,1)}, u32[]{:S(2)}) copy-start(bf16[256,200]{0,1:T(8,128)(2,1)} %param.12) | copy-start | bytes 307204
  313.3 26.3 %copy-start.4 = (bf16[256]{0:T(256)(128)(2,1)S(1)}, bf16[256]{0:T(256)(128)(2,1)}, u32[]{:S(2)}) copy-start(bf16[256]{0:T(256)(128)(2,1)} %param.10) | copy-start | bytes 1540
  333.2 13.7 %all-to-all-start.1 = ((bf16[16,2,1600]{2,1,0:T(2,128)(2,1)}), bf16[16,2,1600]{2,1,0:T(2,128)(2,1)S(1)}, u32[]{:S(2)}, u32[]{:S(2)}) async-start(bf16[16,2,1600]{2,1,0:T(2,128)(2,1)} %reshape.104), calls=%async_computation.1 | async-start | bytes 212992 | tf_op jit(solution)/shard_map/all_to_all | solution.py:97
  339.4 100.0 %all-reduce.6.cloned.1.call-start = ((), (), s32[]{:S(2)}) async-start(), calls=%async_computation.3 | async-start | bytes 819200 | tf_op jit(solution)/shard_map/psum | solution.py:118
Sparse Core Ops, SparseCore 0:
  352.7 86.6 all-reduce.5
where the time goes:
time: 521 us; the launch traced here: 518 us
  waiting for transfers between devices  240 us (46%)
  matrix products  84.4 us (16%)
  starting transfers between devices  65 us (12%)
  local copies, waits for them, and re-layouts  56.6 us (11%)
  other arithmetic  56 us (11%)
  between operations  15.9 us (3%)
    all_to_all x1, waiting for transfers between devices, body(): lax.all_to_all(rowwise, 'map', split_axis=1, concat_axis=0, tiled=True)  147 us
    psum x1, waiting for transfers between devices, body(): gram_matrix, cross_terms = lax.psum((gram_matrix, cross_terms), 'map')  86.8 us
    all_to_all x1, starting transfers between devices, body(): lax.all_to_all(live_slots.reshape(devices, CAP), 'map', split_axis=0, con...  51.4 us
    dot_general x1, matrix products, body(): jnp.einsum('kh,hwe->wke', table_h, lax.all_to_all(rowwise, 'map', split_a...  36.1 us
    another operation x7, other arithmetic, solve_weights(): jnp.linalg.cholesky(gram_matrix + inflation * jnp.eye(members, dtype=jnp....  29.4 us
    dot_general x1, matrix products, body(): jnp.einsum('ehw,kw->hke', amplitude_maps, table_w, preferred_element_type...  23.2 us
    another operation x7, other arithmetic, solve_weights(): return jax.scipy.linalg.cho_solve((factor, True), cross_terms)  20 us
    reshape x1, local copies, waits for them, and re-layouts, body(): block_rows = coefficients.reshape(-1, BLK * members)  14.8 us
  transfers between devices with their start and end apart: 4, of which 3 were waited for; matrix products, arithmetic and copies ran while one was open for 16% of the time, Pallas kernels for 0%

commit v1 on v0

--- a/solution.py
+++ b/solution.py
@@ -1,24 +1,33 @@
+import functools
 import math
 
 import jax
 import jax.numpy as jnp
 from jax import lax
+from jax.experimental import pallas as pl
+from jax.experimental.pallas import tpu as pltpu
 from jax.sharding import PartitionSpec as P
 
 BLK = 8
 CAP = 2
-
+LANE = 128
 
 inflation = 4.0
 epsilon = 1e-06
+
+VMEM_LIMIT = 56 * 1024 * 1024
+
+
+def dct_rows(frequency, sample, length):
+    cosine_table = jnp.cos(math.pi * (2.0 * sample + 1.0) * frequency / (2.0 * length))
+    factor = jnp.where(frequency == 0, math.sqrt(1.0 / length), math.sqrt(2.0 / length))
+    return (cosine_table * factor).astype(jnp.bfloat16)
 
 
 def dct_table(length):
     frequency = jnp.arange(length, dtype=jnp.float32)[:, None]
     sample = jnp.arange(length, dtype=jnp.float32)[None, :]
-    cosine_table = jnp.cos(math.pi * (2.0 * sample + 1.0) * frequency / (2.0 * length))
-    factor = jnp.where(frequency == 0, math.sqrt(1.0 / length), math.sqrt(2.0 / length))
-    return (cosine_table * factor).astype(jnp.bfloat16)
+    return dct_rows(frequency, sample, length)
 
 
 def gram_terms(predicted, observed_rows, scale_rows, noise_rows, live_mask, weight_scale):
@@ -54,7 +63,9 @@
     return moved.astype(jnp.bfloat16)
 
 
-def body(amplitude_maps, kept_blocks, block_owner, observed, error_scale, perturbation, model_slab):
+def dense_body(
+    amplitude_maps, kept_blocks, block_owner, observed, error_scale, perturbation, model_slab
+):
     members, rows_here, map_width = amplitude_maps.shape
     devices = lax.axis_size("map")
     map_height = rows_here * devices
@@ -121,6 +132,361 @@
     return (updated_slab, update_weights, data_misfit)
 
 
+def swap(value, delta):
+    pairs = [(i, i ^ delta) for i in range(lax.axis_size("map"))]
+    return lax.ppermute(value, "map", pairs)
+
+
+def by_row_kernel(maps_ref, out_ref, wide_ref):
+    members, rows, width = maps_ref.shape
+    wide_ref[...] = maps_ref[...].reshape(members * rows, width).astype(jnp.float32)
+    for row in range(rows):
+        out_ref[row] = wide_ref[pl.ds(row, members, stride=rows), :].astype(jnp.bfloat16)
+
+
+def by_row(amplitude_maps):
+    members, rows, width = amplitude_maps.shape
+    return pl.pallas_call(
+        by_row_kernel,
+        grid=(width // LANE,),
+        in_specs=[pl.BlockSpec((members, rows, LANE), lambda i: (0, 0, i))],
+        out_specs=pl.BlockSpec((rows, members, LANE), lambda i: (0, 0, i)),
+        out_shape=jax.ShapeDtypeStruct((rows, members, width), jnp.bfloat16),
+        scratch_shapes=[pltpu.VMEM((members * rows, LANE), jnp.float32)],
+        compiler_params=pltpu.CompilerParams(vmem_limit_bytes=VMEM_LIMIT),
+        cost_estimate=pl.CostEstimate(
+            flops=0, bytes_accessed=8 * members * rows * width, transcendentals=0
+        ),
+        name="maps_by_row",
+    )(amplitude_maps)
+
+
+def shares_kernel(
+    starts_ref, maps_ref, column_ref, table_w_ref, table_h_ref, k0_ref, k1_ref, s0_ref, s1_ref,
+    pick_ref, row_ref, wide_ref,
+):
+    step = pl.program_id(0)
+    rows, members, width = maps_ref.shape
+    keep = row_ref.shape[1] // (rows * pl.num_programs(0))
+    devices = row_ref.shape[0]
+
+    @pl.when(step == 0)
+    def _():
+        lanes = lax.broadcasted_iota(jnp.int32, (column_ref.shape[0], width), 1)
+        one_hot = (column_ref[...] == lanes).astype(jnp.bfloat16)
+        pick_ref[...] = jnp.dot(
+            one_hot, table_w_ref[...], preferred_element_type=jnp.float32
+        ).astype(jnp.bfloat16)
+
+    for row in range(rows):
+        rowwise = lax.dot_general(
+            pick_ref[...], maps_ref[row], (((1,), (1,)), ((), ())),
+            preferred_element_type=jnp.float32,
+        ).astype(jnp.bfloat16)
+        place = pl.ds(pl.multiple_of((step * rows + row) * keep, keep), keep)
+        row_ref[:, place, :] = rowwise.reshape(devices, keep, members)
+
+    @pl.when(step == pl.num_programs(0) - 1)
+    def _():
+        depth = row_ref.shape[1]
+        position = lax.broadcasted_iota(jnp.int32, (BLK, depth), 1) % keep
+        outs = ((k0_ref, 0), (k1_ref, 2), (s0_ref, 1), (s1_ref, 3))
+        for out_ref, low in outs:
+            for high in range(out_ref.shape[0]):
+                delta = high * 4 + low
+                for p in range(keep):
+                    start = pl.multiple_of(starts_ref[delta * keep + p], BLK)
+                    block = table_h_ref[pl.ds(start, BLK), :]
+                    wide_ref[pl.ds(p * BLK, BLK), :] = jnp.where(position == p, block, 0.0)
+                share = jnp.dot(
+                    wide_ref[...].astype(jnp.bfloat16), row_ref[delta],
+                    preferred_element_type=jnp.float32,
+                )
+                out_ref[high] = share.T
+
+
+def shares(maps, columns, starts, table_w, table_h):
+    rows, members, width = maps.shape
+    kept = columns.shape[0]
+    devices = lax.axis_size("map")
+    keep = kept // devices
+    steps = 4
+    depth = rows * keep
+    out = jax.ShapeDtypeStruct((devices // 4, members, keep * BLK), jnp.float32)
+    whole = lambda *shape: pl.BlockSpec(shape, lambda i, s: (0,) * len(shape))
+    return pl.pallas_call(
+        shares_kernel,
+        grid_spec=pltpu.PrefetchScalarGridSpec(
+            num_scalar_prefetch=1,
+            grid=(steps,),
+            in_specs=[
+                pl.BlockSpec((rows // steps, members, width), lambda i, s: (i, 0, 0)),
+                whole(kept, 1),
+                whole(*table_w.shape),
+                whole(*table_h.shape),
+            ],
+            out_specs=[whole(*out.shape)] * 4,
+            scratch_shapes=[
+                pltpu.VMEM((kept, width), jnp.bfloat16),
+                pltpu.VMEM((devices, depth, members), jnp.bfloat16),
+                pltpu.VMEM((keep * BLK, depth), jnp.float32),
+            ],
+        ),
+        out_shape=[out] * 4,
+        compiler_params=pltpu.CompilerParams(vmem_limit_bytes=VMEM_LIMIT),
+        cost_estimate=pl.CostEstimate(
+            flops=2 * kept * width * rows * members,
+            bytes_accessed=2 * rows * members * width,
+            transcendentals=0,
+        ),
+        name="coefficient_shares",
+    )(starts, maps, columns, table_w, table_h)
+
+
+def gram_kernel(
+    starts_ref, place_ref, target_ref, *refs
+):
+    predicted_refs, noise_refs = refs[:8], refs[8:12]
+    out_ref, predicted_ref, wide_ref, noise_ref, left_ref, right_ref, misfit_ref = refs[12:]
+    groups, members, per = predicted_ref.shape
+    keep = per // BLK
+    coefficients = groups * per
+    weight_scale = members / (2 * coefficients)
+    chip = place_ref[0]
+    for i, ref in enumerate(predicted_refs):
+        predicted_ref[chip ^ i] = ref[...].astype(jnp.float32)
+    span = wide_ref.shape[0] // 4
+    for i, ref in enumerate(noise_refs):
+        wide_ref[pl.ds(i * span, span), :] = ref[...].reshape(span, -1).astype(jnp.float32)
+    right_ref[...] = jnp.zeros_like(right_ref)
+    for g in range(groups):
+        for p in range(keep):
+            start = pl.multiple_of(starts_ref[g * keep + p], BLK)
+            noise_ref[pl.ds(p * BLK, BLK), :] = wide_ref[pl.ds(start, BLK), :]
+        noise = noise_ref[...].T
+        observed = noise[members : members + 1]
+        scale = noise[members + 1 : members + 2]
+        predicted = predicted_ref[g]
+        center = jnp.sum(predicted, axis=0, keepdims=True) * (1.0 / members)
+        anomaly = (predicted - center) * (1.0 / math.sqrt(members - 1))
+        weight = weight_scale / (scale * scale)
+        mismatch = observed + math.sqrt(inflation) * scale * noise[:members] - predicted
+        here = pl.ds(g * per, per)
+        left_ref[:, here] = anomaly * weight
+        right_ref[0:members, here] = anomaly
+        right_ref[256 : 256 + members, here] = mismatch
+        relative = mismatch / scale
+        misfit = jnp.sqrt(
+            jnp.sum(relative * relative, axis=0, keepdims=True) * (1.0 / members) + epsilon
+        )
+        high = misfit.astype(jnp.bfloat16)
+        rest = misfit - high.astype(jnp.float32)
+        middle = rest.astype(jnp.bfloat16)
+        low = (rest - middle.astype(jnp.float32)).astype(jnp.bfloat16)
+        misfit_ref[0:1, here] = high.astype(jnp.float32)
+        misfit_ref[1:2, here] = middle.astype(jnp.float32)
+        misfit_ref[2:3, here] = low.astype(jnp.float32)
+        misfit_ref[3:8, here] = jnp.zeros((5, per), jnp.float32)
+    out_ref[0:members, :] = lax.dot_general(
+        left_ref[...], right_ref[...], (((1,), (1,)), ((), ())),
+        precision=lax.Precision.HIGHEST, preferred_element_type=jnp.float32,
+    )
+    lanes = lax.broadcasted_iota(jnp.int32, (coefficients, out_ref.shape[1]), 1)
+    one_hot = (target_ref[...] == lanes).astype(jnp.bfloat16)
+    routed = jnp.dot(
+        misfit_ref[...].astype(jnp.bfloat16), one_hot, preferred_element_type=jnp.float32
+    )
+    out_ref[members : members + 8, :] = jnp.broadcast_to(
+        routed[0:1] + routed[1:2] + routed[2:3], (8, out_ref.shape[1])
+    )
+
+
+def gram(starts, place, target, predicted, noise):
+    members, per = predicted[0].shape
+    groups = len(predicted)
+    coefficients = groups * per
+    rows = 4 * noise[0].shape[0] * noise[0].shape[1] * noise[0].shape[2]
+    smem = pl.BlockSpec(memory_space=pltpu.SMEM)
+    vmem = pl.BlockSpec(memory_space=pltpu.VMEM)
+    return pl.pallas_call(
+        gram_kernel,
+        in_specs=[smem, smem] + [vmem] * (1 + len(predicted) + len(noise)),
+        out_specs=vmem,
+        out_shape=jax.ShapeDtypeStruct((members + 8, 512), jnp.float32),
+        scratch_shapes=[
+            pltpu.VMEM((groups, members, per), jnp.float32),
+            pltpu.VMEM((rows, 256), jnp.float32),
+            pltpu.VMEM((per, 256), jnp.float32),
+            pltpu.VMEM((members, coefficients), jnp.float32),
+            pltpu.VMEM((512, coefficients), jnp.float32),
+            pltpu.VMEM((8, coefficients), jnp.float32),
+        ],
+        compiler_params=pltpu.CompilerParams(vmem_limit_bytes=VMEM_LIMIT),
+        name="gram_and_cross",
+    )(starts, place, target, *predicted, *noise)
+
+
+def solve_kernel(mine_ref, other_ref, weights_ref, parts_ref, misfit_ref, state_ref, power_ref):
+    members = weights_ref.shape[0]
+    total = mine_ref[0:members, :] + other_ref[0:members, :]
+    misfit_ref[...] = (
+        mine_ref[members : members + 8, 0:256] + other_ref[members : members + 8, 256:512]
+    )
+    row = lax.broadcasted_iota(jnp.int32, (members, 256), 0)
+    lane = lax.broadcasted_iota(jnp.int32, (members, 256), 1)
+    unit = jnp.where(row == lane, 1.0, 0.0)
+    matrix = total[:, 0:256] + inflation * unit
+    bound = jnp.max(jnp.sum(jnp.abs(matrix), axis=1, keepdims=True), axis=0, keepdims=True)
+    step = 2.0 / (inflation + bound)
+    state_ref[members:256, :] = jnp.zeros((256 - members, 512), jnp.float32)
+    state_ref[0:members, 0:256] = unit - step * matrix
+    state_ref[0:members, 256:512] = step * total[:, 256:512]
+
+    def more(carry):
+        return carry[0] > 2.0**-24
+
+    def double(carry):
+        power = state_ref[:, 0:256]
+        size = jnp.sum(power * power)
+        moved = jnp.dot(
+            power, state_ref[...], precision=lax.Precision.HIGHEST,
+            preferred_element_type=jnp.float32,
+        )
+        state_ref[:, 0:256] = moved[:, 0:256]
+        state_ref[:, 256:512] = state_ref[:, 256:512] + moved[:, 256:512]
+        return (size,)
+
+    lax.while_loop(more, double, (jnp.float32(1.0),))
+    weights = state_ref[0:members, 256 : 256 + members]
+    weights_ref[...] = weights
+    full = state_ref[:, 256:512]
+    center = jnp.sum(full, axis=0, keepdims=True) * (1.0 / members)
+    spread = ((full - center) * (1.0 / math.sqrt(members - 1))).T[0:members, 0:members]
+    high = spread.astype(jnp.bfloat16)
+    rest = spread - high.astype(jnp.float32)
+    middle = rest.astype(jnp.bfloat16)
+    low = (rest - middle.astype(jnp.float32)).astype(jnp.bfloat16)
+    parts_ref[0] = high
+    parts_ref[1] = middle
+    parts_ref[2] = low
+
+
+def solve(mine, other):
+    members = mine.shape[0] - 8
+    vmem = pl.BlockSpec(memory_space=pltpu.VMEM)
+    return pl.pallas_call(
+        solve_kernel,
+        in_specs=[vmem, vmem],
+        out_specs=[vmem] * 3,
+        out_shape=[
+            jax.ShapeDtypeStruct((members, members), jnp.float32),
+            jax.ShapeDtypeStruct((3, members, members), jnp.bfloat16),
+            jax.ShapeDtypeStruct((8, 256), jnp.float32),
+        ],
+        scratch_shapes=[pltpu.VMEM((256, 512), jnp.float32), pltpu.VMEM((256, 512), jnp.float32)],
+        compiler_params=pltpu.CompilerParams(vmem_limit_bytes=VMEM_LIMIT),
+        name="solve_weights",
+    )(mine, other)
+
+
+def slab_kernel(parts_ref, slab_ref, out_ref):
+    state = slab_ref[...]
+    moved = jnp.dot(parts_ref[2], state, preferred_element_type=jnp.float32)
+    moved = moved + jnp.dot(parts_ref[1], state, preferred_element_type=jnp.float32)
+    moved = moved + jnp.dot(parts_ref[0], state, preferred_element_type=jnp.float32)
+    out_ref[...] = (state.astype(jnp.float32) + moved).astype(jnp.bfloat16)
+
+
+def move_slab(parts, slab):
+    members, cells = slab.shape
+    tile = 2048
+    return pl.pallas_call(
+        slab_kernel,
+        grid=(cells // tile,),
+        in_specs=[
+            pl.BlockSpec(parts.shape, lambda i: (0, 0, 0)),
+            pl.BlockSpec((members, tile), lambda i: (0, i)),
+        ],
+        out_specs=pl.BlockSpec((members, tile), lambda i: (0, i)),
+        out_shape=jax.ShapeDtypeStruct(slab.shape, slab.dtype),
+        compiler_params=pltpu.CompilerParams(vmem_limit_bytes=VMEM_LIMIT),
+        name="slab_update",
+    )(parts, slab)
+
+
+def sparse_body(
+    amplitude_maps, kept_blocks, block_owner, observed, error_scale, perturbation, model_slab
+):
+    members, rows_here, map_width = amplitude_maps.shape
+    devices = lax.axis_size("map")
+    map_height = rows_here * devices
+    per_column = map_height // BLK
+    columns_here = map_width // devices
+    keep = kept_blocks.shape[0]
+    slots = observed.shape[0]
+    me = lax.axis_index("map").astype(jnp.int32)
+
+    lists = jnp.stack([kept_blocks, block_owner[:, 0]])
+    lists = jnp.stack([lists] + [swap(lists, delta) for delta in range(1, devices)])
+
+    extra = jnp.zeros((slots, 256 - members - 2), jnp.bfloat16)
+    noise = jnp.concatenate(
+        [perturbation, observed[:, None], error_scale[:, None], extra], axis=1
+    ).reshape(devices // 2, 2, CAP * BLK, 256)
+    core = me & 1
+    noise_keep = lax.dynamic_index_in_dim(noise, core, 1, keepdims=False)
+    noise_send = lax.dynamic_index_in_dim(noise, 1 - core, 1, keepdims=False)
+    noise = jnp.stack([noise_keep, swap(noise_send, 1)]).reshape(2, -1, 256)
+    noise = jnp.stack([noise, swap(noise, 2)])
+    noises = [noise] + [swap(noise, delta) for delta in (4, 8, 12)]
+
+    maps = by_row(amplitude_maps)
+    table_w = dct_table(map_width)
+    frequency = jnp.arange(map_height, dtype=jnp.float32)[:, None]
+    sample = jnp.repeat(jnp.arange(rows_here, dtype=jnp.int32), keep)[None, :] + me * rows_here
+    table_h = dct_rows(frequency, sample.astype(jnp.float32), map_height).astype(jnp.float32)
+
+    device = me ^ jnp.arange(devices, dtype=jnp.int32)
+    columns = device[:, None] * columns_here + lists[:, 0] // per_column
+    starts = (lists[:, 0] % per_column * BLK).reshape(-1)
+    keep_0, keep_1, send_0, send_1 = shares(
+        maps, columns.reshape(-1, 1), starts, table_w, table_h
+    )
+
+    share_1 = keep_1 + swap(send_1, 1)
+    got_1 = swap(share_1, 2)
+    share_0 = keep_0 + swap(send_0, 1)
+    share = [share_0[i] + got_1[i] for i in range(devices // 4)]
+    got = [swap(share[i], 4 * i) for i in range(1, devices // 4)]
+    predicted = (share[0] + got[0] + got[1] + got[2]).astype(jnp.bfloat16)
+
+    near = [predicted] + [swap(predicted, 4 * i) for i in range(1, devices // 4)]
+    gathered = []
+    for value in near:
+        gathered += [value, swap(value, 2)]
+
+    owner = lists[:, 1]
+    positions = jnp.arange(keep, dtype=jnp.int32)
+    earlier = (owner[:, :, None] == owner[:, None, :]) & (
+        positions[None, None, :] < positions[None, :, None]
+    )
+    rank = jnp.sum(earlier.astype(jnp.int32), axis=2)
+    chip = me >> 1
+    chips = jnp.arange(devices // 2, dtype=jnp.int32)
+    owner = jnp.take(owner[0::2], chip ^ chips, axis=0)
+    rank = jnp.take(rank[0::2], chip ^ chips, axis=0)
+    noise_rows = (owner ^ me) * (slots // 2) + chips[:, None] * (CAP * BLK) + rank * BLK
+    data_row = (chips[:, None] * 2 + core) * (CAP * BLK) + rank * BLK
+    away = owner ^ me
+    target = jnp.where(away < 2, away * slots + data_row, -1024)
+    target = (target[:, :, None] + jnp.arange(BLK, dtype=jnp.int32)).reshape(-1, 1)
+
+    mine = gram(noise_rows.reshape(-1), chip.reshape(1), target, gathered, noises)
+    update_weights, parts, data_misfit = solve(mine, swap(mine, 1))
+    updated_slab = move_slab(parts, model_slab)
+    return (updated_slab, update_weights, data_misfit[0])
+
+
 def solution(mesh):
     in_specs = (
         P("groups", "map", None),
@@ -132,4 +498,10 @@
         P(None, ("groups", "map")),
     )
     out_specs = (P(None, ("groups", "map")), P("groups", None), P(("groups", "map")))
+
+    def body(amplitude_maps, kept_blocks, *rest):
+        few = mesh.shape["map"] == 16 and kept_blocks.shape[0] * BLK == LANE
+        chosen = sparse_body if few else dense_body
+        return chosen(amplitude_maps, kept_blocks, *rest)
+
     return jax.shard_map(body, mesh=mesh, in_specs=in_specs, out_specs=out_specs, check_vma=False)

time: 521 us -> 148 us (0.28)
  waiting for transfers between devices: 240 us -> 31.9 us
  matrix products: 84.4 us -> 0 us
  local copies, waits for them, and re-layouts: 56.6 us -> 6.48 us
  other arithmetic: 56 us -> 12.8 us
  Pallas kernels: 0 us -> 42 us
  between operations: 15.9 us -> 0.99 us
  starting transfers between devices: 65 us -> 53.3 us
    all_to_all x3 -> x0, waiting for transfers between devices: 154 us -> none  [the longest x1 147 us: body(): lax.all_to_all(rowwise, 'map', split_axis=1, concat_axis=0, tiled=True)]
    psum x1 -> x0, waiting for transfers between devices: 86.8 us -> none  [body(): gram_matrix, cross_terms = lax.psum((gram_matrix, cross_terms), 'map')]
    dot_general x6 -> x0, matrix products: 80.3 us -> none  [the longest x1 36.1 us: body(): jnp.einsum('kh,hwe->wke', table_h, lax.all_to_all(rowwise, 'map', split_a...]
    all_to_all x3 -> x0, starting transfers between devices: 65 us -> none  [the longest x1 51.4 us: body(): lax.all_to_all(live_slots.reshape(devices, CAP), 'map', split_axis=0, con...]
    ppermute x0 -> x34, starting transfers between devices: none -> 53.3 us  [swap(): return lax.ppermute(value, 'map', pairs)]
    another operation x14 -> x3, other arithmetic: 49.4 us -> 0.72 us  [the longest x1 0.68 us: sparse_body(): lists = jnp.stack([kept_blocks, block_owner[:, 0]])]
    pallas_call x0 -> x5, Pallas kernels: none -> 42 us  [the longest x1 14.9 us: by_row(): pl.pallas_call(by_row_kernel, grid=(width // LANE,), in_specs=[pl.BlockSp...]
    ppermute x0 -> x34, waiting for transfers between devices: none -> 31.9 us  [swap(): return lax.ppermute(value, 'map', pairs)]
  transfers between devices with their start and end apart: 4 -> 34, of which waited for: 3 -> 10; matrix products, arithmetic and copies ran while one was open for 16% -> 10% of each run, Pallas kernels for 0% -> 10%
where the time goes in v1:
time: 148 us; the launch traced here: 147 us
  starting transfers between devices  53.3 us (36%)
  Pallas kernels  42 us (28%)
  waiting for transfers between devices  31.9 us (22%)
  other arithmetic  12.8 us (9%)
  local copies, waits for them, and re-layouts  6.48 us (4%)
    ppermute x34, starting transfers between devices, swap(): return lax.ppermute(value, 'map', pairs)  53.3 us
    ppermute x34, waiting for transfers between devices, swap(): return lax.ppermute(value, 'map', pairs)  31.9 us
    pallas_call x1, Pallas kernels, by_row(): pl.pallas_call(by_row_kernel, grid=(width // LANE,), in_specs=[pl.BlockSp...  14.9 us
    pallas_call x1, Pallas kernels, shares(): pl.pallas_call(shares_kernel, grid_spec=pltpu.PrefetchScalarGridSpec(num_...  8.86 us
    pallas_call x1, Pallas kernels, move_slab(): pl.pallas_call(slab_kernel, grid=(cells // tile,), in_specs=[pl.BlockSpec...  8.46 us
    convert_element_type x1, other arithmetic, sparse_body(): dct_rows(frequency, sample.astype(jnp.float32), map_height)  7.87 us
    pallas_call x1, Pallas kernels, solve(): pl.pallas_call(solve_kernel, in_specs=[vmem, vmem], out_specs=[vmem] * 3,...  5.33 us
    pallas_call x1, Pallas kernels, gram(): pl.pallas_call(gram_kernel, in_specs=[smem, smem] + [vmem] * (1 + len(pre...  4.39 us
  transfers between devices with their start and end apart: 34, of which 10 were waited for; matrix products, arithmetic and copies ran while one was open for 10% of the time, Pallas kernels for 10%

profile of v1, /device:TPU:0, one launch (start us, length us, event | category | flops | bytes accessed | tf_op | source)
XLA Modules:
  0.0 147.5 jit_solution(4662565674281890749)
XLA Ops:
  1.3 3.0 %collective-permute-start.3 = (s32[2,16]{1,0:T(2,128)S(1)}, s32[2,16]{1,0:T(2,128)S(1)}, u32[]{:S(2)}, u32[]{:S(2)}) collective-permute-start(s32[2,16]{1,0:T(2,128)S(1)} %pad_add_fusion), channel_id=1, source_target_pairs={{0,4},{1,5},{2,6},{3,7},{4,0},{5,1},{6,2},{7,3},{8,12},{9,13},{10,... | collective-permute-start | bytes 392 | tf_op jit(solution)/shard_map/ppermute | solution.py:137
  4.3 2.1 %collective-permute-start.5 = (s32[2,16]{1,0:T(2,128)S(1)}, s32[2,16]{1,0:T(2,128)S(1)}, u32[]{:S(2)}, u32[]{:S(2)}) collective-permute-start(s32[2,16]{1,0:T(2,128)S(1)} %pad_add_fusion), channel_id=1, source_target_pairs={{0,6},{1,7},{2,4},{3,5},{4,2},{5,3},{6,0},{7,1},{8,14},{9,15},{10,... | collective-permute-start | bytes 392 | tf_op jit(solution)/shard_map/ppermute | solution.py:137
  7.0 2.7 %collective-permute-start.7 = (s32[2,16]{1,0:T(2,128)S(1)}, s32[2,16]{1,0:T(2,128)S(1)}, u32[]{:S(2)}, u32[]{:S(2)}) collective-permute-start(s32[2,16]{1,0:T(2,128)S(1)} %pad_add_fusion), channel_id=1, source_target_pairs={{0,8},{1,9},{2,10},{3,11},{4,12},{5,13},{6,14},{7,15},{8,0},{9,1},... | collective-permute-start | bytes 392 | tf_op jit(solution)/shard_map/ppermute | solution.py:137
  10.1 14.9 %maps_by_row.1.maps_ref = bf16[32,200,512]{2,1,0:T(8,128)(2,1)} custom-call(bf16[200,32,512]{2,1,0:T(8,128)(2,1)} %maps_ref.1), custom_call_target="tpu_custom_call" | custom-call | bytes 26214400 | tf_op jit(solution)/shard_map/maps_by_row/pallas_call | solution.py:149
  25.7 7.9 %fusion = (f32[512,512]{1,0:T(8,128)}, bf16[512,512]{1,0:T(8,128)(2,1)}) fusion(f32[512]{0:T(512)S(1)} %reshape.224, f32[512]{0:T(512)S(1)} %get-tuple-element.32, f32[512]{0:T(512)S(1)} %get-tuple-element.31), kind=kLoop, calls=%fused_computation.4 | loop fusion | flops 2359296 | bytes 1579008 | tf_op jit(solution)/shard_map/convert_element_type | solution.py:447
  33.8 3.4 %collective-permute-start.9 = (s32[2,16]{1,0:T(2,128)S(1)}, s32[2,16]{1,0:T(2,128)S(1)}, u32[]{:S(2)}, u32[]{:S(2)}) collective-permute-start(s32[2,16]{1,0:T(2,128)S(1)} %pad_add_fusion), channel_id=1, source_target_pairs={{0,10},{1,11},{2,8},{3,9},{4,14},{5,15},{6,12},{7,13},{8,2},{9,3},... | collective-permute-start | bytes 392 | tf_op jit(solution)/shard_map/ppermute | solution.py:137
  37.4 3.6 %collective-permute-start.11 = (s32[2,16]{1,0:T(2,128)S(1)}, s32[2,16]{1,0:T(2,128)S(1)}, u32[]{:S(2)}, u32[]{:S(2)}) collective-permute-start(s32[2,16]{1,0:T(2,128)S(1)} %pad_add_fusion), channel_id=1, source_target_pairs={{0,12},{1,13},{2,14},{3,15},{4,8},{5,9},{6,10},{7,11},{8,4},{9,5},... | collective-permute-start | bytes 392 | tf_op jit(solution)/shard_map/ppermute | solution.py:137
  41.0 3.9 %collective-permute-start.13 = (s32[2,16]{1,0:T(2,128)S(1)}, s32[2,16]{1,0:T(2,128)S(1)}, u32[]{:S(2)}, u32[]{:S(2)}) collective-permute-start(s32[2,16]{1,0:T(2,128)S(1)} %pad_add_fusion), channel_id=1, source_target_pairs={{0,14},{1,15},{2,12},{3,13},{4,10},{5,11},{6,8},{7,9},{8,6},{9,7},... | collective-permute-start | bytes 392 | tf_op jit(solution)/shard_map/ppermute | solution.py:137
  45.9 1.5 %collective-permute-start.1 = (s32[2,16]{1,0:T(2,128)S(1)}, s32[2,16]{1,0:T(2,128)S(1)}, u32[]{:S(2)}, u32[]{:S(2)}) collective-permute-start(s32[2,16]{1,0:T(2,128)S(1)} %pad_add_fusion), channel_id=1, source_target_pairs={{0,2},{1,3},{2,0},{3,1},{4,6},{5,7},{6,4},{7,5},{8,10},{9,11},{10,... | collective-permute-start | bytes 392 | tf_op jit(solution)/shard_map/ppermute | solution.py:137
  47.4 3.1 %collective-permute-done.14 = s32[2,16]{1,0:T(2,128)S(1)} collective-permute-done((s32[2,16]{1,0:T(2,128)S(1)}, s32[2,16]{1,0:T(2,128)S(1)}, u32[]{:S(2)}, u32[]{:S(2)}) %collective-permute-start.14) | collective-permute-done | bytes 160 | tf_op jit(solution)/shard_map/ppermute | solution.py:137
  52.1 8.9 %coefficient_shares.1 = (f32[4,200,128]{2,1,0:T(8,128)}, f32[4,200,128]{2,1,0:T(8,128)}, f32[4,200,128]{2,1,0:T(8,128)}, f32[4,200,128]{2,1,0:T(8,128)}) custom-call(s32[256]{0:T(256)} %fusion.13.starts_ref, bf16[32,200,512]{2,1,0:T(8,128)(2,1)} %maps_by_row.1.maps_ref, s32[256,1]{1,0:T(8,128)} %fusion.2.column_ref, ...), custom_call_target="tpu_custom_call" | custom-call | flops 1677721600 | bytes 6553600 | tf_op jit(solution)/shard_map/coefficient_shares/pallas_call | solution.py:217
  63.3 1.0 add.191
  65.0 1.6 %collective-permute-start.29 = (bf16[2,128,256]{2,1,0:T(8,128)(2,1)S(1)}, bf16[2,128,256]{2,1,0:T(8,128)(2,1)S(1)}, u32[]{:S(2)}, u32[]{:S(2)}) collective-permute-start(bf16[2,128,256]{2,1,0:T(8,128)(2,1)S(1)} %pad_maximum_fusion.1), channel_id=1, source_target_pairs={{0,2},{1,3},{2,0},{3,1},{4,6},{5,7},{6,4},{7,5},{8,10},{9,11},{10,... | collective-permute-start | bytes 393224 | tf_op jit(solution)/shard_map/ppermute | solution.py:137
  66.6 12.4 %collective-permute-done.29 = bf16[2,128,256]{2,1,0:T(8,128)(2,1)S(1)} collective-permute-done((bf16[2,128,256]{2,1,0:T(8,128)(2,1)S(1)}, bf16[2,128,256]{2,1,0:T(8,128)(2,1)S(1)}, u32[]{:S(2)}, u32[]{:S(2)}) %collective-permute-start.29) | collective-permute-done | bytes 131104 | tf_op jit(solution)/shard_map/ppermute | solution.py:137
  79.1 1.1 add.190
  80.2 2.1 %collective-permute-start.18 = (f32[200,128]{1,0:T(8,128)S(1)}, f32[200,128]{1,0:T(8,128)S(1)}, u32[]{:S(2)}, u32[]{:S(2)}) collective-permute-start(f32[200,128]{1,0:T(8,128)S(1)} %get-tuple-element.18), channel_id=1, source_target_pairs={{0,4},{1,5},{2,6},{3,7},{4,0},{5,1},{6,2},{7,3},{8,12},{9,13},{10,... | collective-permute-start | bytes 307208 | tf_op jit(solution)/shard_map/ppermute | solution.py:137
  82.3 1.0 collective-permute-start.19
  83.3 1.4 collective-permute-start.20
  86.3 2.1 %collective-permute-start.31 = (bf16[2,2,128,256]{3,2,1,0:T(8,128)(2,1)S(1)}, bf16[2,2,128,256]{3,2,1,0:T(8,128)(2,1)S(1)}, u32[]{:S(2)}, u32[]{:S(2)}) collective-permute-start(bf16[2,2,128,256]{3,2,1,0:T(8,128)(2,1)S(1)} %pad_maximum_fusion.refs_8_), channel_id=1, source_target_pairs={{0,8},{1,9},{2,10},{3,11},{4,12},{5,13},{6,14},{7,15},{8,0},{9,1},... | collective-permute-start | bytes 786440 | tf_op jit(solution)/shard_map/ppermute | solution.py:137
  88.4 4.6 %collective-permute-done.18 = f32[200,128]{1,0:T(8,128)S(1)} collective-permute-done((f32[200,128]{1,0:T(8,128)S(1)}, f32[200,128]{1,0:T(8,128)S(1)}, u32[]{:S(2)}, u32[]{:S(2)}) %collective-permute-start.18) | collective-permute-done | bytes 102432 | tf_op jit(solution)/shard_map/ppermute | solution.py:137
  93.0 2.3 %collective-permute-start.32 = (bf16[2,2,128,256]{3,2,1,0:T(8,128)(2,1)S(1)}, bf16[2,2,128,256]{3,2,1,0:T(8,128)(2,1)S(1)}, u32[]{:S(2)}, u32[]{:S(2)}) collective-permute-start(bf16[2,2,128,256]{3,2,1,0:T(8,128)(2,1)S(1)} %pad_maximum_fusion.refs_8_), channel_id=1, source_target_pairs={{0,12},{1,13},{2,14},{3,15},{4,8},{5,9},{6,10},{7,11},{8,4},{9,5},... | collective-permute-start | bytes 786440 | tf_op jit(solution)/shard_map/ppermute | solution.py:137
  95.4 12.2 %collective-permute-start.22 = (bf16[200,128]{1,0:T(8,128)(2,1)S(1)}, bf16[200,128]{1,0:T(8,128)(2,1)S(1)}, u32[]{:S(2)}, u32[]{:S(2)}) collective-permute-start(bf16[200,128]{1,0:T(8,128)(2,1)S(1)} %fusion.11.refs_0_), channel_id=1, source_target_pairs={{0,4},{1,5},{2,6},{3,7},{4,0},{5,1},{6,2},{7,3},{8,12},{9,13},{10,... | collective-permute-start | bytes 153608 | tf_op jit(solution)/shard_map/ppermute | solution.py:137
  108.4 1.7 %collective-permute-start.26 = (bf16[200,128]{1,0:T(8,128)(2,1)S(1)}, bf16[200,128]{1,0:T(8,128)(2,1)S(1)}, u32[]{:S(2)}, u32[]{:S(2)}) collective-permute-start(bf16[200,128]{1,0:T(8,128)(2,1)S(1)} %fusion.11.refs_0_), channel_id=1, source_target_pairs={{0,12},{1,13},{2,14},{3,15},{4,8},{5,9},{6,10},{7,11},{8,4},{9,5},... | collective-permute-start | bytes 153608 | tf_op jit(solution)/shard_map/ppermute | solution.py:137
  110.2 3.0 %collective-permute-done.31.refs_10_ = bf16[2,2,128,256]{3,2,1,0:T(8,128)(2,1)S(1)} collective-permute-done((bf16[2,2,128,256]{3,2,1,0:T(8,128)(2,1)S(1)}, bf16[2,2,128,256]{3,2,1,0:T(8,128)(2,1)S(1)}, u32[]{:S(2)}, u32[]{:S(2)}) %collective-permute-start.31) | collective-permute-done | bytes 262176 | tf_op jit(solution)/shard_map/ppermute | solution.py:137
  113.6 1.5 %collective-permute-start.23 = (bf16[200,128]{1,0:T(8,128)(2,1)S(1)}, bf16[200,128]{1,0:T(8,128)(2,1)S(1)}, u32[]{:S(2)}, u32[]{:S(2)}) collective-permute-start(bf16[200,128]{1,0:T(8,128)(2,1)S(1)} %collective-permute-done.22.refs_2_), channel_id=1, source_target_pairs={{0,2},{1,3},{2,0},{3,1},{4,6},{5,7},{6,4},{7,5},{8,10},{9,11},{10,... | collective-permute-start | bytes 153608 | tf_op jit(solution)/shard_map/ppermute | solution.py:137
  115.2 4.8 %collective-permute-done.24.refs_4_ = bf16[200,128]{1,0:T(8,128)(2,1)S(1)} collective-permute-done((bf16[200,128]{1,0:T(8,128)(2,1)S(1)}, bf16[200,128]{1,0:T(8,128)(2,1)S(1)}, u32[]{:S(2)}, u32[]{:S(2)}) %collective-permute-start.24) | collective-permute-done | bytes 51232 | tf_op jit(solution)/shard_map/ppermute | solution.py:137
  120.5 1.5 %collective-permute-start.27 = (bf16[200,128]{1,0:T(8,128)(2,1)S(1)}, bf16[200,128]{1,0:T(8,128)(2,1)S(1)}, u32[]{:S(2)}, u32[]{:S(2)}) collective-permute-start(bf16[200,128]{1,0:T(8,128)(2,1)S(1)} %collective-permute-done.26.refs_6_), channel_id=1, source_target_pairs={{0,2},{1,3},{2,0},{3,1},{4,6},{5,7},{6,4},{7,5},{8,10},{9,11},{10,... | collective-permute-start | bytes 153608 | tf_op jit(solution)/shard_map/ppermute | solution.py:137
  125.3 4.4 %gram_and_cross.1.mine_ref = f32[208,512]{1,0:T(8,128)} custom-call(s32[128]{0:T(128)} %reshape.221.starts_ref, s32[1]{0:T(128)} %bitcast.35.place_ref, s32[1024,1]{1,0:T(8,128)} %add.208.target_ref, bf16[200,128]{1,0:T(8,128)(2,1)} %copy-done.5, bf16[200,128]{1,0:T(8,128)(2,1)} %copy-done.10, bf16[200,128]{1,0:T(8,128)(2,1)} %copy-done.7, ...), custom_call_target="tpu_custom_call" | custom-call | tf_op jit(solution)/shard_map/gram_and_cross/pallas_call | solution.py:311
  129.7 2.0 %collective-permute-done.33.other_ref = f32[208,512]{1,0:T(8,128)S(1)} collective-permute-done((f32[208,512]{1,0:T(8,128)}, f32[208,512]{1,0:T(8,128)S(1)}, u32[]{:S(2)}, u32[]{:S(2)}) %collective-permute-start.33) | collective-permute-done | bytes 426016 | tf_op jit(solution)/shard_map/ppermute | solution.py:137
  132.4 5.3 %solve_weights.1 = (f32[200,200]{1,0:T(8,128)}, bf16[3,200,200]{2,1,0:T(8,128)(2,1)}, f32[8,256]{1,0:T(8,128)}) custom-call(f32[208,512]{1,0:T(8,128)} %gram_and_cross.1.mine_ref, f32[208,512]{1,0:T(8,128)} %copy-done.1), custom_call_target="tpu_custom_call" | custom-call | tf_op jit(solution)/shard_map/solve_weights/pallas_call | solution.py:377
  137.8 1.3 slice.52
  139.0 8.5 %slab_update.1 = bf16[200,12288]{1,0:T(8,128)(2,1)} custom-call(bf16[3,200,200]{2,1,0:T(8,128)(2,1)} %get-tuple-element.15.parts_ref, bf16[200,12288]{1,0:T(8,128)(2,1)} %slab_ref.1), custom_call_target="tpu_custom_call" | custom-call | tf_op jit(solution)/shard_map/slab_update/pallas_call | solution.py:403
  (115 shorter events, 15.8 us)
Async XLA Ops:
  1.3 32.4 %collective-permute-start.3 = (s32[2,16]{1,0:T(2,128)S(1)}, s32[2,16]{1,0:T(2,128)S(1)}, u32[]{:S(2)}, u32[]{:S(2)}) collective-permute-start(s32[2,16]{1,0:T(2,128)S(1)} %pad_add_fusion), channel_id=1, source_target_pairs={{0,4},{1,5},{2,6},{3,7},{4,0},{5,1},{6,2},{7,3},{8,12},{9,13},{10,... | collective-permute-start | bytes 392 | tf_op jit(solution)/shard_map/ppermute | solution.py:137
  4.3 29.4 %collective-permute-start.4 = (s32[2,16]{1,0:T(2,128)S(1)}, s32[2,16]{1,0:T(2,128)S(1)}, u32[]{:S(2)}, u32[]{:S(2)}) collective-permute-start(s32[2,16]{1,0:T(2,128)S(1)} %pad_add_fusion), channel_id=1, source_target_pairs={{0,5},{1,4},{2,7},{3,6},{4,1},{5,0},{6,3},{7,2},{8,13},{9,12},{10,... | collective-permute-start | bytes 392 | tf_op jit(solution)/shard_map/ppermute | solution.py:137
  4.3 32.8 %collective-permute-start.5 = (s32[2,16]{1,0:T(2,128)S(1)}, s32[2,16]{1,0:T(2,128)S(1)}, u32[]{:S(2)}, u32[]{:S(2)}) collective-permute-start(s32[2,16]{1,0:T(2,128)S(1)} %pad_add_fusion), channel_id=1, source_target_pairs={{0,6},{1,7},{2,4},{3,5},{4,2},{5,3},{6,0},{7,1},{8,14},{9,15},{10,... | collective-permute-start | bytes 392 | tf_op jit(solution)/shard_map/ppermute | solution.py:137
  6.4 30.9 %collective-permute-start.6 = (s32[2,16]{1,0:T(2,128)S(1)}, s32[2,16]{1,0:T(2,128)S(1)}, u32[]{:S(2)}, u32[]{:S(2)}) collective-permute-start(s32[2,16]{1,0:T(2,128)S(1)} %pad_add_fusion), channel_id=1, source_target_pairs={{0,7},{1,6},{2,5},{3,4},{4,3},{5,2},{6,1},{7,0},{8,15},{9,14},{10,... | collective-permute-start | bytes 392 | tf_op jit(solution)/shard_map/ppermute | solution.py:137
  7.0 33.9 %collective-permute-start.7 = (s32[2,16]{1,0:T(2,128)S(1)}, s32[2,16]{1,0:T(2,128)S(1)}, u32[]{:S(2)}, u32[]{:S(2)}) collective-permute-start(s32[2,16]{1,0:T(2,128)S(1)} %pad_add_fusion), channel_id=1, source_target_pairs={{0,8},{1,9},{2,10},{3,11},{4,12},{5,13},{6,14},{7,15},{8,0},{9,1},... | collective-permute-start | bytes 392 | tf_op jit(solution)/shard_map/ppermute | solution.py:137
  33.7 7.3 %collective-permute-start.8 = (s32[2,16]{1,0:T(2,128)S(1)}, s32[2,16]{1,0:T(2,128)S(1)}, u32[]{:S(2)}, u32[]{:S(2)}) collective-permute-start(s32[2,16]{1,0:T(2,128)S(1)} %pad_add_fusion), channel_id=1, source_target_pairs={{0,9},{1,8},{2,11},{3,10},{4,13},{5,12},{6,15},{7,14},{8,1},{9,0},... | collective-permute-start | bytes 392 | tf_op jit(solution)/shard_map/ppermute | solution.py:137
  33.8 11.1 %collective-permute-start.9 = (s32[2,16]{1,0:T(2,128)S(1)}, s32[2,16]{1,0:T(2,128)S(1)}, u32[]{:S(2)}, u32[]{:S(2)}) collective-permute-start(s32[2,16]{1,0:T(2,128)S(1)} %pad_add_fusion), channel_id=1, source_target_pairs={{0,10},{1,11},{2,8},{3,9},{4,14},{5,15},{6,12},{7,13},{8,2},{9,3},... | collective-permute-start | bytes 392 | tf_op jit(solution)/shard_map/ppermute | solution.py:137
  37.1 8.4 %collective-permute-start.10 = (s32[2,16]{1,0:T(2,128)S(1)}, s32[2,16]{1,0:T(2,128)S(1)}, u32[]{:S(2)}, u32[]{:S(2)}) collective-permute-start(s32[2,16]{1,0:T(2,128)S(1)} %pad_add_fusion), channel_id=1, source_target_pairs={{0,11},{1,10},{2,9},{3,8},{4,15},{5,14},{6,13},{7,12},{8,3},{9,2},... | collective-permute-start | bytes 392 | tf_op jit(solution)/shard_map/ppermute | solution.py:137
  37.4 8.5 %collective-permute-start.11 = (s32[2,16]{1,0:T(2,128)S(1)}, s32[2,16]{1,0:T(2,128)S(1)}, u32[]{:S(2)}, u32[]{:S(2)}) collective-permute-start(s32[2,16]{1,0:T(2,128)S(1)} %pad_add_fusion), channel_id=1, source_target_pairs={{0,12},{1,13},{2,14},{3,15},{4,8},{5,9},{6,10},{7,11},{8,4},{9,5},... | collective-permute-start | bytes 392 | tf_op jit(solution)/shard_map/ppermute | solution.py:137
  41.0 6.4 %collective-permute-start.12 = (s32[2,16]{1,0:T(2,128)S(1)}, s32[2,16]{1,0:T(2,128)S(1)}, u32[]{:S(2)}, u32[]{:S(2)}) collective-permute-start(s32[2,16]{1,0:T(2,128)S(1)} %pad_add_fusion), channel_id=1, source_target_pairs={{0,13},{1,12},{2,15},{3,14},{4,9},{5,8},{6,11},{7,10},{8,5},{9,4},... | collective-permute-start | bytes 392 | tf_op jit(solution)/shard_map/ppermute | solution.py:137
  41.0 6.5 %collective-permute-start.13 = (s32[2,16]{1,0:T(2,128)S(1)}, s32[2,16]{1,0:T(2,128)S(1)}, u32[]{:S(2)}, u32[]{:S(2)}) collective-permute-start(s32[2,16]{1,0:T(2,128)S(1)} %pad_add_fusion), channel_id=1, source_target_pairs={{0,14},{1,15},{2,12},{3,13},{4,10},{5,11},{6,8},{7,9},{8,6},{9,7},... | collective-permute-start | bytes 392 | tf_op jit(solution)/shard_map/ppermute | solution.py:137
  44.9 5.7 %collective-permute-start.14 = (s32[2,16]{1,0:T(2,128)S(1)}, s32[2,16]{1,0:T(2,128)S(1)}, u32[]{:S(2)}, u32[]{:S(2)}) collective-permute-start(s32[2,16]{1,0:T(2,128)S(1)} %pad_add_fusion), channel_id=1, source_target_pairs={{0,15},{1,14},{2,13},{3,12},{4,11},{5,10},{6,9},{7,8},{8,7},{9,6},... | collective-permute-start | bytes 392 | tf_op jit(solution)/shard_map/ppermute | solution.py:137
  45.5 5.0 %collective-permute-start = (s32[2,16]{1,0:T(2,128)S(1)}, s32[2,16]{1,0:T(2,128)S(1)}, u32[]{:S(2)}, u32[]{:S(2)}) collective-permute-start(s32[2,16]{1,0:T(2,128)S(1)} %pad_add_fusion), channel_id=1, source_target_pairs={{0,1},{1,0},{2,3},{3,2},{4,5},{5,4},{6,7},{7,6},{8,9},{9,8},{10,11... | collective-permute-start | bytes 392 | tf_op jit(solution)/shard_map/ppermute | solution.py:137
  45.9 4.7 %collective-permute-start.1 = (s32[2,16]{1,0:T(2,128)S(1)}, s32[2,16]{1,0:T(2,128)S(1)}, u32[]{:S(2)}, u32[]{:S(2)}) collective-permute-start(s32[2,16]{1,0:T(2,128)S(1)} %pad_add_fusion), channel_id=1, source_target_pairs={{0,2},{1,3},{2,0},{3,1},{4,6},{5,7},{6,4},{7,5},{8,10},{9,11},{10,... | collective-permute-start | bytes 392 | tf_op jit(solution)/shard_map/ppermute | solution.py:137
  47.4 3.2 %collective-permute-start.2 = (s32[2,16]{1,0:T(2,128)S(1)}, s32[2,16]{1,0:T(2,128)S(1)}, u32[]{:S(2)}, u32[]{:S(2)}) collective-permute-start(s32[2,16]{1,0:T(2,128)S(1)} %pad_add_fusion), channel_id=1, source_target_pairs={{0,3},{1,2},{2,1},{3,0},{4,7},{5,6},{6,5},{7,4},{8,11},{9,10},{10,... | collective-permute-start | bytes 392 | tf_op jit(solution)/shard_map/ppermute | solution.py:137
  61.7 3.2 %collective-permute-start.28 = (bf16[8,16,256]{2,1,0:T(8,128)(2,1)S(1)}, bf16[8,16,256]{2,1,0:T(8,128)(2,1)S(1)}, u32[]{:S(2)}, u32[]{:S(2)}) collective-permute-start(bf16[8,16,256]{2,1,0:T(8,128)(2,1)S(1)} %get-tuple-element.22), channel_id=1, source_target_pairs={{0,1},{1,0},{2,3},{3,2},{4,5},{5,4},{6,7},{7,6},{8,9},{9,8},{10,11... | collective-permute-start | bytes 196616 | tf_op jit(solution)/shard_map/ppermute | solution.py:137
  61.8 17.2 %collective-permute-start.15 = (f32[4,200,128]{2,1,0:T(8,128)}, f32[4,200,128]{2,1,0:T(8,128)S(1)}, u32[]{:S(2)}, u32[]{:S(2)}) collective-permute-start(f32[4,200,128]{2,1,0:T(8,128)} %get-tuple-element.12), channel_id=1, source_target_pairs={{0,1},{1,0},{2,3},{3,2},{4,5},{5,4},{6,7},{7,6},{8,9},{9,8},{10,11... | collective-permute-start | bytes 1228808 | tf_op jit(solution)/shard_map/ppermute | solution.py:137
  64.3 15.8 %collective-permute-start.17 = (f32[4,200,128]{2,1,0:T(8,128)S(1)}, f32[4,200,128]{2,1,0:T(8,128)S(1)}, u32[]{:S(2)}, u32[]{:S(2)}) collective-permute-start(f32[4,200,128]{2,1,0:T(8,128)S(1)} %add.191), channel_id=1, source_target_pairs={{0,2},{1,3},{2,0},{3,1},{4,6},{5,7},{6,4},{7,5},{8,10},{9,11},{10,... | collective-permute-start | bytes 1228808 | tf_op jit(solution)/shard_map/ppermute | solution.py:137
  65.0 14.0 %collective-permute-start.29 = (bf16[2,128,256]{2,1,0:T(8,128)(2,1)S(1)}, bf16[2,128,256]{2,1,0:T(8,128)(2,1)S(1)}, u32[]{:S(2)}, u32[]{:S(2)}) collective-permute-start(bf16[2,128,256]{2,1,0:T(8,128)(2,1)S(1)} %pad_maximum_fusion.1), channel_id=1, source_target_pairs={{0,2},{1,3},{2,0},{3,1},{4,6},{5,7},{6,4},{7,5},{8,10},{9,11},{10,... | collective-permute-start | bytes 393224 | tf_op jit(solution)/shard_map/ppermute | solution.py:137
  79.0 29.4 %collective-permute-start.30 = (bf16[2,2,128,256]{3,2,1,0:T(8,128)(2,1)S(1)}, bf16[2,2,128,256]{3,2,1,0:T(8,128)(2,1)S(1)}, u32[]{:S(2)}, u32[]{:S(2)}) collective-permute-start(bf16[2,2,128,256]{3,2,1,0:T(8,128)(2,1)S(1)} %pad_maximum_fusion.refs_8_), channel_id=1, source_target_pairs={{0,4},{1,5},{2,6},{3,7},{4,0},{5,1},{6,2},{7,3},{8,12},{9,13},{10,... | collective-permute-start | bytes 786440 | tf_op jit(solution)/shard_map/ppermute | solution.py:137
  80.2 12.7 %collective-permute-start.18 = (f32[200,128]{1,0:T(8,128)S(1)}, f32[200,128]{1,0:T(8,128)S(1)}, u32[]{:S(2)}, u32[]{:S(2)}) collective-permute-start(f32[200,128]{1,0:T(8,128)S(1)} %get-tuple-element.18), channel_id=1, source_target_pairs={{0,4},{1,5},{2,6},{3,7},{4,0},{5,1},{6,2},{7,3},{8,12},{9,13},{10,... | collective-permute-start | bytes 307208 | tf_op jit(solution)/shard_map/ppermute | solution.py:137
  82.3 13.0 %collective-permute-start.19 = (f32[200,128]{1,0:T(8,128)S(1)}, f32[200,128]{1,0:T(8,128)S(1)}, u32[]{:S(2)}, u32[]{:S(2)}) collective-permute-start(f32[200,128]{1,0:T(8,128)S(1)} %get-tuple-element.20), channel_id=1, source_target_pairs={{0,8},{1,9},{2,10},{3,11},{4,12},{5,13},{6,14},{7,15},{8,0},{9,1},... | collective-permute-start | bytes 307208 | tf_op jit(solution)/shard_map/ppermute | solution.py:137
  83.3 12.1 %collective-permute-start.20 = (f32[200,128]{1,0:T(8,128)S(1)}, f32[200,128]{1,0:T(8,128)S(1)}, u32[]{:S(2)}, u32[]{:S(2)}) collective-permute-start(f32[200,128]{1,0:T(8,128)S(1)} %get-tuple-element.19), channel_id=1, source_target_pairs={{0,12},{1,13},{2,14},{3,15},{4,8},{5,9},{6,10},{7,11},{8,4},{9,5},... | collective-permute-start | bytes 307208 | tf_op jit(solution)/shard_map/ppermute | solution.py:137
  86.3 26.8 %collective-permute-start.31 = (bf16[2,2,128,256]{3,2,1,0:T(8,128)(2,1)S(1)}, bf16[2,2,128,256]{3,2,1,0:T(8,128)(2,1)S(1)}, u32[]{:S(2)}, u32[]{:S(2)}) collective-permute-start(bf16[2,2,128,256]{3,2,1,0:T(8,128)(2,1)S(1)} %pad_maximum_fusion.refs_8_), channel_id=1, source_target_pairs={{0,8},{1,9},{2,10},{3,11},{4,12},{5,13},{6,14},{7,15},{8,0},{9,1},... | collective-permute-start | bytes 786440 | tf_op jit(solution)/shard_map/ppermute | solution.py:137
  93.0 30.7 %collective-permute-start.32 = (bf16[2,2,128,256]{3,2,1,0:T(8,128)(2,1)S(1)}, bf16[2,2,128,256]{3,2,1,0:T(8,128)(2,1)S(1)}, u32[]{:S(2)}, u32[]{:S(2)}) collective-permute-start(bf16[2,2,128,256]{3,2,1,0:T(8,128)(2,1)S(1)} %pad_maximum_fusion.refs_8_), channel_id=1, source_target_pairs={{0,12},{1,13},{2,14},{3,15},{4,8},{5,9},{6,10},{7,11},{8,4},{9,5},... | collective-permute-start | bytes 786440 | tf_op jit(solution)/shard_map/ppermute | solution.py:137
  95.4 18.2 %collective-permute-start.22 = (bf16[200,128]{1,0:T(8,128)(2,1)S(1)}, bf16[200,128]{1,0:T(8,128)(2,1)S(1)}, u32[]{:S(2)}, u32[]{:S(2)}) collective-permute-start(bf16[200,128]{1,0:T(8,128)(2,1)S(1)} %fusion.11.refs_0_), channel_id=1, source_target_pairs={{0,4},{1,5},{2,6},{3,7},{4,0},{5,1},{6,2},{7,3},{8,12},{9,13},{10,... | collective-permute-start | bytes 153608 | tf_op jit(solution)/shard_map/ppermute | solution.py:137
  107.7 12.3 %collective-permute-start.24 = (bf16[200,128]{1,0:T(8,128)(2,1)S(1)}, bf16[200,128]{1,0:T(8,128)(2,1)S(1)}, u32[]{:S(2)}, u32[]{:S(2)}) collective-permute-start(bf16[200,128]{1,0:T(8,128)(2,1)S(1)} %fusion.11.refs_0_), channel_id=1, source_target_pairs={{0,8},{1,9},{2,10},{3,11},{4,12},{5,13},{6,14},{7,15},{8,0},{9,1},... | collective-permute-start | bytes 153608 | tf_op jit(solution)/shard_map/ppermute | solution.py:137
  108.4 12.1 %collective-permute-start.26 = (bf16[200,128]{1,0:T(8,128)(2,1)S(1)}, bf16[200,128]{1,0:T(8,128)(2,1)S(1)}, u32[]{:S(2)}, u32[]{:S(2)}) collective-permute-start(bf16[200,128]{1,0:T(8,128)(2,1)S(1)} %fusion.11.refs_0_), channel_id=1, source_target_pairs={{0,12},{1,13},{2,14},{3,15},{4,8},{5,9},{6,10},{7,11},{8,4},{9,5},... | collective-permute-start | bytes 153608 | tf_op jit(solution)/shard_map/ppermute | solution.py:137
  113.1 10.6 %collective-permute-start.21 = (bf16[200,128]{1,0:T(8,128)(2,1)S(1)}, bf16[200,128]{1,0:T(8,128)(2,1)S(1)}, u32[]{:S(2)}, u32[]{:S(2)}) collective-permute-start(bf16[200,128]{1,0:T(8,128)(2,1)S(1)} %fusion.11.refs_0_), channel_id=1, source_target_pairs={{0,2},{1,3},{2,0},{3,1},{4,6},{5,7},{6,4},{7,5},{8,10},{9,11},{10,... | collective-permute-start | bytes 153608 | tf_op jit(solution)/shard_map/ppermute | solution.py:137
  113.6 10.1 %collective-permute-start.23 = (bf16[200,128]{1,0:T(8,128)(2,1)S(1)}, bf16[200,128]{1,0:T(8,128)(2,1)S(1)}, u32[]{:S(2)}, u32[]{:S(2)}) collective-permute-start(bf16[200,128]{1,0:T(8,128)(2,1)S(1)} %collective-permute-done.22.refs_2_), channel_id=1, source_target_pairs={{0,2},{1,3},{2,0},{3,1},{4,6},{5,7},{6,4},{7,5},{8,10},{9,11},{10,... | collective-permute-start | bytes 153608 | tf_op jit(solution)/shard_map/ppermute | solution.py:137
  120.0 4.1 %collective-permute-start.25 = (bf16[200,128]{1,0:T(8,128)(2,1)S(1)}, bf16[200,128]{1,0:T(8,128)(2,1)S(1)}, u32[]{:S(2)}, u32[]{:S(2)}) collective-permute-start(bf16[200,128]{1,0:T(8,128)(2,1)S(1)} %collective-permute-done.24.refs_4_), channel_id=1, source_target_pairs={{0,2},{1,3},{2,0},{3,1},{4,6},{5,7},{6,4},{7,5},{8,10},{9,11},{10,... | collective-permute-start | bytes 153608 | tf_op jit(solution)/shard_map/ppermute | solution.py:137
  120.5 4.2 %collective-permute-start.27 = (bf16[200,128]{1,0:T(8,128)(2,1)S(1)}, bf16[200,128]{1,0:T(8,128)(2,1)S(1)}, u32[]{:S(2)}, u32[]{:S(2)}) collective-permute-start(bf16[200,128]{1,0:T(8,128)(2,1)S(1)} %collective-permute-done.26.refs_6_), channel_id=1, source_target_pairs={{0,2},{1,3},{2,0},{3,1},{4,6},{5,7},{6,4},{7,5},{8,10},{9,11},{10,... | collective-permute-start | bytes 153608 | tf_op jit(solution)/shard_map/ppermute | solution.py:137
  (18 other events, 177.3 us)

commit v2 on v1

--- a/solution.py
+++ b/solution.py
@@ -1,8 +1,8 @@
-import functools
 import math
 
 import jax
 import jax.numpy as jnp
+import numpy as np
 from jax import lax
 from jax.experimental import pallas as pl
 from jax.experimental.pallas import tpu as pltpu
@@ -18,16 +18,23 @@
 VMEM_LIMIT = 56 * 1024 * 1024
 
 
-def dct_rows(frequency, sample, length):
+def dct_table(length):
+    frequency = jnp.arange(length, dtype=jnp.float32)[:, None]
+    sample = jnp.arange(length, dtype=jnp.float32)[None, :]
     cosine_table = jnp.cos(math.pi * (2.0 * sample + 1.0) * frequency / (2.0 * length))
     factor = jnp.where(frequency == 0, math.sqrt(1.0 / length), math.sqrt(2.0 / length))
     return (cosine_table * factor).astype(jnp.bfloat16)
 
 
-def dct_table(length):
-    frequency = jnp.arange(length, dtype=jnp.float32)[:, None]
-    sample = jnp.arange(length, dtype=jnp.float32)[None, :]
-    return dct_rows(frequency, sample, length)
+def dct_constant(length):
+    frequency = np.arange(length, dtype=np.float32)[:, None]
+    sample = np.arange(length, dtype=np.float32)[None, :]
+    angle = np.float32(math.pi) * (np.float32(2.0) * sample + np.float32(1.0)) * frequency
+    cosine_table = np.cos(angle / np.float32(2.0 * length))
+    factor = np.where(
+        frequency == 0, np.float32(math.sqrt(1.0 / length)), np.float32(math.sqrt(2.0 / length))
+    )
+    return (cosine_table * factor).astype(jnp.bfloat16)
 
 
 def gram_terms(predicted, observed_rows, scale_rows, noise_rows, live_mask, weight_scale):
@@ -137,11 +144,8 @@
     return lax.ppermute(value, "map", pairs)
 
 
-def by_row_kernel(maps_ref, out_ref, wide_ref):
-    members, rows, width = maps_ref.shape
-    wide_ref[...] = maps_ref[...].reshape(members * rows, width).astype(jnp.float32)
-    for row in range(rows):
-        out_ref[row] = wide_ref[pl.ds(row, members, stride=rows), :].astype(jnp.bfloat16)
+def by_row_kernel(maps_ref, out_ref):
+    out_ref[...] = jnp.swapaxes(maps_ref[...], 0, 1)
 
 
 def by_row(amplitude_maps):
@@ -152,26 +156,35 @@
         in_specs=[pl.BlockSpec((members, rows, LANE), lambda i: (0, 0, i))],
         out_specs=pl.BlockSpec((rows, members, LANE), lambda i: (0, 0, i)),
         out_shape=jax.ShapeDtypeStruct((rows, members, width), jnp.bfloat16),
-        scratch_shapes=[pltpu.VMEM((members * rows, LANE), jnp.float32)],
         compiler_params=pltpu.CompilerParams(vmem_limit_bytes=VMEM_LIMIT),
         cost_estimate=pl.CostEstimate(
-            flops=0, bytes_accessed=8 * members * rows * width, transcendentals=0
+            flops=0, bytes_accessed=4 * members * rows * width, transcendentals=0
         ),
         name="maps_by_row",
     )(amplitude_maps)
 
 
 def shares_kernel(
-    starts_ref, maps_ref, column_ref, table_w_ref, table_h_ref, k0_ref, k1_ref, s0_ref, s1_ref,
-    pick_ref, row_ref, wide_ref,
+    starts_ref, place_ref, maps_ref, column_ref, table_w_ref, table_h_ref,
+    k0_ref, k1_ref, s0_ref, s1_ref,
+    pick_ref, row_ref, spread_ref, wide_ref,
 ):
     step = pl.program_id(0)
     rows, members, width = maps_ref.shape
     keep = row_ref.shape[1] // (rows * pl.num_programs(0))
     devices = row_ref.shape[0]
+    depth = row_ref.shape[1]
+    me = place_ref[0]
 
     @pl.when(step == 0)
     def _():
+        height = table_h_ref.shape[1]
+        sample = lax.broadcasted_iota(jnp.int32, (height, depth), 0) - me * (depth // keep)
+        held = lax.broadcasted_iota(jnp.int32, (height, depth), 1) // keep
+        spread_ref[...] = jnp.dot(
+            table_h_ref[...], (sample == held).astype(jnp.bfloat16),
+            preferred_element_type=jnp.float32,
+        )
         lanes = lax.broadcasted_iota(jnp.int32, (column_ref.shape[0], width), 1)
         one_hot = (column_ref[...] == lanes).astype(jnp.bfloat16)
         pick_ref[...] = jnp.dot(
@@ -188,24 +201,23 @@
 
     @pl.when(step == pl.num_programs(0) - 1)
     def _():
-        depth = row_ref.shape[1]
         position = lax.broadcasted_iota(jnp.int32, (BLK, depth), 1) % keep
         outs = ((k0_ref, 0), (k1_ref, 2), (s0_ref, 1), (s1_ref, 3))
         for out_ref, low in outs:
             for high in range(out_ref.shape[0]):
                 delta = high * 4 + low
                 for p in range(keep):
-                    start = pl.multiple_of(starts_ref[delta * keep + p], BLK)
-                    block = table_h_ref[pl.ds(start, BLK), :]
+                    start = pl.multiple_of(starts_ref[(me ^ delta) * keep + p], BLK)
+                    block = spread_ref[pl.ds(start, BLK), :]
                     wide_ref[pl.ds(p * BLK, BLK), :] = jnp.where(position == p, block, 0.0)
                 share = jnp.dot(
-                    wide_ref[...].astype(jnp.bfloat16), row_ref[delta],
+                    wide_ref[...].astype(jnp.bfloat16), row_ref[me ^ delta],
                     preferred_element_type=jnp.float32,
                 )
                 out_ref[high] = share.T
 
 
-def shares(maps, columns, starts, table_w, table_h):
+def shares(maps, columns, starts, place, table_w, table_h):
     rows, members, width = maps.shape
     kept = columns.shape[0]
     devices = lax.axis_size("map")
@@ -213,14 +225,14 @@
     steps = 4
     depth = rows * keep
     out = jax.ShapeDtypeStruct((devices // 4, members, keep * BLK), jnp.float32)
-    whole = lambda *shape: pl.BlockSpec(shape, lambda i, s: (0,) * len(shape))
+    whole = lambda *shape: pl.BlockSpec(shape, lambda i, s, t: (0,) * len(shape))
     return pl.pallas_call(
         shares_kernel,
         grid_spec=pltpu.PrefetchScalarGridSpec(
-            num_scalar_prefetch=1,
+            num_scalar_prefetch=2,
             grid=(steps,),
             in_specs=[
-                pl.BlockSpec((rows // steps, members, width), lambda i, s: (i, 0, 0)),
+                pl.BlockSpec((rows // steps, members, width), lambda i, s, t: (i, 0, 0)),
                 whole(kept, 1),
                 whole(*table_w.shape),
                 whole(*table_h.shape),
@@ -229,6 +241,7 @@
             scratch_shapes=[
                 pltpu.VMEM((kept, width), jnp.bfloat16),
                 pltpu.VMEM((devices, depth, members), jnp.bfloat16),
+                pltpu.VMEM((table_h.shape[0], depth), jnp.float32),
                 pltpu.VMEM((keep * BLK, depth), jnp.float32),
             ],
         ),
@@ -240,14 +253,14 @@
             transcendentals=0,
         ),
         name="coefficient_shares",
-    )(starts, maps, columns, table_w, table_h)
+    )(starts, place, maps, columns, table_w, table_h)
 
 
 def gram_kernel(
     starts_ref, place_ref, target_ref, *refs
 ):
-    predicted_refs, noise_refs = refs[:8], refs[8:12]
-    out_ref, predicted_ref, wide_ref, noise_ref, left_ref, right_ref, misfit_ref = refs[12:]
+    predicted_refs, noise_refs = refs[:8], refs[8:10]
+    out_ref, predicted_ref, wide_ref, noise_ref, left_ref, right_ref, misfit_ref = refs[10:]
     groups, members, per = predicted_ref.shape
     keep = per // BLK
     coefficients = groups * per
@@ -255,7 +268,7 @@
     chip = place_ref[0]
     for i, ref in enumerate(predicted_refs):
         predicted_ref[chip ^ i] = ref[...].astype(jnp.float32)
-    span = wide_ref.shape[0] // 4
+    span = wide_ref.shape[0] // len(noise_refs)
     for i, ref in enumerate(noise_refs):
         wide_ref[pl.ds(i * span, span), :] = ref[...].reshape(span, -1).astype(jnp.float32)
     right_ref[...] = jnp.zeros_like(right_ref)
@@ -305,7 +318,7 @@
     members, per = predicted[0].shape
     groups = len(predicted)
     coefficients = groups * per
-    rows = 4 * noise[0].shape[0] * noise[0].shape[1] * noise[0].shape[2]
+    rows = len(noise) * math.prod(noise[0].shape[:-1])
     smem = pl.BlockSpec(memory_space=pltpu.SMEM)
     vmem = pl.BlockSpec(memory_space=pltpu.VMEM)
     return pl.pallas_call(
@@ -326,11 +339,11 @@
     )(starts, place, target, *predicted, *noise)
 
 
-def solve_kernel(mine_ref, other_ref, weights_ref, parts_ref, misfit_ref, state_ref, power_ref):
+def solve_kernel(mine_ref, other_ref, weights_ref, parts_ref, lean_ref, misfit_ref, state_ref):
     members = weights_ref.shape[0]
     total = mine_ref[0:members, :] + other_ref[0:members, :]
     misfit_ref[...] = (
-        mine_ref[members : members + 8, 0:256] + other_ref[members : members + 8, 256:512]
+        mine_ref[members : members + 1, 0:256] + other_ref[members : members + 1, 256:512]
     )
     row = lax.broadcasted_iota(jnp.int32, (members, 256), 0)
     lane = lax.broadcasted_iota(jnp.int32, (members, 256), 1)
@@ -363,12 +376,13 @@
     center = jnp.sum(full, axis=0, keepdims=True) * (1.0 / members)
     spread = ((full - center) * (1.0 / math.sqrt(members - 1))).T[0:members, 0:members]
     high = spread.astype(jnp.bfloat16)
-    rest = spread - high.astype(jnp.float32)
-    middle = rest.astype(jnp.bfloat16)
-    low = (rest - middle.astype(jnp.float32)).astype(jnp.bfloat16)
-    parts_ref[0] = high
-    parts_ref[1] = middle
-    parts_ref[2] = low
+    low = (spread - high.astype(jnp.float32)).astype(jnp.bfloat16)
+    kept = high.astype(jnp.float32) + low.astype(jnp.float32)
+    lean_ref[...] = jnp.broadcast_to(jnp.sum(kept, axis=1, keepdims=True), lean_ref.shape)
+    ones = jnp.ones((16, members), jnp.float32)
+    parts_ref[...] = jnp.concatenate(
+        [high.astype(jnp.float32), low.astype(jnp.float32), ones], axis=0
+    ).astype(jnp.bfloat16)
 
 
 def solve(mine, other):
@@ -377,41 +391,44 @@
     return pl.pallas_call(
         solve_kernel,
         in_specs=[vmem, vmem],
-        out_specs=[vmem] * 3,
+        out_specs=[vmem] * 4,
         out_shape=[
             jax.ShapeDtypeStruct((members, members), jnp.float32),
-            jax.ShapeDtypeStruct((3, members, members), jnp.bfloat16),
-            jax.ShapeDtypeStruct((8, 256), jnp.float32),
+            jax.ShapeDtypeStruct((2 * members + 16, members), jnp.bfloat16),
+            jax.ShapeDtypeStruct((members, LANE), jnp.float32),
+            jax.ShapeDtypeStruct((1, 256), jnp.float32),
         ],
-        scratch_shapes=[pltpu.VMEM((256, 512), jnp.float32), pltpu.VMEM((256, 512), jnp.float32)],
+        scratch_shapes=[pltpu.VMEM((256, 512), jnp.float32)],
         compiler_params=pltpu.CompilerParams(vmem_limit_bytes=VMEM_LIMIT),
         name="solve_weights",
     )(mine, other)
 
 
-def slab_kernel(parts_ref, slab_ref, out_ref):
+def slab_kernel(parts_ref, lean_ref, slab_ref, out_ref):
+    members = slab_ref.shape[0]
     state = slab_ref[...]
-    moved = jnp.dot(parts_ref[2], state, preferred_element_type=jnp.float32)
-    moved = moved + jnp.dot(parts_ref[1], state, preferred_element_type=jnp.float32)
-    moved = moved + jnp.dot(parts_ref[0], state, preferred_element_type=jnp.float32)
+    moved = jnp.dot(parts_ref[...], state, preferred_element_type=jnp.float32)
+    center = moved[2 * members : 2 * members + 1] * (1.0 / members)
+    moved = moved[0:members] + (moved[members : 2 * members] - lean_ref[:, 0:1] * center)
     out_ref[...] = (state.astype(jnp.float32) + moved).astype(jnp.bfloat16)
 
 
-def move_slab(parts, slab):
+def move_slab(parts, lean, slab):
     members, cells = slab.shape
     tile = 2048
     return pl.pallas_call(
         slab_kernel,
         grid=(cells // tile,),
         in_specs=[
-            pl.BlockSpec(parts.shape, lambda i: (0, 0, 0)),
+            pl.BlockSpec(parts.shape, lambda i: (0, 0)),
+            pl.BlockSpec(lean.shape, lambda i: (0, 0)),
             pl.BlockSpec((members, tile), lambda i: (0, i)),
         ],
         out_specs=pl.BlockSpec((members, tile), lambda i: (0, i)),
         out_shape=jax.ShapeDtypeStruct(slab.shape, slab.dtype),
         compiler_params=pltpu.CompilerParams(vmem_limit_bytes=VMEM_LIMIT),
         name="slab_update",
-    )(parts, slab)
+    )(parts, lean, slab)
 
 
 def sparse_body(
@@ -426,65 +443,70 @@
     slots = observed.shape[0]
     me = lax.axis_index("map").astype(jnp.int32)
 
-    lists = jnp.stack([kept_blocks, block_owner[:, 0]])
-    lists = jnp.stack([lists] + [swap(lists, delta) for delta in range(1, devices)])
+    core, chip = me & 1, me >> 1
+
+    lists = jnp.stack([kept_blocks, block_owner[:, 0]]).reshape(1, -1)
+    lists = lax.all_to_all(
+        jnp.broadcast_to(lists, (devices, 2 * keep)), "map", split_axis=0, concat_axis=0, tiled=True
+    ).reshape(devices, 2, keep)
+    blocks, owner = lists[:, 0], lists[:, 1]
 
     extra = jnp.zeros((slots, 256 - members - 2), jnp.bfloat16)
     noise = jnp.concatenate(
         [perturbation, observed[:, None], error_scale[:, None], extra], axis=1
     ).reshape(devices // 2, 2, CAP * BLK, 256)
-    core = me & 1
     noise_keep = lax.dynamic_index_in_dim(noise, core, 1, keepdims=False)
     noise_send = lax.dynamic_index_in_dim(noise, 1 - core, 1, keepdims=False)
-    noise = jnp.stack([noise_keep, swap(noise_send, 1)]).reshape(2, -1, 256)
-    noise = jnp.stack([noise, swap(noise, 2)])
-    noises = [noise] + [swap(noise, delta) for delta in (4, 8, 12)]
+    noise = jnp.stack([noise_keep, swap(noise_send, 1)]).reshape(slots, 256)
+    noises = [noise] + [swap(noise, 4 * i) for i in range(1, devices // 4)]
 
     maps = by_row(amplitude_maps)
-    table_w = dct_table(map_width)
-    frequency = jnp.arange(map_height, dtype=jnp.float32)[:, None]
-    sample = jnp.repeat(jnp.arange(rows_here, dtype=jnp.int32), keep)[None, :] + me * rows_here
-    table_h = dct_rows(frequency, sample.astype(jnp.float32), map_height).astype(jnp.float32)
-
-    device = me ^ jnp.arange(devices, dtype=jnp.int32)
-    columns = device[:, None] * columns_here + lists[:, 0] // per_column
-    starts = (lists[:, 0] % per_column * BLK).reshape(-1)
+    table_w = jnp.asarray(dct_constant(map_width))
+    table_h = table_w if map_height == map_width else jnp.asarray(dct_constant(map_height))
+    device = jnp.arange(devices, dtype=jnp.int32)
+    columns = device[:, None] * columns_here + blocks // per_column
+    starts = (blocks % per_column * BLK).reshape(-1)
     keep_0, keep_1, send_0, send_1 = shares(
-        maps, columns.reshape(-1, 1), starts, table_w, table_h
+        maps, columns.reshape(-1, 1), starts, me.reshape(1), table_w, table_h
     )
 
     share_1 = keep_1 + swap(send_1, 1)
     got_1 = swap(share_1, 2)
     share_0 = keep_0 + swap(send_0, 1)
     share = [share_0[i] + got_1[i] for i in range(devices // 4)]
+    share, noises = lax.optimization_barrier((share, noises))
+    near_noise = jnp.stack(noises)
+    far_noise = swap(near_noise, 2)
     got = [swap(share[i], 4 * i) for i in range(1, devices // 4)]
     predicted = (share[0] + got[0] + got[1] + got[2]).astype(jnp.bfloat16)
+    predicted, far_noise = lax.optimization_barrier((predicted, far_noise))
 
     near = [predicted] + [swap(predicted, 4 * i) for i in range(1, devices // 4)]
     gathered = []
     for value in near:
         gathered += [value, swap(value, 2)]
 
-    owner = lists[:, 1]
     positions = jnp.arange(keep, dtype=jnp.int32)
     earlier = (owner[:, :, None] == owner[:, None, :]) & (
         positions[None, None, :] < positions[None, :, None]
     )
     rank = jnp.sum(earlier.astype(jnp.int32), axis=2)
-    chip = me >> 1
-    chips = jnp.arange(devices // 2, dtype=jnp.int32)
-    owner = jnp.take(owner[0::2], chip ^ chips, axis=0)
-    rank = jnp.take(rank[0::2], chip ^ chips, axis=0)
-    noise_rows = (owner ^ me) * (slots // 2) + chips[:, None] * (CAP * BLK) + rank * BLK
-    data_row = (chips[:, None] * 2 + core) * (CAP * BLK) + rank * BLK
+    pairs = jnp.stack([owner, rank]).reshape(2, devices // 2, 2, keep)
+    owner, rank = lax.dynamic_index_in_dim(pairs, core, 2, keepdims=False)
+    chips = jnp.arange(devices // 2, dtype=jnp.int32)[:, None]
     away = owner ^ me
+    held = (away >> 1 & 1) * 8 + (away >> 2) * 2 + (away & 1)
+    noise_rows = held * (slots // 2) + chips * (CAP * BLK) + rank * BLK
+    data_row = (chips * 2 + core) * (CAP * BLK) + rank * BLK
     target = jnp.where(away < 2, away * slots + data_row, -1024)
     target = (target[:, :, None] + jnp.arange(BLK, dtype=jnp.int32)).reshape(-1, 1)
 
-    mine = gram(noise_rows.reshape(-1), chip.reshape(1), target, gathered, noises)
-    update_weights, parts, data_misfit = solve(mine, swap(mine, 1))
-    updated_slab = move_slab(parts, model_slab)
-    return (updated_slab, update_weights, data_misfit[0])
+    mine = gram(
+        noise_rows.reshape(-1), chip.reshape(1), target, gathered, [near_noise, far_noise]
+    )
+    update_weights, parts, lean, data_misfit = solve(mine, swap(mine, 1))
+    updated_slab = move_slab(parts, lean, model_slab)
+    return (updated_slab, update_weights, data_misfit.reshape(-1))
 
 
 def solution(mesh):

time: 148 us -> 96.9 us (0.65)
  starting transfers between devices: 53.3 us -> 28.9 us
  waiting for transfers between devices: 31.9 us -> 21.3 us
  Pallas kernels: 42 us -> 34 us
  other arithmetic: 12.8 us -> 6.16 us
  local copies, waits for them, and re-layouts: 6.48 us -> 4.98 us
    ppermute x34 -> x19, starting transfers between devices: 53.3 us -> 21.5 us  [swap(): return lax.ppermute(value, 'map', pairs)]
    ppermute x34 -> x19, waiting for transfers between devices: 31.9 us -> 21.3 us  [swap(): return lax.ppermute(value, 'map', pairs)]
    pallas_call x1, Pallas kernels: 14.9 us -> 6.25 us  [by_row(): pl.pallas_call(by_row_kernel, grid=(width // LANE,), in_specs=[pl.BlockSp...]
    convert_element_type x1 -> x0, other arithmetic: 7.87 us -> none  [sparse_body(): dct_rows(frequency, sample.astype(jnp.float32), map_height)]
    all_to_all x0 -> x1, starting transfers between devices: none -> 7.36 us  [sparse_body(): lax.all_to_all(jnp.broadcast_to(lists, (devices, 2 * keep)), 'map', split...]
  transfers between devices with their start and end apart: 34 -> 20, of which waited for: 10 -> 11; matrix products, arithmetic and copies ran while one was open for 10% -> 6% of each run, Pallas kernels for 10% -> 6%
where the time goes in v2:
time: 96.9 us; the launch traced here: 96.4 us
  Pallas kernels  34 us (35%)
  starting transfers between devices  28.9 us (30%)
  waiting for transfers between devices  21.3 us (22%)
  other arithmetic  6.16 us (6%)
  local copies, waits for them, and re-layouts  4.98 us (5%)
    ppermute x19, starting transfers between devices, swap(): return lax.ppermute(value, 'map', pairs)  21.5 us
    ppermute x19, waiting for transfers between devices, swap(): return lax.ppermute(value, 'map', pairs)  21.3 us
    pallas_call x1, Pallas kernels, shares(): pl.pallas_call(shares_kernel, grid_spec=pltpu.PrefetchScalarGridSpec(num_...  9.29 us
    pallas_call x1, Pallas kernels, move_slab(): pl.pallas_call(slab_kernel, grid=(cells // tile,), in_specs=[pl.BlockSpec...  8.72 us
    all_to_all x1, starting transfers between devices, sparse_body(): lax.all_to_all(jnp.broadcast_to(lists, (devices, 2 * keep)), 'map', split...  7.36 us
    pallas_call x1, Pallas kernels, by_row(): pl.pallas_call(by_row_kernel, grid=(width // LANE,), in_specs=[pl.BlockSp...  6.25 us
    pallas_call x1, Pallas kernels, solve(): pl.pallas_call(solve_kernel, in_specs=[vmem, vmem], out_specs=[vmem] * 4,...  5.38 us
    pallas_call x1, Pallas kernels, gram(): pl.pallas_call(gram_kernel, in_specs=[smem, smem] + [vmem] * (1 + len(pre...  4.4 us
  transfers between devices with their start and end apart: 20, of which 11 were waited for; matrix products, arithmetic and copies ran while one was open for 6% of the time, Pallas kernels for 6%

profile of v2, /device:TPU:0, one launch (start us, length us, event | category | flops | bytes accessed | tf_op | source)
XLA Modules:
  0.0 96.4 jit_solution(8142759648577543825)
XLA Ops:
  0.6 0.7 pad_add_fusion
  2.0 7.4 %all-to-all-start = ((s32[16,1,32]{2,1,0:T(1,128)}), s32[16,1,32]{2,1,0:T(1,128)S(1)}, u32[]{:S(2)}, u32[]{:S(2)}) async-start(s32[16,1,32]{2,1,0:T(1,128)} %broadcast_in_dim.10), calls=%async_computation | async-start | bytes 16384 | tf_op jit(solution)/shard_map/all_to_all | solution.py:449
  9.4 6.3 %maps_by_row.1.maps_ref = bf16[32,200,512]{2,1,0:T(8,128)(2,1)} custom-call(bf16[200,32,512]{2,1,0:T(8,128)(2,1)} %maps_ref.1), custom_call_target="tpu_custom_call" | custom-call | bytes 13107200 | tf_op jit(solution)/shard_map/maps_by_row/pallas_call | solution.py:153
  17.1 0.7 reduce.9
  18.6 0.7 fusion.1.column_ref
  19.4 9.3 %coefficient_shares.1 = (f32[4,200,128]{2,1,0:T(8,128)}, f32[4,200,128]{2,1,0:T(8,128)}, f32[4,200,128]{2,1,0:T(8,128)}, f32[4,200,128]{2,1,0:T(8,128)}) custom-call(s32[256]{0:T(256)} %fusion.10.starts_ref, s32[1]{0:T(128)} %bitcast.9.place_ref, bf16[32,200,512]{2,1,0:T(8,128)(2,1)} %maps_by_row.1.maps_ref, s32[256,1]{1,0:T(8,128)} %fusion.1.column_ref, ...), custom_call_target="tpu_custom_call" | custom-call | flops 1677721600 | bytes 6553600 | tf_op jit(solution)/shard_map/coefficient_shares/pallas_call | solution.py:229
  30.0 0.6 collective-permute-done.1
  30.6 1.0 %add.178 = f32[4,200,128]{2,1,0:T(8,128)S(1)} add(f32[4,200,128]{2,1,0:T(8,128)} %get-tuple-element.23, f32[4,200,128]{2,1,0:T(8,128)S(1)} %collective-permute-done.1) | non-fusion elementwise | flops 102400 | bytes 1228800 | tf_op jit(solution)/shard_map/add | solution.py:473
  31.7 2.0 %collective-permute-start.2 = (f32[4,200,128]{2,1,0:T(8,128)S(1)}, f32[4,200,128]{2,1,0:T(8,128)S(1)}, u32[]{:S(2)}, u32[]{:S(2)}) collective-permute-start(f32[4,200,128]{2,1,0:T(8,128)S(1)} %add.178), channel_id=1, source_target_pairs={{0,2},{1,3},{2,0},{3,1},{4,6},{5,7},{6,4},{7,5},{8,10},{9,11},{10,... | collective-permute-start | bytes 1228808 | tf_op jit(solution)/shard_map/ppermute | solution.py:144
  34.1 1.5 %collective-permute-start.4 = (bf16[256,256]{1,0:T(8,128)(2,1)S(1)}, bf16[256,256]{1,0:T(8,128)(2,1)S(1)}, u32[]{:S(2)}, u32[]{:S(2)}) collective-permute-start(bf16[256,256]{1,0:T(8,128)(2,1)S(1)} %bitcast.47), channel_id=1, source_target_pairs={{0,4},{1,5},{2,6},{3,7},{4,0},{5,1},{6,2},{7,3},{8,12},{9,13},{10,... | collective-permute-start | bytes 393224 | tf_op jit(solution)/shard_map/ppermute | solution.py:144
  35.7 2.4 %collective-permute-start.5 = (bf16[256,256]{1,0:T(8,128)(2,1)S(1)}, bf16[256,256]{1,0:T(8,128)(2,1)S(1)}, u32[]{:S(2)}, u32[]{:S(2)}) collective-permute-start(bf16[256,256]{1,0:T(8,128)(2,1)S(1)} %bitcast.48), channel_id=1, source_target_pairs={{0,8},{1,9},{2,10},{3,11},{4,12},{5,13},{6,14},{7,15},{8,0},{9,1},... | collective-permute-start | bytes 393224 | tf_op jit(solution)/shard_map/ppermute | solution.py:144
  38.6 1.1 %add.177 = f32[4,200,128]{2,1,0:T(8,128)S(1)} add(f32[4,200,128]{2,1,0:T(8,128)} %get-tuple-element.21, f32[4,200,128]{2,1,0:T(8,128)S(1)} %collective-permute-done) | non-fusion elementwise | flops 102400 | bytes 1228800 | tf_op jit(solution)/shard_map/add | solution.py:475
  39.6 3.8 %collective-permute-done.2 = f32[4,200,128]{2,1,0:T(8,128)S(1)} collective-permute-done((f32[4,200,128]{2,1,0:T(8,128)S(1)}, f32[4,200,128]{2,1,0:T(8,128)S(1)}, u32[]{:S(2)}, u32[]{:S(2)}) %collective-permute-start.2) | collective-permute-done | bytes 409632 | tf_op jit(solution)/shard_map/ppermute | solution.py:144
  43.5 5.0 %collective-permute-done.5 = bf16[256,256]{1,0:T(8,128)(2,1)S(1)} collective-permute-done((bf16[256,256]{1,0:T(8,128)(2,1)S(1)}, bf16[256,256]{1,0:T(8,128)(2,1)S(1)}, u32[]{:S(2)}, u32[]{:S(2)}) %collective-permute-start.5) | collective-permute-done | bytes 131104 | tf_op jit(solution)/shard_map/ppermute | solution.py:144
  49.4 2.1 %collective-permute-start.9 = (f32[200,128]{1,0:T(8,128)S(1)}, f32[200,128]{1,0:T(8,128)S(1)}, u32[]{:S(2)}, u32[]{:S(2)}) collective-permute-start(f32[200,128]{1,0:T(8,128)S(1)} %get-tuple-element.28), channel_id=1, source_target_pairs={{0,12},{1,13},{2,14},{3,15},{4,8},{5,9},{6,10},{7,11},{8,4},{9,5},... | collective-permute-start | bytes 307208 | tf_op jit(solution)/shard_map/ppermute | solution.py:144
  51.5 1.3 %collective-permute-start.8 = (f32[200,128]{1,0:T(8,128)S(1)}, f32[200,128]{1,0:T(8,128)S(1)}, u32[]{:S(2)}, u32[]{:S(2)}) collective-permute-start(f32[200,128]{1,0:T(8,128)S(1)} %get-tuple-element.27), channel_id=1, source_target_pairs={{0,8},{1,9},{2,10},{3,11},{4,12},{5,13},{6,14},{7,15},{8,0},{9,1},... | collective-permute-start | bytes 307208 | tf_op jit(solution)/shard_map/ppermute | solution.py:144
  52.8 0.9 collective-permute-start.7
  53.8 3.1 %collective-permute-done.9 = f32[200,128]{1,0:T(8,128)S(1)} collective-permute-done((f32[200,128]{1,0:T(8,128)S(1)}, f32[200,128]{1,0:T(8,128)S(1)}, u32[]{:S(2)}, u32[]{:S(2)}) %collective-permute-start.9) | collective-permute-done | bytes 102432 | tf_op jit(solution)/shard_map/ppermute | solution.py:144
  56.9 2.7 %collective-permute-done.8 = f32[200,128]{1,0:T(8,128)S(1)} collective-permute-done((f32[200,128]{1,0:T(8,128)S(1)}, f32[200,128]{1,0:T(8,128)S(1)}, u32[]{:S(2)}, u32[]{:S(2)}) %collective-permute-start.8) | collective-permute-done | bytes 102432 | tf_op jit(solution)/shard_map/ppermute | solution.py:144
  59.9 3.4 %collective-permute-start.12 = (bf16[200,128]{1,0:T(8,128)(2,1)S(1)}, bf16[200,128]{1,0:T(8,128)(2,1)S(1)}, u32[]{:S(2)}, u32[]{:S(2)}) collective-permute-start(bf16[200,128]{1,0:T(8,128)(2,1)S(1)} %add_convert_fusion.refs_0_), channel_id=1, source_target_pairs={{0,4},{1,5},{2,6},{3,7},{4,0},{5,1},{6,2},{7,3},{8,12},{9,13},{10,... | collective-permute-start | bytes 153608 | tf_op jit(solution)/shard_map/ppermute | solution.py:144
  63.3 1.0 %collective-permute-start.14 = (bf16[200,128]{1,0:T(8,128)(2,1)S(1)}, bf16[200,128]{1,0:T(8,128)(2,1)S(1)}, u32[]{:S(2)}, u32[]{:S(2)}) collective-permute-start(bf16[200,128]{1,0:T(8,128)(2,1)S(1)} %add_convert_fusion.refs_0_), channel_id=1, source_target_pairs={{0,8},{1,9},{2,10},{3,11},{4,12},{5,13},{6,14},{7,15},{8,0},{9,1},... | collective-permute-start | bytes 153608 | tf_op jit(solution)/shard_map/ppermute | solution.py:144
  64.3 1.5 %collective-permute-start.16 = (bf16[200,128]{1,0:T(8,128)(2,1)S(1)}, bf16[200,128]{1,0:T(8,128)(2,1)S(1)}, u32[]{:S(2)}, u32[]{:S(2)}) collective-permute-start(bf16[200,128]{1,0:T(8,128)(2,1)S(1)} %add_convert_fusion.refs_0_), channel_id=1, source_target_pairs={{0,12},{1,13},{2,14},{3,15},{4,8},{5,9},{6,10},{7,11},{8,4},{9,5},... | collective-permute-start | bytes 153608 | tf_op jit(solution)/shard_map/ppermute | solution.py:144
  66.5 1.5 %collective-permute-start.13 = (bf16[200,128]{1,0:T(8,128)(2,1)S(1)}, bf16[200,128]{1,0:T(8,128)(2,1)S(1)}, u32[]{:S(2)}, u32[]{:S(2)}) collective-permute-start(bf16[200,128]{1,0:T(8,128)(2,1)S(1)} %collective-permute-done.12.refs_2_), channel_id=1, source_target_pairs={{0,2},{1,3},{2,0},{3,1},{4,6},{5,7},{6,4},{7,5},{8,10},{9,11},{10,... | collective-permute-start | bytes 153608 | tf_op jit(solution)/shard_map/ppermute | solution.py:144
  68.0 0.9 collective-permute-done.14.refs_4_
  69.4 0.9 collective-permute-done.16.refs_6_
  71.4 1.0 %add.193.target_ref = s32[1024,1]{1,0:T(8,128)} reshape(s32[8,16,8]{2,1,0:T(8,128)S(1)} %iota_add_fusion) | data formatting | bytes 8192 | tf_op jit(solution)/shard_map/add | solution.py:502
  73.0 1.5 %collective-permute-done.17.refs_7_ = bf16[200,128]{1,0:T(8,128)(2,1)S(1)} collective-permute-done((bf16[200,128]{1,0:T(8,128)(2,1)S(1)}, bf16[200,128]{1,0:T(8,128)(2,1)S(1)}, u32[]{:S(2)}, u32[]{:S(2)}) %collective-permute-start.17) | collective-permute-done | bytes 51232 | tf_op jit(solution)/shard_map/ppermute | solution.py:144
  75.1 4.4 %gram_and_cross.1.mine_ref = f32[208,512]{1,0:T(8,128)} custom-call(s32[128]{0:T(128)} %add_add_fusion.starts_ref, s32[1]{0:T(128)} %bitcast.5.place_ref, s32[1024,1]{1,0:T(8,128)} %add.193.target_ref, bf16[200,128]{1,0:T(8,128)(2,1)} %copy-done.3, bf16[200,128]{1,0:T(8,128)(2,1)} %copy-done.8, bf16[200,128]{1,0:T(8,128)(2,1)} %copy-done.5, ...), custom_call_target="tpu_custom_call" | custom-call | tf_op jit(solution)/shard_map/gram_and_cross/pallas_call | solution.py:324
  79.5 2.0 %collective-permute-done.18.other_ref = f32[208,512]{1,0:T(8,128)S(1)} collective-permute-done((f32[208,512]{1,0:T(8,128)}, f32[208,512]{1,0:T(8,128)S(1)}, u32[]{:S(2)}, u32[]{:S(2)}) %collective-permute-start.18) | collective-permute-done | bytes 426016 | tf_op jit(solution)/shard_map/ppermute | solution.py:144
  81.5 0.8 copy-done.2
  82.2 5.4 %solve_weights.1 = (f32[200,200]{1,0:T(8,128)}, bf16[416,200]{1,0:T(8,128)(2,1)}, f32[200,128]{1,0:T(8,128)}, f32[1,256]{1,0:T(1,128)}) custom-call(f32[208,512]{1,0:T(8,128)} %gram_and_cross.1.mine_ref, f32[208,512]{1,0:T(8,128)} %copy-done.2), custom_call_target="tpu_custom_call" | custom-call | tf_op jit(solution)/shard_map/solve_weights/pallas_call | solution.py:391
  87.6 8.7 %slab_update.1 = bf16[200,12288]{1,0:T(8,128)(2,1)} custom-call(bf16[416,200]{1,0:T(8,128)(2,1)} %get-tuple-element.35.parts_ref, f32[200,128]{1,0:T(8,128)} %get-tuple-element.36.lean_ref, bf16[200,12288]{1,0:T(8,128)(2,1)} %slab_ref.1), custom_call_target="tpu_custom_call" | custom-call | tf_op jit(solution)/shard_map/slab_update/pallas_call | solution.py:419
  (84 shorter events, 10.0 us)
Async XLA Ops:
  2.0 14.5 %all-to-all-start = ((s32[16,1,32]{2,1,0:T(1,128)}), s32[16,1,32]{2,1,0:T(1,128)S(1)}, u32[]{:S(2)}, u32[]{:S(2)}) async-start(s32[16,1,32]{2,1,0:T(1,128)} %broadcast_in_dim.10), calls=%async_computation | async-start | bytes 16384 | tf_op jit(solution)/shard_map/all_to_all | solution.py:449
  9.4 6.5 %copy-start.12 = (bf16[256]{0:T(256)(128)(2,1)S(1)}, bf16[256]{0:T(256)(128)(2,1)}, u32[]{:S(2)}) copy-start(bf16[256]{0:T(256)(128)(2,1)} %param.12) | copy-start | bytes 1540
  9.4 6.7 %copy-start.13 = (bf16[256]{0:T(256)(128)(2,1)S(1)}, bf16[256]{0:T(256)(128)(2,1)}, u32[]{:S(2)}) copy-start(bf16[256]{0:T(256)(128)(2,1)} %param.11) | copy-start | bytes 1540
  9.4 6.9 %copy-start.4 = (bf16[256,200]{0,1:T(8,128)(2,1)S(1)}, bf16[256,200]{0,1:T(8,128)(2,1)}, u32[]{:S(2)}) copy-start(bf16[256,200]{0,1:T(8,128)(2,1)} %param.13) | copy-start | bytes 307204
  28.6 2.0 %collective-permute-start.1 = (f32[4,200,128]{2,1,0:T(8,128)}, f32[4,200,128]{2,1,0:T(8,128)S(1)}, u32[]{:S(2)}, u32[]{:S(2)}) collective-permute-start(f32[4,200,128]{2,1,0:T(8,128)} %get-tuple-element.24), channel_id=1, source_target_pairs={{0,1},{1,0},{2,3},{3,2},{4,5},{5,4},{6,7},{7,6},{8,9},{9,8},{10,11... | collective-permute-start | bytes 1228808 | tf_op jit(solution)/shard_map/ppermute | solution.py:144
  29.2 4.9 %collective-permute-start.3 = (bf16[8,16,256]{2,1,0:T(8,128)(2,1)S(1)}, bf16[8,16,256]{2,1,0:T(8,128)(2,1)S(1)}, u32[]{:S(2)}, u32[]{:S(2)}) collective-permute-start(bf16[8,16,256]{2,1,0:T(8,128)(2,1)S(1)} %get-tuple-element.44), channel_id=1, source_target_pairs={{0,1},{1,0},{2,3},{3,2},{4,5},{5,4},{6,7},{7,6},{8,9},{9,8},{10,11... | collective-permute-start | bytes 196616 | tf_op jit(solution)/shard_map/ppermute | solution.py:144
  29.5 9.1 %collective-permute-start = (f32[4,200,128]{2,1,0:T(8,128)}, f32[4,200,128]{2,1,0:T(8,128)S(1)}, u32[]{:S(2)}, u32[]{:S(2)}) collective-permute-start(f32[4,200,128]{2,1,0:T(8,128)} %get-tuple-element.22), channel_id=1, source_target_pairs={{0,1},{1,0},{2,3},{3,2},{4,5},{5,4},{6,7},{7,6},{8,9},{9,8},{10,11... | collective-permute-start | bytes 1228808 | tf_op jit(solution)/shard_map/ppermute | solution.py:144
  31.7 11.8 %collective-permute-start.2 = (f32[4,200,128]{2,1,0:T(8,128)S(1)}, f32[4,200,128]{2,1,0:T(8,128)S(1)}, u32[]{:S(2)}, u32[]{:S(2)}) collective-permute-start(f32[4,200,128]{2,1,0:T(8,128)S(1)} %add.178), channel_id=1, source_target_pairs={{0,2},{1,3},{2,0},{3,1},{4,6},{5,7},{6,4},{7,5},{8,10},{9,11},{10,... | collective-permute-start | bytes 1228808 | tf_op jit(solution)/shard_map/ppermute | solution.py:144
  34.1 9.4 %collective-permute-start.4 = (bf16[256,256]{1,0:T(8,128)(2,1)S(1)}, bf16[256,256]{1,0:T(8,128)(2,1)S(1)}, u32[]{:S(2)}, u32[]{:S(2)}) collective-permute-start(bf16[256,256]{1,0:T(8,128)(2,1)S(1)} %bitcast.47), channel_id=1, source_target_pairs={{0,4},{1,5},{2,6},{3,7},{4,0},{5,1},{6,2},{7,3},{8,12},{9,13},{10,... | collective-permute-start | bytes 393224 | tf_op jit(solution)/shard_map/ppermute | solution.py:144
  35.7 12.9 %collective-permute-start.5 = (bf16[256,256]{1,0:T(8,128)(2,1)S(1)}, bf16[256,256]{1,0:T(8,128)(2,1)S(1)}, u32[]{:S(2)}, u32[]{:S(2)}) collective-permute-start(bf16[256,256]{1,0:T(8,128)(2,1)S(1)} %bitcast.48), channel_id=1, source_target_pairs={{0,8},{1,9},{2,10},{3,11},{4,12},{5,13},{6,14},{7,15},{8,0},{9,1},... | collective-permute-start | bytes 393224 | tf_op jit(solution)/shard_map/ppermute | solution.py:144
  38.0 10.6 %collective-permute-start.6 = (bf16[256,256]{1,0:T(8,128)(2,1)S(1)}, bf16[256,256]{1,0:T(8,128)(2,1)S(1)}, u32[]{:S(2)}, u32[]{:S(2)}) collective-permute-start(bf16[256,256]{1,0:T(8,128)(2,1)S(1)} %bitcast.49), channel_id=1, source_target_pairs={{0,12},{1,13},{2,14},{3,15},{4,8},{5,9},{6,10},{7,11},{8,4},{9,5},... | collective-permute-start | bytes 393224 | tf_op jit(solution)/shard_map/ppermute | solution.py:144
  48.7 25.8 %copy-start = (bf16[4,256,256]{2,1,0:T(8,128)(2,1)}, bf16[4,256,256]{2,1,0:T(8,128)(2,1)S(1)}, u32[]{:S(2)}) copy-start(bf16[4,256,256]{2,1,0:T(8,128)(2,1)S(1)} %pad_maximum_fusion.refs_8_) | copy-start | bytes 1572868
  48.7 11.2 %collective-permute-start.10 = (bf16[4,256,256]{2,1,0:T(8,128)(2,1)S(1)}, bf16[4,256,256]{2,1,0:T(8,128)(2,1)S(1)}, u32[]{:S(2)}, u32[]{:S(2)}) collective-permute-start(bf16[4,256,256]{2,1,0:T(8,128)(2,1)S(1)} %pad_maximum_fusion.refs_8_), channel_id=1, source_target_pairs={{0,2},{1,3},{2,0},{3,1},{4,6},{5,7},{6,4},{7,5},{8,10},{9,11},{10,... | collective-permute-start | bytes 1572872 | tf_op jit(solution)/shard_map/ppermute | solution.py:144
  49.4 7.5 %collective-permute-start.9 = (f32[200,128]{1,0:T(8,128)S(1)}, f32[200,128]{1,0:T(8,128)S(1)}, u32[]{:S(2)}, u32[]{:S(2)}) collective-permute-start(f32[200,128]{1,0:T(8,128)S(1)} %get-tuple-element.28), channel_id=1, source_target_pairs={{0,12},{1,13},{2,14},{3,15},{4,8},{5,9},{6,10},{7,11},{8,4},{9,5},... | collective-permute-start | bytes 307208 | tf_op jit(solution)/shard_map/ppermute | solution.py:144
  51.5 8.1 %collective-permute-start.8 = (f32[200,128]{1,0:T(8,128)S(1)}, f32[200,128]{1,0:T(8,128)S(1)}, u32[]{:S(2)}, u32[]{:S(2)}) collective-permute-start(f32[200,128]{1,0:T(8,128)S(1)} %get-tuple-element.27), channel_id=1, source_target_pairs={{0,8},{1,9},{2,10},{3,11},{4,12},{5,13},{6,14},{7,15},{8,0},{9,1},... | collective-permute-start | bytes 307208 | tf_op jit(solution)/shard_map/ppermute | solution.py:144
  52.8 6.8 %collective-permute-start.7 = (f32[200,128]{1,0:T(8,128)S(1)}, f32[200,128]{1,0:T(8,128)S(1)}, u32[]{:S(2)}, u32[]{:S(2)}) collective-permute-start(f32[200,128]{1,0:T(8,128)S(1)} %get-tuple-element.26), channel_id=1, source_target_pairs={{0,4},{1,5},{2,6},{3,7},{4,0},{5,1},{6,2},{7,3},{8,12},{9,13},{10,... | collective-permute-start | bytes 307208 | tf_op jit(solution)/shard_map/ppermute | solution.py:144
  59.6 14.8 %copy-start.3 = (bf16[200,128]{1,0:T(8,128)(2,1)}, bf16[200,128]{1,0:T(8,128)(2,1)S(1)}, u32[]{:S(2)}) copy-start(bf16[200,128]{1,0:T(8,128)(2,1)S(1)} %add_convert_fusion.refs_0_) | copy-start | bytes 153604
  59.9 14.6 %copy-start.1 = (bf16[4,256,256]{2,1,0:T(8,128)(2,1)}, bf16[4,256,256]{2,1,0:T(8,128)(2,1)S(1)}, u32[]{:S(2)}) copy-start(bf16[4,256,256]{2,1,0:T(8,128)(2,1)S(1)} %collective-permute-done.10.refs_9_) | copy-start | bytes 1572868
  59.9 6.6 %collective-permute-start.12 = (bf16[200,128]{1,0:T(8,128)(2,1)S(1)}, bf16[200,128]{1,0:T(8,128)(2,1)S(1)}, u32[]{:S(2)}, u32[]{:S(2)}) collective-permute-start(bf16[200,128]{1,0:T(8,128)(2,1)S(1)} %add_convert_fusion.refs_0_), channel_id=1, source_target_pairs={{0,4},{1,5},{2,6},{3,7},{4,0},{5,1},{6,2},{7,3},{8,12},{9,13},{10,... | collective-permute-start | bytes 153608 | tf_op jit(solution)/shard_map/ppermute | solution.py:144
  63.3 5.6 %collective-permute-start.14 = (bf16[200,128]{1,0:T(8,128)(2,1)S(1)}, bf16[200,128]{1,0:T(8,128)(2,1)S(1)}, u32[]{:S(2)}, u32[]{:S(2)}) collective-permute-start(bf16[200,128]{1,0:T(8,128)(2,1)S(1)} %add_convert_fusion.refs_0_), channel_id=1, source_target_pairs={{0,8},{1,9},{2,10},{3,11},{4,12},{5,13},{6,14},{7,15},{8,0},{9,1},... | collective-permute-start | bytes 153608 | tf_op jit(solution)/shard_map/ppermute | solution.py:144
  64.3 6.0 %collective-permute-start.16 = (bf16[200,128]{1,0:T(8,128)(2,1)S(1)}, bf16[200,128]{1,0:T(8,128)(2,1)S(1)}, u32[]{:S(2)}, u32[]{:S(2)}) collective-permute-start(bf16[200,128]{1,0:T(8,128)(2,1)S(1)} %add_convert_fusion.refs_0_), channel_id=1, source_target_pairs={{0,12},{1,13},{2,14},{3,15},{4,8},{5,9},{6,10},{7,11},{8,4},{9,5},... | collective-permute-start | bytes 153608 | tf_op jit(solution)/shard_map/ppermute | solution.py:144
  66.0 6.4 %collective-permute-start.11 = (bf16[200,128]{1,0:T(8,128)(2,1)S(1)}, bf16[200,128]{1,0:T(8,128)(2,1)S(1)}, u32[]{:S(2)}, u32[]{:S(2)}) collective-permute-start(bf16[200,128]{1,0:T(8,128)(2,1)S(1)} %add_convert_fusion.refs_0_), channel_id=1, source_target_pairs={{0,2},{1,3},{2,0},{3,1},{4,6},{5,7},{6,4},{7,5},{8,10},{9,11},{10,... | collective-permute-start | bytes 153608 | tf_op jit(solution)/shard_map/ppermute | solution.py:144
  66.5 7.9 %copy-start.5 = (bf16[200,128]{1,0:T(8,128)(2,1)}, bf16[200,128]{1,0:T(8,128)(2,1)S(1)}, u32[]{:S(2)}) copy-start(bf16[200,128]{1,0:T(8,128)(2,1)S(1)} %collective-permute-done.12.refs_2_) | copy-start | bytes 153604
  66.5 5.9 %collective-permute-start.13 = (bf16[200,128]{1,0:T(8,128)(2,1)S(1)}, bf16[200,128]{1,0:T(8,128)(2,1)S(1)}, u32[]{:S(2)}, u32[]{:S(2)}) collective-permute-start(bf16[200,128]{1,0:T(8,128)(2,1)S(1)} %collective-permute-done.12.refs_2_), channel_id=1, source_target_pairs={{0,2},{1,3},{2,0},{3,1},{4,6},{5,7},{6,4},{7,5},{8,10},{9,11},{10,... | collective-permute-start | bytes 153608 | tf_op jit(solution)/shard_map/ppermute | solution.py:144
  68.9 5.6 %copy-start.6 = (bf16[200,128]{1,0:T(8,128)(2,1)}, bf16[200,128]{1,0:T(8,128)(2,1)S(1)}, u32[]{:S(2)}) copy-start(bf16[200,128]{1,0:T(8,128)(2,1)S(1)} %collective-permute-done.14.refs_4_) | copy-start | bytes 153604
  68.9 4.1 %collective-permute-start.15 = (bf16[200,128]{1,0:T(8,128)(2,1)S(1)}, bf16[200,128]{1,0:T(8,128)(2,1)S(1)}, u32[]{:S(2)}, u32[]{:S(2)}) collective-permute-start(bf16[200,128]{1,0:T(8,128)(2,1)S(1)} %collective-permute-done.14.refs_4_), channel_id=1, source_target_pairs={{0,2},{1,3},{2,0},{3,1},{4,6},{5,7},{6,4},{7,5},{8,10},{9,11},{10,... | collective-permute-start | bytes 153608 | tf_op jit(solution)/shard_map/ppermute | solution.py:144
  70.4 4.2 %copy-start.7 = (bf16[200,128]{1,0:T(8,128)(2,1)}, bf16[200,128]{1,0:T(8,128)(2,1)S(1)}, u32[]{:S(2)}) copy-start(bf16[200,128]{1,0:T(8,128)(2,1)S(1)} %collective-permute-done.16.refs_6_) | copy-start | bytes 153604
  70.4 4.1 %collective-permute-start.17 = (bf16[200,128]{1,0:T(8,128)(2,1)S(1)}, bf16[200,128]{1,0:T(8,128)(2,1)S(1)}, u32[]{:S(2)}, u32[]{:S(2)}) collective-permute-start(bf16[200,128]{1,0:T(8,128)(2,1)S(1)} %collective-permute-done.16.refs_6_), channel_id=1, source_target_pairs={{0,2},{1,3},{2,0},{3,1},{4,6},{5,7},{6,4},{7,5},{8,10},{9,11},{10,... | collective-permute-start | bytes 153608 | tf_op jit(solution)/shard_map/ppermute | solution.py:144
  72.4 2.1 %copy-start.8 = (bf16[200,128]{1,0:T(8,128)(2,1)}, bf16[200,128]{1,0:T(8,128)(2,1)S(1)}, u32[]{:S(2)}) copy-start(bf16[200,128]{1,0:T(8,128)(2,1)S(1)} %collective-permute-done.11.refs_1_) | copy-start | bytes 153604
  72.4 2.1 %copy-start.9 = (bf16[200,128]{1,0:T(8,128)(2,1)}, bf16[200,128]{1,0:T(8,128)(2,1)S(1)}, u32[]{:S(2)}) copy-start(bf16[200,128]{1,0:T(8,128)(2,1)S(1)} %collective-permute-done.13.refs_3_) | copy-start | bytes 153604
  73.0 1.6 %copy-start.10 = (bf16[200,128]{1,0:T(8,128)(2,1)}, bf16[200,128]{1,0:T(8,128)(2,1)S(1)}, u32[]{:S(2)}) copy-start(bf16[200,128]{1,0:T(8,128)(2,1)S(1)} %collective-permute-done.15.refs_5_) | copy-start | bytes 153604
  79.5 2.0 %collective-permute-start.18 = (f32[208,512]{1,0:T(8,128)}, f32[208,512]{1,0:T(8,128)S(1)}, u32[]{:S(2)}, u32[]{:S(2)}) collective-permute-start(f32[208,512]{1,0:T(8,128)} %gram_and_cross.1.mine_ref), channel_id=1, source_target_pairs={{0,1},{1,0},{2,3},{3,2},{4,5},{5,4},{6,7},{7,6},{8,9},{9,8},{10,11... | collective-permute-start | bytes 1277960 | tf_op jit(solution)/shard_map/ppermute | solution.py:144
  (2 other events, 1.4 us)

commit v3 on v2

v3 whole, which is shorter than its diff:
```python
import math

import jax
import jax.numpy as jnp
import numpy as np
from jax import lax
from jax.experimental import pallas as pl
from jax.experimental.pallas import tpu as pltpu
from jax.sharding import PartitionSpec as P

BLK = 8
CAP = 2
LANE = 128

inflation = 4.0
epsilon = 1e-06

VMEM_LIMIT = 24 * 1024 * 1024
MAPS_LIMIT = 44 * 1024 * 1024
SLAB_LIMIT = 50 * 1024 * 1024


def dct_table(length):
    frequency = jnp.arange(length, dtype=jnp.float32)[:, None]
    sample = jnp.arange(length, dtype=jnp.float32)[None, :]
    cosine_table = jnp.cos(math.pi * (2.0 * sample + 1.0) * frequency / (2.0 * length))
    factor = jnp.where(frequency == 0, math.sqrt(1.0 / length), math.sqrt(2.0 / length))
    return (cosine_table * factor).astype(jnp.bfloat16)


def dct_constant(length):
    frequency = np.arange(length, dtype=np.float32)[:, None]
    sample = np.arange(length, dtype=np.float32)[None, :]
    angle = np.float32(math.pi) * (np.float32(2.0) * sample + np.float32(1.0)) * frequency
    cosine_table = np.cos(angle / np.float32(2.0 * length))
    factor = np.where(
        frequency == 0, np.float32(math.sqrt(1.0 / length)), np.float32(math.sqrt(2.0 / length))
    )
    return (cosine_table * factor).astype(jnp.bfloat16)


def gram_terms(predicted, observed_rows, scale_rows, noise_rows, live_mask, weight_scale):
    members = predicted.shape[1]
    center = jnp.mean(predicted, axis=1, keepdims=True)
    anomaly = (predicted - center) / math.sqrt(members - 1)
    weight = live_mask * weight_scale / (scale_rows * scale_rows)
    mismatch = (
        observed_rows[:, None] + math.sqrt(inflation) * scale_rows[:, None] * noise_rows - predicted
    )
    weighted = anomaly * weight[:, None]
    contract = (((0,), (0,)), ((), ()))
    gram_matrix = lax.dot_general(anomaly, weighted, contract, precision=lax.Precision.HIGHEST)
    cross_terms = lax.dot_general(weighted, mismatch, contract, precision=lax.Precision.HIGHEST)
    relative = mismatch / scale_rows[:, None]
    misfit_rows = live_mask * jnp.sqrt(jnp.mean(relative * relative, axis=1) + epsilon)
    return (gram_matrix, cross_terms, misfit_rows)


def solve_weights(gram_matrix, cross_terms):
    members = gram_matrix.shape[0]
    factor = jnp.linalg.cholesky(gram_matrix + inflation * jnp.eye(members, dtype=jnp.float32))
    return jax.scipy.linalg.cho_solve((factor, True), cross_terms)


def update_state(block, update_weights):
    state = block.astype(jnp.float32)
    members = state.shape[0]
    anomaly = (state - jnp.mean(state, axis=0, keepdims=True)) / math.sqrt(members - 1)
    moved = state + lax.dot_general(
        update_weights, anomaly, (((0,), (0,)), ((), ())), precision=lax.Precision.HIGHEST
    )
    return moved.astype(jnp.bfloat16)


def dense_body(
    amplitude_maps, kept_blocks, block_owner, observed, error_scale, perturbation, model_slab
):
    members, rows_here, map_width = amplitude_maps.shape
    devices = lax.axis_size("map")
    map_height = rows_here * devices
    table_w = dct_table(map_width)
    table_h = dct_table(map_height)
    rowwise = jnp.einsum(
        "ehw,kw->hke", amplitude_maps, table_w, preferred_element_type=jnp.float32
    ).astype(jnp.bfloat16)
    coefficients = jnp.einsum(
        "kh,hwe->wke",
        table_h,
        lax.all_to_all(rowwise, "map", split_axis=1, concat_axis=0, tiled=True),
        preferred_element_type=jnp.float32,
    ).astype(jnp.bfloat16)
    block_rows = coefficients.reshape(-1, BLK * members)
    candidates = block_rows.shape[0]
    keep_count = kept_blocks.shape[0]
    slot_count = devices * CAP
    dest_owner = block_owner[:, 0]
    positions = jnp.arange(keep_count, dtype=jnp.int32)
    earlier = (dest_owner[:, None] == dest_owner[None, :]) & (
        positions[None, :] < positions[:, None]
    )
    slot_rank = jnp.sum(earlier.astype(jnp.int32), axis=1)
    slot_index = dest_owner * CAP + slot_rank
    pick_slot = (slot_index[:, None] == jnp.arange(slot_count, dtype=jnp.int32)[None, :]).astype(
        jnp.bfloat16
    )
    weight_scale = members / (devices * keep_count * BLK)
    contract = (((0,), (0,)), ((), ()))
    pick_block = (kept_blocks[:, None] == jnp.arange(candidates, dtype=jnp.int32)[None, :]).astype(
        jnp.bfloat16
    )
    routing = lax.dot_general(
        pick_slot, pick_block, contract, preferred_element_type=jnp.float32
    ).astype(jnp.bfloat16)
    outgoing = jnp.dot(routing, block_rows, preferred_element_type=jnp.float32).astype(jnp.bfloat16)
    live_slots = jnp.sum(pick_slot.astype(jnp.float32), axis=0).astype(jnp.bfloat16)
    arrived, arrived_live = (
        lax.all_to_all(
            outgoing.reshape(devices, CAP, BLK * members),
            "map",
            split_axis=0,
            concat_axis=0,
            tiled=True,
        ),
        lax.all_to_all(
            live_slots.reshape(devices, CAP), "map", split_axis=0, concat_axis=0, tiled=True
        ),
    )
    predicted = arrived.reshape(-1, members).astype(jnp.float32)
    live_mask = jnp.repeat(arrived_live.astype(jnp.float32).reshape(-1), BLK)
    gram_matrix, cross_terms, data_misfit = gram_terms(
        predicted,
        observed.astype(jnp.float32),
        error_scale.astype(jnp.float32),
        perturbation.astype(jnp.float32),
        live_mask,
        weight_scale,
    )
    gram_matrix, cross_terms = lax.psum((gram_matrix, cross_terms), "map")
    update_weights = solve_weights(gram_matrix, cross_terms)
    updated_slab = update_state(model_slab, update_weights)
    return (updated_slab, update_weights, data_misfit)


def swap(value, delta):
    pairs = [(i, i ^ delta) for i in range(lax.axis_size("map"))]
    return lax.ppermute(value, "map", pairs)


VMEM = pl.BlockSpec(memory_space=pltpu.VMEM)
SMEM = pl.BlockSpec(memory_space=pltpu.SMEM)
HBM = pl.BlockSpec(memory_space=pltpu.HBM)


def by_row_kernel(maps_ref, out_ref, held_ref, arrived):
    width = maps_ref.shape[2]
    copies = []
    for i in range(width // LANE):
        part = pl.ds(i * LANE, LANE)
        copies.append(
            pltpu.make_async_copy(maps_ref.at[:, :, part], held_ref.at[i], arrived.at[i])
        )
        copies[i].start()
    for i in range(width // LANE):
        copies[i].wait()
        out_ref[:, :, i * LANE : (i + 1) * LANE] = jnp.swapaxes(held_ref[i], 0, 1)


def by_row(amplitude_maps):
    members, rows, width = amplitude_maps.shape
    parts = width // LANE
    return pl.pallas_call(
        by_row_kernel,
        in_specs=[HBM],
        out_specs=VMEM,
        out_shape=jax.ShapeDtypeStruct((rows, members, width), jnp.bfloat16),
        scratch_shapes=[
            pltpu.VMEM((parts, members, rows, LANE), jnp.bfloat16),
            pltpu.SemaphoreType.DMA((parts,)),
        ],
        compiler_params=pltpu.CompilerParams(vmem_limit_bytes=MAPS_LIMIT),
        cost_estimate=pl.CostEstimate(
            flops=0, bytes_accessed=4 * members * rows * width, transcendentals=0
        ),
        name="maps_by_row",
    )(amplitude_maps)


def shares_kernel(
    list0_ref, list1_ref, list2_ref, list3_ref, place_ref, maps_ref, table_w_ref, table_h_ref, k0_ref, k1_ref, s0_ref, s1_ref,
    full_ref, pick_ref, row_ref, spread_ref, wide_ref,
):
    rows, members, width = maps_ref.shape
    devices, depth, _ = row_ref.shape
    keep = depth // rows
    height = table_h_ref.shape[0]
    per_column = height // BLK
    columns_here = width // devices
    me = place_ref[0]
    list_refs = (list0_ref, list1_ref, list2_ref, list3_ref)

    def block(delta, p):
        return list_refs[delta // 4][delta % 4, p]

    full_ref[...] = table_w_ref[...].astype(jnp.float32)
    for delta in range(devices):
        for p in range(keep):
            column = (me ^ delta) * columns_here + block(delta, p) // per_column
            pick_ref[pl.ds(delta * keep + p, 1), :] = full_ref[pl.ds(column, 1), :]
    sample = lax.broadcasted_iota(jnp.int32, (height, depth), 0) - me * rows
    held = lax.broadcasted_iota(jnp.int32, (height, depth), 1) // keep
    spread_ref[...] = jnp.dot(
        table_h_ref[...], (sample == held).astype(jnp.bfloat16), preferred_element_type=jnp.float32
    )

    pick = pick_ref[...].astype(jnp.bfloat16)
    for row in range(rows):
        rowwise = lax.dot_general(
            pick, maps_ref[row], (((1,), (1,)), ((), ())), preferred_element_type=jnp.float32
        ).astype(jnp.bfloat16)
        row_ref[:, row * keep : (row + 1) * keep, :] = rowwise.reshape(devices, keep, members)

    position = lax.broadcasted_iota(jnp.int32, (BLK, depth), 1) % keep
    for out_ref, low in ((s1_ref, 3), (k1_ref, 2), (s0_ref, 1), (k0_ref, 0)):
        for high in range(out_ref.shape[0]):
            delta = high * 4 + low
            for p in range(keep):
                start = pl.multiple_of(block(delta, p) % per_column * BLK, BLK)
                cosines = spread_ref[pl.ds(start, BLK), :]
                wide_ref[p * BLK : (p + 1) * BLK, :] = jnp.where(position == p, cosines, 0.0)
            share = jnp.dot(
                wide_ref[...].astype(jnp.bfloat16), row_ref[delta],
                preferred_element_type=jnp.float32,
            )
            out_ref[high] = share.T


def shares(lists, place, maps, table_w, table_h):
    rows, members, width = maps.shape
    devices = sum(part.shape[0] for part in lists)
    keep = lists[0].shape[1] // 2
    depth = rows * keep
    out = jax.ShapeDtypeStruct((devices // 4, members, keep * BLK), jnp.float32)
    return pl.pallas_call(
        shares_kernel,
        in_specs=[SMEM] * 5 + [VMEM] * 3,
        out_specs=[VMEM] * 4,
        out_shape=[out] * 4,
        scratch_shapes=[
            pltpu.VMEM(table_w.shape, jnp.float32),
            pltpu.VMEM((devices * keep, width), jnp.float32),
            pltpu.VMEM((devices, depth, members), jnp.bfloat16),
            pltpu.VMEM((table_h.shape[0], depth), jnp.float32),
            pltpu.VMEM((keep * BLK, depth), jnp.float32),
        ],
        compiler_params=pltpu.CompilerParams(vmem_limit_bytes=VMEM_LIMIT),
        cost_estimate=pl.CostEstimate(
            flops=2 * devices * keep * width * rows * members,
            bytes_accessed=2 * rows * members * width,
            transcendentals=0,
        ),
        name="coefficient_shares",
    )(*lists, place, maps, table_w, table_h)


def split_noise_kernel(place_ref, noise_ref, observed_ref, scale_ref, keep_ref, send_ref):
    members, slots = noise_ref.shape
    half = slots // 2
    core = place_ref[0] & 1
    span = 2 * CAP * BLK // 2
    row = lax.broadcasted_iota(jnp.int32, (slots, slots), 0)
    lane = lax.broadcasted_iota(jnp.int32, (slots, slots), 1)
    kind = lane // half ^ core
    source = lane % half // span * (2 * span) + kind * span + lane % span
    picked = (row == source).astype(jnp.bfloat16)
    extra = jnp.zeros((keep_ref.shape[0] - members - 2, slots), jnp.float32)
    value = jnp.concatenate(
        [
            noise_ref[...].astype(jnp.float32),
            observed_ref[...].astype(jnp.float32),
            scale_ref[...].astype(jnp.float32),
            extra,
        ],
        axis=0,
    ).astype(jnp.bfloat16)
    moved = jnp.dot(value, picked, preferred_element_type=jnp.float32).astype(jnp.bfloat16)
    keep_ref[...] = moved[:, 0:half]
    send_ref[...] = moved[:, half:slots]


def split_noise(place, noise, observed, scale):
    members, slots = noise.shape
    rows = -(-(members + 2) // 16) * 16
    out = jax.ShapeDtypeStruct((rows, slots // 2), jnp.bfloat16)
    return pl.pallas_call(
        split_noise_kernel,
        in_specs=[SMEM] + [VMEM] * 3,
        out_specs=[VMEM] * 2,
        out_shape=[out] * 2,
        compiler_params=pltpu.CompilerParams(vmem_limit_bytes=VMEM_LIMIT),
        name="split_noise",
    )(place, noise, observed, scale)


def select_noise_kernel(starts_ref, place_ref, near_ref, far_ref, out_ref, wide_ref, rows_ref):
    rows, per = near_ref.shape[-2:]
    chips = out_ref.shape[0]
    keep = per // BLK
    chip = place_ref[0]
    units = near_ref.shape[0] * near_ref.shape[1]
    wide_ref[:, rows:256] = jnp.zeros((wide_ref.shape[0], 256 - rows), jnp.float32)
    for i, ref in enumerate((near_ref, far_ref)):
        for z in range(near_ref.shape[0]):
            for c in range(near_ref.shape[1]):
                unit = i * units + z * near_ref.shape[1] + c
                wide_ref[unit * per : (unit + 1) * per, 0:rows] = ref[z, c].astype(jnp.float32).T
    for i in range(chips):
        for p in range(keep):
            start = pl.multiple_of(starts_ref[i * keep + p], BLK)
            rows_ref[p * BLK : (p + 1) * BLK, :] = wide_ref[pl.ds(start, BLK), :]
        out_ref[chip ^ i] = rows_ref[...].T[0:rows]


def select_noise(starts, place, near, far):
    rows, per = near.shape[-2:]
    chips = starts.shape[0] * BLK // per
    return pl.pallas_call(
        select_noise_kernel,
        in_specs=[SMEM, SMEM, VMEM, VMEM],
        out_specs=VMEM,
        out_shape=jax.ShapeDtypeStruct((chips, rows, per), jnp.float32),
        scratch_shapes=[
            pltpu.VMEM((2 * near.shape[0] * near.shape[1] * per, 256), jnp.float32),
            pltpu.VMEM((per, 256), jnp.float32),
        ],
        compiler_params=pltpu.CompilerParams(vmem_limit_bytes=VMEM_LIMIT),
        name="select_noise",
    )(starts, place, near, far)


def gram_kernel(place_ref, target_ref, noise_ref, *refs):
    predicted_refs = refs[:8]
    out_ref, predicted_ref, left_ref, right_ref, misfit_ref = refs[8:]
    groups, members, per = predicted_ref.shape
    coefficients = groups * per
    weight_scale = members / (2 * coefficients)
    chip = place_ref[0]
    for i, ref in enumerate(predicted_refs):
        predicted_ref[chip ^ i] = ref[...].astype(jnp.float32)
    right_ref[...] = jnp.zeros_like(right_ref)
    for g in range(groups):
        noise = noise_ref[g]
        observed = noise[members : members + 1]
        scale = noise[members + 1 : members + 2]
        predicted = predicted_ref[g]
        center = jnp.sum(predicted, axis=0, keepdims=True) * (1.0 / members)
        anomaly = (predicted - center) * (1.0 / math.sqrt(members - 1))
        weight = weight_scale / (scale * scale)
        mismatch = observed + math.sqrt(inflation) * scale * noise[:members] - predicted
        here = pl.ds(g * per, per)
        left_ref[:, here] = anomaly * weight
        right_ref[0:members, here] = anomaly
        right_ref[256 : 256 + members, here] = mismatch
        relative = mismatch / scale
        misfit = jnp.sqrt(
            jnp.sum(relative * relative, axis=0, keepdims=True) * (1.0 / members) + epsilon
        )
        high = misfit.astype(jnp.bfloat16)
        rest = misfit - high.astype(jnp.float32)
        middle = rest.astype(jnp.bfloat16)
        low = (rest - middle.astype(jnp.float32)).astype(jnp.bfloat16)
        misfit_ref[0:1, here] = high.astype(jnp.float32)
        misfit_ref[1:2, here] = middle.astype(jnp.float32)
        misfit_ref[2:3, here] = low.astype(jnp.float32)
        misfit_ref[3:8, here] = jnp.zeros((5, per), jnp.float32)
    out_ref[0:members, :] = lax.dot_general(
        left_ref[...], right_ref[...], (((1,), (1,)), ((), ())),
        precision=lax.Precision.HIGHEST, preferred_element_type=jnp.float32,
    )
    lanes = lax.broadcasted_iota(jnp.int32, (per, out_ref.shape[1]), 1)
    one_hot = jnp.concatenate(
        [(target_ref[chip ^ g] == lanes).astype(jnp.bfloat16) for g in range(groups)], axis=0
    )
    routed = jnp.dot(
        misfit_ref[...].astype(jnp.bfloat16), one_hot, preferred_element_type=jnp.float32
    )
    out_ref[members : members + 8, :] = jnp.broadcast_to(
        routed[0:1] + routed[1:2] + routed[2:3], (8, out_ref.shape[1])
    )


def gram(place, target, noise, predicted):
    members, per = predicted[0].shape
    groups = len(predicted)
    coefficients = groups * per
    return pl.pallas_call(
        gram_kernel,
        in_specs=[SMEM] + [VMEM] * (2 + len(predicted)),
        out_specs=VMEM,
        out_shape=jax.ShapeDtypeStruct((members + 8, 512), jnp.float32),
        scratch_shapes=[
            pltpu.VMEM((groups, members, per), jnp.float32),
            pltpu.VMEM((members, coefficients), jnp.float32),
            pltpu.VMEM((512, coefficients), jnp.float32),
            pltpu.VMEM((8, coefficients), jnp.float32),
        ],
        compiler_params=pltpu.CompilerParams(vmem_limit_bytes=VMEM_LIMIT),
        name="gram_and_cross",
    )(place, target, noise, *predicted)


def update_kernel(
    mine_ref, other_ref, slab_ref, out_ref, weights_ref, misfit_ref,
    state_ref, held_ref, arrived, left,
):
    members, cells = held_ref.shape
    tiles = arrived.shape[0]
    tile = cells // tiles
    parts = [pl.ds(i * tile, tile) for i in range(tiles)]
    reads = [
        pltpu.make_async_copy(slab_ref.at[:, part], held_ref.at[:, part], arrived.at[i])
        for i, part in enumerate(parts)
    ]
    writes = [
        pltpu.make_async_copy(held_ref.at[:, part], out_ref.at[:, part], left.at[i])
        for i, part in enumerate(parts)
    ]
    for read in reads:
        read.start()

    total = mine_ref[0:members, :] + other_ref[0:members, :]
    misfit_ref[...] = (
        mine_ref[members : members + 1, 0:256] + other_ref[members : members + 1, 256:512]
    )
    row = lax.broadcasted_iota(jnp.int32, (members, 256), 0)
    lane = lax.broadcasted_iota(jnp.int32, (members, 256), 1)
    unit = jnp.where(row == lane, 1.0, 0.0)
    matrix = total[:, 0:256] + inflation * unit
    bound = jnp.max(jnp.sum(jnp.abs(matrix), axis=1, keepdims=True), axis=0, keepdims=True)
    step = 2.0 / (inflation + bound)
    state_ref[members:256, :] = jnp.zeros((256 - members, 512), jnp.float32)
    state_ref[0:members, 0:256] = unit - step * matrix
    state_ref[0:members, 256:512] = step * total[:, 256:512]

    def more(carry):
        return carry[0] > 2.0**-24

    def double(carry):
        power = state_ref[:, 0:256]
        size = jnp.sum(power * power)
        moved = jnp.dot(
            power, state_ref[...], precision=lax.Precision.HIGHEST,
            preferred_element_type=jnp.float32,
        )
        state_ref[:, 0:256] = moved[:, 0:256]
        state_ref[:, 256:512] = state_ref[:, 256:512] + moved[:, 256:512]
        return (size,)

    lax.while_loop(more, double, (jnp.float32(1.0),))
    weights_ref[...] = state_ref[0:members, 256 : 256 + members]

    full = state_ref[:, 256:512]
    center = jnp.sum(full, axis=0, keepdims=True) * (1.0 / members)
    spread = ((full - center) * (1.0 / math.sqrt(members - 1))).T[0:members, 0:members]
    high = spread.astype(jnp.bfloat16)
    rest = spread - high.astype(jnp.float32)
    middle = rest.astype(jnp.bfloat16)
    low = (rest - middle.astype(jnp.float32)).astype(jnp.bfloat16)
    for i in range(tiles):
        reads[i].wait()
        for j in range(i * tile, (i + 1) * tile, 256):
            state = held_ref[:, j : j + 256]
            moved = jnp.dot(low, state, preferred_element_type=jnp.float32)
            moved = moved + jnp.dot(middle, state, preferred_element_type=jnp.float32)
            moved = moved + jnp.dot(high, state, preferred_element_type=jnp.float32)
            held_ref[:, j : j + 256] = (state.astype(jnp.float32) + moved).astype(jnp.bfloat16)
        writes[i].start()
    for write in writes:
        write.wait()


def update(mine, other, slab):
    members, cells = slab.shape
    tiles = cells // 1024
    return pl.pallas_call(
        update_kernel,
        in_specs=[VMEM, VMEM, HBM],
        out_specs=[HBM, VMEM, VMEM],
        out_shape=[
            jax.ShapeDtypeStruct(slab.shape, slab.dtype),
            jax.ShapeDtypeStruct((members, members), jnp.float32),
            jax.ShapeDtypeStruct((1, 256), jnp.float32),
        ],
        scratch_shapes=[
            pltpu.VMEM((256, 512), jnp.float32),
            pltpu.VMEM(slab.shape, slab.dtype),
            pltpu.SemaphoreType.DMA((tiles,)),
            pltpu.SemaphoreType.DMA((tiles,)),
        ],
        compiler_params=pltpu.CompilerParams(vmem_limit_bytes=SLAB_LIMIT),
        name="solve_and_update",
    )(mine, other, slab)


def sparse_body(
    amplitude_maps, kept_blocks, block_owner, observed, error_scale, perturbation, model_slab
):
    members, rows_here, map_width = amplitude_maps.shape
    devices = lax.axis_size("map")
    map_height = rows_here * devices
    keep = kept_blocks.shape[0]
    slots = observed.shape[0]
    me = lax.axis_index("map").astype(jnp.int32)
    core, chip = me & 1, me >> 1

    lists = jnp.concatenate([kept_blocks, block_owner[:, 0]])
    lists = jnp.stack([lists] + [swap(lists, delta) for delta in range(1, 4)])

    noise_keep, noise_send = split_noise(
        me.reshape(1), perturbation.T, observed[None, :], error_scale[None, :]
    )
    noise = jnp.stack([noise_keep, swap(noise_send, 1)])
    amplitude_maps, noise, lists = lax.optimization_barrier((amplitude_maps, noise, lists))
    lists = [lists] + [swap(lists, 4 * i) for i in range(1, devices // 4)]
    noises = [noise] + [swap(noise, 4 * i) for i in range(1, devices // 4)]

    maps = by_row(amplitude_maps)
    table_w = jnp.asarray(dct_constant(map_width))
    table_h = table_w if map_height == map_width else jnp.asarray(dct_constant(map_height))
    keep_0, keep_1, send_0, send_1 = shares(lists, me.reshape(1), maps, table_w, table_h)

    share_1 = keep_1 + swap(send_1, 1)
    got_1 = swap(share_1, 2)
    share_0 = keep_0 + swap(send_0, 1)
    share = [share_0[i] + got_1[i] for i in range(devices // 4)]
    share, noises = lax.optimization_barrier((share, noises))
    near_noise = jnp.stack(noises)
    far_noise = swap(near_noise, 2)
    got = [swap(share[i], 4 * i) for i in range(1, devices // 4)]
    predicted = (share[0] + got[0] + got[1] + got[2]).astype(jnp.bfloat16)
    predicted, far_noise = lax.optimization_barrier((predicted, far_noise))

    near = [predicted] + [swap(predicted, 4 * i) for i in range(1, devices // 4)]
    gathered = []
    for value in near:
        gathered += [value, swap(value, 2)]

    owner = jnp.concatenate(lists)[0::2, keep:]
    positions = jnp.arange(keep, dtype=jnp.int32)
    earlier = (owner[:, :, None] == owner[:, None, :]) & (
        positions[None, None, :] < positions[None, :, None]
    )
    rank = jnp.sum(earlier.astype(jnp.int32), axis=2)
    chips = chip ^ jnp.arange(devices // 2, dtype=jnp.int32)[:, None]
    away = owner ^ me
    held = (away >> 1 & 1) * 8 + (away >> 2) * 2 + (away & 1)
    noise_rows = held * (slots // 2) + chips * (CAP * BLK) + rank * BLK
    data_row = (chips * 2 + core) * (CAP * BLK) + rank * BLK
    target = jnp.where(away < 2, away * slots + data_row, -1024)
    target = (target[:, :, None] + jnp.arange(BLK, dtype=jnp.int32)).reshape(
        devices // 2, keep * BLK, 1
    )
    noise = select_noise(noise_rows.reshape(-1), chip.reshape(1), near_noise, far_noise)
    mine = gram(chip.reshape(1), target, noise, gathered)
    updated_slab, update_weights, data_misfit = update(mine, swap(mine, 1), model_slab)
    return (updated_slab, update_weights, data_misfit.reshape(-1))


def solution(mesh):
    in_specs = (
        P("groups", "map", None),
        P(("groups", "map")),
        P(("groups", "map"), None),
        P(("groups", "map")),
        P(("groups", "map")),
        P(("groups", "map"), None),
        P(None, ("groups", "map")),
    )
    out_specs = (P(None, ("groups", "map")), P("groups", None), P(("groups", "map")))

    def body(amplitude_maps, kept_blocks, *rest):
        few = mesh.shape["map"] == 16 and kept_blocks.shape[0] * BLK == LANE
        chosen = sparse_body if few else dense_body
        return chosen(amplitude_maps, kept_blocks, *rest)

    return jax.shard_map(body, mesh=mesh, in_specs=in_specs, out_specs=out_specs, check_vma=False)
```

time: 96.9 us -> 79.1 us (0.82)
  Pallas kernels: 34 us -> 23.5 us
  other arithmetic: 6.16 us -> 1.54 us
  local copies, waits for them, and re-layouts: 4.98 us -> 2.74 us
    pallas_call x5 -> x6, Pallas kernels: 34 us -> 23.5 us  [the longest x1 11.1 us: update(): pl.pallas_call(update_kernel, in_specs=[VMEM, VMEM, HBM], out_specs=[HBM,...]
    all_to_all x1 -> x0, starting transfers between devices: 7.36 us -> none  [sparse_body(): lax.all_to_all(jnp.broadcast_to(lists, (devices, 2 * keep)), 'map', split...]
    ppermute x19 -> x25, starting transfers between devices: 21.5 us -> 28.3 us  [swap(): return lax.ppermute(value, 'map', pairs)]
    add x1, other arithmetic: 1.06 us -> 0.05 us  [sparse_body(): share_0 = keep_0 + swap(send_0, 1)]
    add x1, other arithmetic: 1.04 us -> 0.06 us  [sparse_body(): share_1 = keep_1 + swap(send_1, 1)]
    ppermute x19 -> x25, waiting for transfers between devices: 21.3 us -> 21.9 us  [swap(): return lax.ppermute(value, 'map', pairs)]
  transfers between devices with their start and end apart: 20 -> 25, of which waited for: 11 -> 12; matrix products, arithmetic and copies ran while one was open for 6% -> 3% of each run, Pallas kernels for 6% -> 6%
where the time goes in v3:
time: 79.1 us; the launch traced here: 78.9 us
  starting transfers between devices  28.3 us (36%)
  Pallas kernels  23.5 us (30%)
  waiting for transfers between devices  21.9 us (28%)
  local copies, waits for them, and re-layouts  2.74 us (3%)
  other arithmetic  1.54 us (2%)
  between operations  0.98 us (1%)
    ppermute x25, starting transfers between devices, swap(): return lax.ppermute(value, 'map', pairs)  28.3 us
    ppermute x25, waiting for transfers between devices, swap(): return lax.ppermute(value, 'map', pairs)  21.9 us
    pallas_call x1, Pallas kernels, update(): pl.pallas_call(update_kernel, in_specs=[VMEM, VMEM, HBM], out_specs=[HBM,...  11.1 us
    pallas_call x1, Pallas kernels, shares(): pl.pallas_call(shares_kernel, in_specs=[SMEM] * 5 + [VMEM] * 3, out_specs...  5.4 us
    pallas_call x1, Pallas kernels, by_row(): pl.pallas_call(by_row_kernel, in_specs=[HBM], out_specs=VMEM, out_shape=j...  3.66 us
    pallas_call x1, Pallas kernels, gram(): pl.pallas_call(gram_kernel, in_specs=[SMEM] + [VMEM] * (2 + len(predicted...  1.98 us
  transfers between devices with their start and end apart: 25, of which 12 were waited for; matrix products, arithmetic and copies ran while one was open for 3% of the time, Pallas kernels for 6%

profile of v3, /device:TPU:0, one launch (start us, length us, event | category | flops | bytes accessed | tf_op | source)
XLA Modules:
  0.0 78.9 jit_solution(10323744997592526053)
XLA Ops:
  0.6 0.7 pad_add_fusion.2
  1.8 2.5 %collective-permute-start.2 = (s32[32]{0:T(128)S(1)}, s32[32]{0:T(128)S(1)}, u32[]{:S(2)}, u32[]{:S(2)}) collective-permute-start(s32[32]{0:T(128)S(1)} %pad_add_fusion.2), channel_id=1, source_target_pairs={{0,2},{1,3},{2,0},{3,1},{4,6},{5,7},{6,4},{7,5},{8,10},{9,11},{10,... | collective-permute-start | bytes 392 | tf_op jit(solution)/shard_map/ppermute | solution.py:146
  5.8 0.9 %copy-done.1 = bf16[256,200]{0,1:T(8,128)(2,1)S(1)} copy-done((bf16[256,200]{0,1:T(8,128)(2,1)S(1)}, bf16[256,200]{0,1:T(8,128)(2,1)}, u32[]{:S(2)}) %copy-start.1) | copy-done | bytes 102424
  7.4 0.8 %collective-permute-done = bf16[208,128]{1,0:T(8,128)(2,1)S(1)} collective-permute-done((bf16[208,128]{1,0:T(8,128)(2,1)S(1)}, bf16[208,128]{1,0:T(8,128)(2,1)S(1)}, u32[]{:S(2)}, u32[]{:S(2)}) %collective-permute-start) | collective-permute-done | bytes 53280 | tf_op jit(solution)/shard_map/ppermute | solution.py:146
  8.2 1.9 %collective-permute-start.4 = (s32[4,32]{1,0:T(4,128)S(1)}, s32[4,32]{1,0:T(4,128)S(1)}, u32[]{:S(2)}, u32[]{:S(2)}) collective-permute-start(s32[4,32]{1,0:T(4,128)S(1)} %pad_add_fusion.1.list0_ref), channel_id=1, source_target_pairs={{0,4},{1,5},{2,6},{3,7},{4,0},{5,1},{6,2},{7,3},{8,12},{9,13},{10,... | collective-permute-start | bytes 1544 | tf_op jit(solution)/shard_map/ppermute | solution.py:146
  10.1 2.6 %collective-permute-start.5 = (s32[4,32]{1,0:T(4,128)S(1)}, s32[4,32]{1,0:T(4,128)S(1)}, u32[]{:S(2)}, u32[]{:S(2)}) collective-permute-start(s32[4,32]{1,0:T(4,128)S(1)} %pad_add_fusion.1.list0_ref), channel_id=1, source_target_pairs={{0,8},{1,9},{2,10},{3,11},{4,12},{5,13},{6,14},{7,15},{8,0},{9,1},... | collective-permute-start | bytes 1544 | tf_op jit(solution)/shard_map/ppermute | solution.py:146
  12.7 3.7 %maps_by_row.1.maps_ref = bf16[32,200,512]{2,1,0:T(8,128)(2,1)S(1)} custom-call(bf16[200,32,512]{2,1,0:T(8,128)(2,1)} %maps_ref), custom_call_target="tpu_custom_call" | custom-call | bytes 13107200 | tf_op jit(solution)/shard_map/maps_by_row/pallas_call | solution.py:171
  16.3 1.7 %collective-permute-done.6.list3_ref = s32[4,32]{1,0:T(4,128)S(1)} collective-permute-done((s32[4,32]{1,0:T(4,128)S(1)}, s32[4,32]{1,0:T(4,128)S(1)}, u32[]{:S(2)}, u32[]{:S(2)}) %collective-permute-start.6) | collective-permute-done | bytes 544 | tf_op jit(solution)/shard_map/ppermute | solution.py:146
  18.0 5.4 %coefficient_shares.1 = (f32[4,200,128]{2,1,0:T(8,128)S(1)}, f32[4,200,128]{2,1,0:T(8,128)S(1)}, f32[4,200,128]{2,1,0:T(8,128)S(1)}, f32[4,200,128]{2,1,0:T(8,128)S(1)}) custom-call(s32[4,32]{1,0:T(4,128)S(1)} %pad_add_fusion.1.list0_ref, s32[4,32]{1,0:T(4,128)S(1)} %collective-permute-done.4.list1_ref, s32[4,32]{1,0:T(4,128)S(1)} %collective-permute-done.5.list2_ref, ...), custom_call_target="tpu_custom_call" | custom-call | flops 1677721600 | bytes 6553600 | tf_op jit(solution)/shard_map/coefficient_shares/pallas_call | solution.py:243
  24.0 1.2 %collective-permute-done.8 = f32[4,200,128]{2,1,0:T(8,128)S(1)} collective-permute-done((f32[4,200,128]{2,1,0:T(8,128)S(1)}, f32[4,200,128]{2,1,0:T(8,128)S(1)}, u32[]{:S(2)}, u32[]{:S(2)}) %collective-permute-start.8) | collective-permute-done | bytes 409632 | tf_op jit(solution)/shard_map/ppermute | solution.py:146
  25.3 1.5 %collective-permute-start.9 = (f32[4,200,128]{2,1,0:T(8,128)S(1)}, f32[4,200,128]{2,1,0:T(8,128)S(1)}, u32[]{:S(2)}, u32[]{:S(2)}) collective-permute-start(f32[4,200,128]{2,1,0:T(8,128)S(1)} %add.121), channel_id=1, source_target_pairs={{0,2},{1,3},{2,0},{3,1},{4,6},{5,7},{6,4},{7,5},{8,10},{9,11},{10,... | collective-permute-start | bytes 1228808 | tf_op jit(solution)/shard_map/ppermute | solution.py:146
  27.1 2.7 %collective-permute-start.11 = (bf16[2,208,128]{2,1,0:T(8,128)(2,1)S(1)}, bf16[2,208,128]{2,1,0:T(8,128)(2,1)S(1)}, u32[]{:S(2)}, u32[]{:S(2)}) collective-permute-start(bf16[2,208,128]{2,1,0:T(8,128)(2,1)S(1)} %pad_maximum_fusion.1), channel_id=1, source_target_pairs={{0,8},{1,9},{2,10},{3,11},{4,12},{5,13},{6,14},{7,15},{8,0},{9,1},... | collective-permute-start | bytes 319496 | tf_op jit(solution)/shard_map/ppermute | solution.py:146
  29.8 1.7 %collective-permute-start.12 = (bf16[2,208,128]{2,1,0:T(8,128)(2,1)S(1)}, bf16[2,208,128]{2,1,0:T(8,128)(2,1)S(1)}, u32[]{:S(2)}, u32[]{:S(2)}) collective-permute-start(bf16[2,208,128]{2,1,0:T(8,128)(2,1)S(1)} %pad_maximum_fusion.1), channel_id=1, source_target_pairs={{0,12},{1,13},{2,14},{3,15},{4,8},{5,9},{6,10},{7,11},{8,4},{9,5},... | collective-permute-start | bytes 319496 | tf_op jit(solution)/shard_map/ppermute | solution.py:146
  31.5 5.4 %collective-permute-done.9 = f32[4,200,128]{2,1,0:T(8,128)S(1)} collective-permute-done((f32[4,200,128]{2,1,0:T(8,128)S(1)}, f32[4,200,128]{2,1,0:T(8,128)S(1)}, u32[]{:S(2)}, u32[]{:S(2)}) %collective-permute-start.9) | collective-permute-done | bytes 409632 | tf_op jit(solution)/shard_map/ppermute | solution.py:146
  37.0 1.5 %collective-permute-done.11 = bf16[2,208,128]{2,1,0:T(8,128)(2,1)S(1)} collective-permute-done((bf16[2,208,128]{2,1,0:T(8,128)(2,1)S(1)}, bf16[2,208,128]{2,1,0:T(8,128)(2,1)S(1)}, u32[]{:S(2)}, u32[]{:S(2)}) %collective-permute-start.11) | collective-permute-done | bytes 106528 | tf_op jit(solution)/shard_map/ppermute | solution.py:146
  39.2 1.8 %collective-permute-start.13 = (f32[200,128]{1,0:T(8,128)S(1)}, f32[200,128]{1,0:T(8,128)S(1)}, u32[]{:S(2)}, u32[]{:S(2)}) collective-permute-start(f32[200,128]{1,0:T(8,128)S(1)} %get-tuple-element.39), channel_id=1, source_target_pairs={{0,4},{1,5},{2,6},{3,7},{4,0},{5,1},{6,2},{7,3},{8,12},{9,13},{10,... | collective-permute-start | bytes 307208 | tf_op jit(solution)/shard_map/ppermute | solution.py:146
  41.0 1.0 %collective-permute-start.14 = (f32[200,128]{1,0:T(8,128)S(1)}, f32[200,128]{1,0:T(8,128)S(1)}, u32[]{:S(2)}, u32[]{:S(2)}) collective-permute-start(f32[200,128]{1,0:T(8,128)S(1)} %get-tuple-element.40), channel_id=1, source_target_pairs={{0,8},{1,9},{2,10},{3,11},{4,12},{5,13},{6,14},{7,15},{8,0},{9,1},... | collective-permute-start | bytes 307208 | tf_op jit(solution)/shard_map/ppermute | solution.py:146
  41.9 1.7 %collective-permute-start.15 = (f32[200,128]{1,0:T(8,128)S(1)}, f32[200,128]{1,0:T(8,128)S(1)}, u32[]{:S(2)}, u32[]{:S(2)}) collective-permute-start(f32[200,128]{1,0:T(8,128)S(1)} %get-tuple-element.41), channel_id=1, source_target_pairs={{0,12},{1,13},{2,14},{3,15},{4,8},{5,9},{6,10},{7,11},{8,4},{9,5},... | collective-permute-start | bytes 307208 | tf_op jit(solution)/shard_map/ppermute | solution.py:146
  43.9 0.7 collective-permute-done.13
  44.6 6.0 %collective-permute-done.14 = f32[200,128]{1,0:T(8,128)S(1)} collective-permute-done((f32[200,128]{1,0:T(8,128)S(1)}, f32[200,128]{1,0:T(8,128)S(1)}, u32[]{:S(2)}, u32[]{:S(2)}) %collective-permute-start.14) | collective-permute-done | bytes 102432 | tf_op jit(solution)/shard_map/ppermute | solution.py:146
  50.7 1.8 %collective-permute-start.18 = (bf16[200,128]{1,0:T(8,128)(2,1)S(1)}, bf16[200,128]{1,0:T(8,128)(2,1)S(1)}, u32[]{:S(2)}, u32[]{:S(2)}) collective-permute-start(bf16[200,128]{1,0:T(8,128)(2,1)S(1)} %add_convert_fusion.refs_0_), channel_id=1, source_target_pairs={{0,4},{1,5},{2,6},{3,7},{4,0},{5,1},{6,2},{7,3},{8,12},{9,13},{10,... | collective-permute-start | bytes 153608 | tf_op jit(solution)/shard_map/ppermute | solution.py:146
  52.4 0.8 %collective-permute-start.20 = (bf16[200,128]{1,0:T(8,128)(2,1)S(1)}, bf16[200,128]{1,0:T(8,128)(2,1)S(1)}, u32[]{:S(2)}, u32[]{:S(2)}) collective-permute-start(bf16[200,128]{1,0:T(8,128)(2,1)S(1)} %add_convert_fusion.refs_0_), channel_id=1, source_target_pairs={{0,8},{1,9},{2,10},{3,11},{4,12},{5,13},{6,14},{7,15},{8,0},{9,1},... | collective-permute-start | bytes 153608 | tf_op jit(solution)/shard_map/ppermute | solution.py:146
  53.2 1.9 %collective-permute-start.22 = (bf16[200,128]{1,0:T(8,128)(2,1)S(1)}, bf16[200,128]{1,0:T(8,128)(2,1)S(1)}, u32[]{:S(2)}, u32[]{:S(2)}) collective-permute-start(bf16[200,128]{1,0:T(8,128)(2,1)S(1)} %add_convert_fusion.refs_0_), channel_id=1, source_target_pairs={{0,12},{1,13},{2,14},{3,15},{4,8},{5,9},{6,10},{7,11},{8,4},{9,5},... | collective-permute-start | bytes 153608 | tf_op jit(solution)/shard_map/ppermute | solution.py:146
  55.5 1.5 %collective-permute-start.17 = (bf16[200,128]{1,0:T(8,128)(2,1)S(1)}, bf16[200,128]{1,0:T(8,128)(2,1)S(1)}, u32[]{:S(2)}, u32[]{:S(2)}) collective-permute-start(bf16[200,128]{1,0:T(8,128)(2,1)S(1)} %add_convert_fusion.refs_0_), channel_id=1, source_target_pairs={{0,2},{1,3},{2,0},{3,1},{4,6},{5,7},{6,4},{7,5},{8,10},{9,11},{10,... | collective-permute-start | bytes 153608 | tf_op jit(solution)/shard_map/ppermute | solution.py:146
  57.6 0.7 collective-permute-done.20.refs_4_
  58.3 1.5 %collective-permute-start.21 = (bf16[200,128]{1,0:T(8,128)(2,1)S(1)}, bf16[200,128]{1,0:T(8,128)(2,1)S(1)}, u32[]{:S(2)}, u32[]{:S(2)}) collective-permute-start(bf16[200,128]{1,0:T(8,128)(2,1)S(1)} %collective-permute-done.20.refs_4_), channel_id=1, source_target_pairs={{0,2},{1,3},{2,0},{3,1},{4,6},{5,7},{6,4},{7,5},{8,10},{9,11},{10,... | collective-permute-start | bytes 153608 | tf_op jit(solution)/shard_map/ppermute | solution.py:146
  59.8 0.9 %collective-permute-start.23 = (bf16[200,128]{1,0:T(8,128)(2,1)S(1)}, bf16[200,128]{1,0:T(8,128)(2,1)S(1)}, u32[]{:S(2)}, u32[]{:S(2)}) collective-permute-start(bf16[200,128]{1,0:T(8,128)(2,1)S(1)} %collective-permute-done.22.refs_6_), channel_id=1, source_target_pairs={{0,2},{1,3},{2,0},{3,1},{4,6},{5,7},{6,4},{7,5},{8,10},{9,11},{10,... | collective-permute-start | bytes 153608 | tf_op jit(solution)/shard_map/ppermute | solution.py:146
  60.9 1.2 %select_noise.1.noise_ref = f32[8,208,128]{2,1,0:T(8,128)S(1)} custom-call(s32[128]{0:T(128)S(1)} %reshape.93.starts_ref, s32[1]{0:T(128)} %bitcast.place_ref, bf16[4,2,208,128]{3,2,1,0:T(8,128)(2,1)S(1)} %pad_maximum_fusion.near_ref, bf16[4,2,208,128]{3,2,1,0:T(8,128)(2,1)S(1)} %collective-permute-done.16.far_ref), custom_call_target="tpu_custom_call" | custom-call | tf_op jit(solution)/shard_map/select_noise/pallas_call | solution.py:326
  62.4 1.5 %collective-permute-done.23.refs_7_ = bf16[200,128]{1,0:T(8,128)(2,1)S(1)} collective-permute-done((bf16[200,128]{1,0:T(8,128)(2,1)S(1)}, bf16[200,128]{1,0:T(8,128)(2,1)S(1)}, u32[]{:S(2)}, u32[]{:S(2)}) %collective-permute-start.23) | collective-permute-done | bytes 51232 | tf_op jit(solution)/shard_map/ppermute | solution.py:146
  63.9 2.0 %gram_and_cross.1.mine_ref = f32[208,512]{1,0:T(8,128)S(1)} custom-call(s32[1]{0:T(128)} %bitcast.place_ref, s32[8,128,1]{2,1,0:T(8,128)S(1)} %broadcast_add_fusion.target_ref, f32[8,208,128]{2,1,0:T(8,128)S(1)} %select_noise.1.noise_ref, bf16[200,128]{1,0:T(8,128)(2,1)S(1)} %add_convert_fusion.refs_0_, ...), custom_call_target="tpu_custom_call" | custom-call | tf_op jit(solution)/shard_map/gram_and_cross/pallas_call | solution.py:395
  66.0 1.8 %collective-permute-done.24.other_ref = f32[208,512]{1,0:T(8,128)S(1)} collective-permute-done((f32[208,512]{1,0:T(8,128)S(1)}, f32[208,512]{1,0:T(8,128)S(1)}, u32[]{:S(2)}, u32[]{:S(2)}) %collective-permute-start.24) | collective-permute-done | bytes 426016 | tf_op jit(solution)/shard_map/ppermute | solution.py:146
  67.7 11.1 %solve_and_update.1 = (bf16[200,12288]{1,0:T(8,128)(2,1)}, f32[200,200]{1,0:T(8,128)}, f32[1,256]{1,0:T(1,128)}) custom-call(f32[208,512]{1,0:T(8,128)S(1)} %gram_and_cross.1.mine_ref, f32[208,512]{1,0:T(8,128)S(1)} %collective-permute-done.24.other_ref, bf16[200,12288]{1,0:T(8,128)(2,1)} %slab_ref.1), custom_call_target="tpu_custom_call" | custom-call | tf_op jit(solution)/shard_map/solve_and_update/pallas_call | solution.py:484
  (50 shorter events, 6.0 us)
Async XLA Ops:
  1.4 5.7 %collective-permute-start.1 = (s32[32]{0:T(128)S(1)}, s32[32]{0:T(128)S(1)}, u32[]{:S(2)}, u32[]{:S(2)}) collective-permute-start(s32[32]{0:T(128)S(1)} %pad_add_fusion.2), channel_id=1, source_target_pairs={{0,1},{1,0},{2,3},{3,2},{4,5},{5,4},{6,7},{7,6},{8,9},{9,8},{10,11... | collective-permute-start | bytes 392 | tf_op jit(solution)/shard_map/ppermute | solution.py:146
  1.8 5.2 %collective-permute-start.2 = (s32[32]{0:T(128)S(1)}, s32[32]{0:T(128)S(1)}, u32[]{:S(2)}, u32[]{:S(2)}) collective-permute-start(s32[32]{0:T(128)S(1)} %pad_add_fusion.2), channel_id=1, source_target_pairs={{0,2},{1,3},{2,0},{3,1},{4,6},{5,7},{6,4},{7,5},{8,10},{9,11},{10,... | collective-permute-start | bytes 392 | tf_op jit(solution)/shard_map/ppermute | solution.py:146
  4.4 3.0 %collective-permute-start.3 = (s32[32]{0:T(128)S(1)}, s32[32]{0:T(128)S(1)}, u32[]{:S(2)}, u32[]{:S(2)}) collective-permute-start(s32[32]{0:T(128)S(1)} %pad_add_fusion.2), channel_id=1, source_target_pairs={{0,3},{1,2},{2,1},{3,0},{4,7},{5,6},{6,5},{7,4},{8,11},{9,10},{10,... | collective-permute-start | bytes 392 | tf_op jit(solution)/shard_map/ppermute | solution.py:146
  5.8 0.9 %copy-start.1 = (bf16[256,200]{0,1:T(8,128)(2,1)S(1)}, bf16[256,200]{0,1:T(8,128)(2,1)}, u32[]{:S(2)}) copy-start(bf16[256,200]{0,1:T(8,128)(2,1)} %param.13) | copy-start | bytes 307204
  6.9 1.3 %collective-permute-start = (bf16[208,128]{1,0:T(8,128)(2,1)S(1)}, bf16[208,128]{1,0:T(8,128)(2,1)S(1)}, u32[]{:S(2)}, u32[]{:S(2)}) collective-permute-start(bf16[208,128]{1,0:T(8,128)(2,1)S(1)} %get-tuple-element.26), channel_id=1, source_target_pairs={{0,1},{1,0},{2,3},{3,2},{4,5},{5,4},{6,7},{7,6},{8,9},{9,8},{10,11... | collective-permute-start | bytes 159752 | tf_op jit(solution)/shard_map/ppermute | solution.py:146
  8.2 9.9 %copy-start = (bf16[512,512]{1,0:T(8,128)(2,1)S(1)}, bf16[512,512]{1,0:T(8,128)(2,1)}, u32[]{:S(2)}) copy-start(bf16[512,512]{1,0:T(8,128)(2,1)} %constant.8.clone.table_w_ref.table_h_ref) | copy-start | bytes 1572868
  8.2 8.1 %collective-permute-start.4 = (s32[4,32]{1,0:T(4,128)S(1)}, s32[4,32]{1,0:T(4,128)S(1)}, u32[]{:S(2)}, u32[]{:S(2)}) collective-permute-start(s32[4,32]{1,0:T(4,128)S(1)} %pad_add_fusion.1.list0_ref), channel_id=1, source_target_pairs={{0,4},{1,5},{2,6},{3,7},{4,0},{5,1},{6,2},{7,3},{8,12},{9,13},{10,... | collective-permute-start | bytes 1544 | tf_op jit(solution)/shard_map/ppermute | solution.py:146
  10.1 6.3 %collective-permute-start.5 = (s32[4,32]{1,0:T(4,128)S(1)}, s32[4,32]{1,0:T(4,128)S(1)}, u32[]{:S(2)}, u32[]{:S(2)}) collective-permute-start(s32[4,32]{1,0:T(4,128)S(1)} %pad_add_fusion.1.list0_ref), channel_id=1, source_target_pairs={{0,8},{1,9},{2,10},{3,11},{4,12},{5,13},{6,14},{7,15},{8,0},{9,1},... | collective-permute-start | bytes 1544 | tf_op jit(solution)/shard_map/ppermute | solution.py:146
  12.7 5.4 %collective-permute-start.6 = (s32[4,32]{1,0:T(4,128)S(1)}, s32[4,32]{1,0:T(4,128)S(1)}, u32[]{:S(2)}, u32[]{:S(2)}) collective-permute-start(s32[4,32]{1,0:T(4,128)S(1)} %pad_add_fusion.1.list0_ref), channel_id=1, source_target_pairs={{0,12},{1,13},{2,14},{3,15},{4,8},{5,9},{6,10},{7,11},{8,4},{9,5},... | collective-permute-start | bytes 1544 | tf_op jit(solution)/shard_map/ppermute | solution.py:146
  23.5 1.8 %collective-permute-start.8 = (f32[4,200,128]{2,1,0:T(8,128)S(1)}, f32[4,200,128]{2,1,0:T(8,128)S(1)}, u32[]{:S(2)}, u32[]{:S(2)}) collective-permute-start(f32[4,200,128]{2,1,0:T(8,128)S(1)} %get-tuple-element.32), channel_id=1, source_target_pairs={{0,1},{1,0},{2,3},{3,2},{4,5},{5,4},{6,7},{7,6},{8,9},{9,8},{10,11... | collective-permute-start | bytes 1228808 | tf_op jit(solution)/shard_map/ppermute | solution.py:146
  23.5 7.9 %collective-permute-start.7 = (f32[4,200,128]{2,1,0:T(8,128)S(1)}, f32[4,200,128]{2,1,0:T(8,128)S(1)}, u32[]{:S(2)}, u32[]{:S(2)}) collective-permute-start(f32[4,200,128]{2,1,0:T(8,128)S(1)} %get-tuple-element.30), channel_id=1, source_target_pairs={{0,1},{1,0},{2,3},{3,2},{4,5},{5,4},{6,7},{7,6},{8,9},{9,8},{10,11... | collective-permute-start | bytes 1228808 | tf_op jit(solution)/shard_map/ppermute | solution.py:146
  25.3 11.6 %collective-permute-start.9 = (f32[4,200,128]{2,1,0:T(8,128)S(1)}, f32[4,200,128]{2,1,0:T(8,128)S(1)}, u32[]{:S(2)}, u32[]{:S(2)}) collective-permute-start(f32[4,200,128]{2,1,0:T(8,128)S(1)} %add.121), channel_id=1, source_target_pairs={{0,2},{1,3},{2,0},{3,1},{4,6},{5,7},{6,4},{7,5},{8,10},{9,11},{10,... | collective-permute-start | bytes 1228808 | tf_op jit(solution)/shard_map/ppermute | solution.py:146
  27.0 10.0 %collective-permute-start.10 = (bf16[2,208,128]{2,1,0:T(8,128)(2,1)S(1)}, bf16[2,208,128]{2,1,0:T(8,128)(2,1)S(1)}, u32[]{:S(2)}, u32[]{:S(2)}) collective-permute-start(bf16[2,208,128]{2,1,0:T(8,128)(2,1)S(1)} %pad_maximum_fusion.1), channel_id=1, source_target_pairs={{0,4},{1,5},{2,6},{3,7},{4,0},{5,1},{6,2},{7,3},{8,12},{9,13},{10,... | collective-permute-start | bytes 319496 | tf_op jit(solution)/shard_map/ppermute | solution.py:146
  27.1 11.4 %collective-permute-start.11 = (bf16[2,208,128]{2,1,0:T(8,128)(2,1)S(1)}, bf16[2,208,128]{2,1,0:T(8,128)(2,1)S(1)}, u32[]{:S(2)}, u32[]{:S(2)}) collective-permute-start(bf16[2,208,128]{2,1,0:T(8,128)(2,1)S(1)} %pad_maximum_fusion.1), channel_id=1, source_target_pairs={{0,8},{1,9},{2,10},{3,11},{4,12},{5,13},{6,14},{7,15},{8,0},{9,1},... | collective-permute-start | bytes 319496 | tf_op jit(solution)/shard_map/ppermute | solution.py:146
  29.8 8.7 %collective-permute-start.12 = (bf16[2,208,128]{2,1,0:T(8,128)(2,1)S(1)}, bf16[2,208,128]{2,1,0:T(8,128)(2,1)S(1)}, u32[]{:S(2)}, u32[]{:S(2)}) collective-permute-start(bf16[2,208,128]{2,1,0:T(8,128)(2,1)S(1)} %pad_maximum_fusion.1), channel_id=1, source_target_pairs={{0,12},{1,13},{2,14},{3,15},{4,8},{5,9},{6,10},{7,11},{8,4},{9,5},... | collective-permute-start | bytes 319496 | tf_op jit(solution)/shard_map/ppermute | solution.py:146
  38.5 12.1 %collective-permute-start.16 = (bf16[4,2,208,128]{3,2,1,0:T(8,128)(2,1)S(1)}, bf16[4,2,208,128]{3,2,1,0:T(8,128)(2,1)S(1)}, u32[]{:S(2)}, u32[]{:S(2)}) collective-permute-start(bf16[4,2,208,128]{3,2,1,0:T(8,128)(2,1)S(1)} %pad_maximum_fusion.near_ref), channel_id=1, source_target_pairs={{0,2},{1,3},{2,0},{3,1},{4,6},{5,7},{6,4},{7,5},{8,10},{9,11},{10,... | collective-permute-start | bytes 1277960 | tf_op jit(solution)/shard_map/ppermute | solution.py:146
  39.2 5.4 %collective-permute-start.13 = (f32[200,128]{1,0:T(8,128)S(1)}, f32[200,128]{1,0:T(8,128)S(1)}, u32[]{:S(2)}, u32[]{:S(2)}) collective-permute-start(f32[200,128]{1,0:T(8,128)S(1)} %get-tuple-element.39), channel_id=1, source_target_pairs={{0,4},{1,5},{2,6},{3,7},{4,0},{5,1},{6,2},{7,3},{8,12},{9,13},{10,... | collective-permute-start | bytes 307208 | tf_op jit(solution)/shard_map/ppermute | solution.py:146
  41.0 9.6 %collective-permute-start.14 = (f32[200,128]{1,0:T(8,128)S(1)}, f32[200,128]{1,0:T(8,128)S(1)}, u32[]{:S(2)}, u32[]{:S(2)}) collective-permute-start(f32[200,128]{1,0:T(8,128)S(1)} %get-tuple-element.40), channel_id=1, source_target_pairs={{0,8},{1,9},{2,10},{3,11},{4,12},{5,13},{6,14},{7,15},{8,0},{9,1},... | collective-permute-start | bytes 307208 | tf_op jit(solution)/shard_map/ppermute | solution.py:146
  41.9 8.7 %collective-permute-start.15 = (f32[200,128]{1,0:T(8,128)S(1)}, f32[200,128]{1,0:T(8,128)S(1)}, u32[]{:S(2)}, u32[]{:S(2)}) collective-permute-start(f32[200,128]{1,0:T(8,128)S(1)} %get-tuple-element.41), channel_id=1, source_target_pairs={{0,12},{1,13},{2,14},{3,15},{4,8},{5,9},{6,10},{7,11},{8,4},{9,5},... | collective-permute-start | bytes 307208 | tf_op jit(solution)/shard_map/ppermute | solution.py:146
  50.7 6.4 %collective-permute-start.18 = (bf16[200,128]{1,0:T(8,128)(2,1)S(1)}, bf16[200,128]{1,0:T(8,128)(2,1)S(1)}, u32[]{:S(2)}, u32[]{:S(2)}) collective-permute-start(bf16[200,128]{1,0:T(8,128)(2,1)S(1)} %add_convert_fusion.refs_0_), channel_id=1, source_target_pairs={{0,4},{1,5},{2,6},{3,7},{4,0},{5,1},{6,2},{7,3},{8,12},{9,13},{10,... | collective-permute-start | bytes 153608 | tf_op jit(solution)/shard_map/ppermute | solution.py:146
  52.4 5.9 %collective-permute-start.20 = (bf16[200,128]{1,0:T(8,128)(2,1)S(1)}, bf16[200,128]{1,0:T(8,128)(2,1)S(1)}, u32[]{:S(2)}, u32[]{:S(2)}) collective-permute-start(bf16[200,128]{1,0:T(8,128)(2,1)S(1)} %add_convert_fusion.refs_0_), channel_id=1, source_target_pairs={{0,8},{1,9},{2,10},{3,11},{4,12},{5,13},{6,14},{7,15},{8,0},{9,1},... | collective-permute-start | bytes 153608 | tf_op jit(solution)/shard_map/ppermute | solution.py:146
  53.2 6.6 %collective-permute-start.22 = (bf16[200,128]{1,0:T(8,128)(2,1)S(1)}, bf16[200,128]{1,0:T(8,128)(2,1)S(1)}, u32[]{:S(2)}, u32[]{:S(2)}) collective-permute-start(bf16[200,128]{1,0:T(8,128)(2,1)S(1)} %add_convert_fusion.refs_0_), channel_id=1, source_target_pairs={{0,12},{1,13},{2,14},{3,15},{4,8},{5,9},{6,10},{7,11},{8,4},{9,5},... | collective-permute-start | bytes 153608 | tf_op jit(solution)/shard_map/ppermute | solution.py:146
  55.5 6.7 %collective-permute-start.17 = (bf16[200,128]{1,0:T(8,128)(2,1)S(1)}, bf16[200,128]{1,0:T(8,128)(2,1)S(1)}, u32[]{:S(2)}, u32[]{:S(2)}) collective-permute-start(bf16[200,128]{1,0:T(8,128)(2,1)S(1)} %add_convert_fusion.refs_0_), channel_id=1, source_target_pairs={{0,2},{1,3},{2,0},{3,1},{4,6},{5,7},{6,4},{7,5},{8,10},{9,11},{10,... | collective-permute-start | bytes 153608 | tf_op jit(solution)/shard_map/ppermute | solution.py:146
  57.0 5.2 %collective-permute-start.19 = (bf16[200,128]{1,0:T(8,128)(2,1)S(1)}, bf16[200,128]{1,0:T(8,128)(2,1)S(1)}, u32[]{:S(2)}, u32[]{:S(2)}) collective-permute-start(bf16[200,128]{1,0:T(8,128)(2,1)S(1)} %collective-permute-done.18.refs_2_), channel_id=1, source_target_pairs={{0,2},{1,3},{2,0},{3,1},{4,6},{5,7},{6,4},{7,5},{8,10},{9,11},{10,... | collective-permute-start | bytes 153608 | tf_op jit(solution)/shard_map/ppermute | solution.py:146
  58.3 4.1 %collective-permute-start.21 = (bf16[200,128]{1,0:T(8,128)(2,1)S(1)}, bf16[200,128]{1,0:T(8,128)(2,1)S(1)}, u32[]{:S(2)}, u32[]{:S(2)}) collective-permute-start(bf16[200,128]{1,0:T(8,128)(2,1)S(1)} %collective-permute-done.20.refs_4_), channel_id=1, source_target_pairs={{0,2},{1,3},{2,0},{3,1},{4,6},{5,7},{6,4},{7,5},{8,10},{9,11},{10,... | collective-permute-start | bytes 153608 | tf_op jit(solution)/shard_map/ppermute | solution.py:146
  59.8 4.1 %collective-permute-start.23 = (bf16[200,128]{1,0:T(8,128)(2,1)S(1)}, bf16[200,128]{1,0:T(8,128)(2,1)S(1)}, u32[]{:S(2)}, u32[]{:S(2)}) collective-permute-start(bf16[200,128]{1,0:T(8,128)(2,1)S(1)} %collective-permute-done.22.refs_6_), channel_id=1, source_target_pairs={{0,2},{1,3},{2,0},{3,1},{4,6},{5,7},{6,4},{7,5},{8,10},{9,11},{10,... | collective-permute-start | bytes 153608 | tf_op jit(solution)/shard_map/ppermute | solution.py:146
  65.9 1.8 %collective-permute-start.24 = (f32[208,512]{1,0:T(8,128)S(1)}, f32[208,512]{1,0:T(8,128)S(1)}, u32[]{:S(2)}, u32[]{:S(2)}) collective-permute-start(f32[208,512]{1,0:T(8,128)S(1)} %gram_and_cross.1.mine_ref), channel_id=1, source_target_pairs={{0,1},{1,0},{2,3},{3,2},{4,5},{5,4},{6,7},{7,6},{8,9},{9,8},{10,11... | collective-permute-start | bytes 1277960 | tf_op jit(solution)/shard_map/ppermute | solution.py:146

commit v4 on v3

--- a/solution.py
+++ b/solution.py
@@ -187,7 +187,7 @@
 
 def shares_kernel(
     list0_ref, list1_ref, list2_ref, list3_ref, place_ref, maps_ref, table_w_ref, table_h_ref, k0_ref, k1_ref, s0_ref, s1_ref,
-    full_ref, pick_ref, row_ref, spread_ref, wide_ref,
+    full_ref, pick_ref, row_ref, spread_ref,
 ):
     rows, members, width = maps_ref.shape
     devices, depth, _ = row_ref.shape
@@ -223,15 +223,14 @@
     for out_ref, low in ((s1_ref, 3), (k1_ref, 2), (s0_ref, 1), (k0_ref, 0)):
         for high in range(out_ref.shape[0]):
             delta = high * 4 + low
+            wide = []
             for p in range(keep):
                 start = pl.multiple_of(block(delta, p) % per_column * BLK, BLK)
-                cosines = spread_ref[pl.ds(start, BLK), :]
-                wide_ref[p * BLK : (p + 1) * BLK, :] = jnp.where(position == p, cosines, 0.0)
-            share = jnp.dot(
-                wide_ref[...].astype(jnp.bfloat16), row_ref[delta],
-                preferred_element_type=jnp.float32,
-            )
-            out_ref[high] = share.T
+                wide.append(jnp.where(position == p, spread_ref[pl.ds(start, BLK), :], 0.0))
+            wide = jnp.concatenate(wide, axis=0).astype(jnp.bfloat16)
+            out_ref[high] = jnp.dot(
+                wide, row_ref[delta], preferred_element_type=jnp.float32
+            ).T
 
 
 def shares(lists, place, maps, table_w, table_h):
@@ -250,7 +249,6 @@
             pltpu.VMEM((devices * keep, width), jnp.float32),
             pltpu.VMEM((devices, depth, members), jnp.bfloat16),
             pltpu.VMEM((table_h.shape[0], depth), jnp.float32),
-            pltpu.VMEM((keep * BLK, depth), jnp.float32),
         ],
         compiler_params=pltpu.CompilerParams(vmem_limit_bytes=VMEM_LIMIT),
         cost_estimate=pl.CostEstimate(
@@ -262,7 +260,7 @@
     )(*lists, place, maps, table_w, table_h)
 
 
-def split_noise_kernel(place_ref, noise_ref, observed_ref, scale_ref, keep_ref, send_ref):
+def split_noise_kernel(place_ref, noise_ref, data_ref, keep_ref, send_ref):
     members, slots = noise_ref.shape
     half = slots // 2
     core = place_ref[0] & 1
@@ -276,8 +274,7 @@
     value = jnp.concatenate(
         [
             noise_ref[...].astype(jnp.float32),
-            observed_ref[...].astype(jnp.float32),
-            scale_ref[...].astype(jnp.float32),
+            data_ref[...].astype(jnp.float32),
             extra,
         ],
         axis=0,
@@ -287,18 +284,18 @@
     send_ref[...] = moved[:, half:slots]
 
 
-def split_noise(place, noise, observed, scale):
+def split_noise(place, noise, data):
     members, slots = noise.shape
     rows = -(-(members + 2) // 16) * 16
     out = jax.ShapeDtypeStruct((rows, slots // 2), jnp.bfloat16)
     return pl.pallas_call(
         split_noise_kernel,
-        in_specs=[SMEM] + [VMEM] * 3,
+        in_specs=[SMEM] + [VMEM] * 2,
         out_specs=[VMEM] * 2,
         out_shape=[out] * 2,
         compiler_params=pltpu.CompilerParams(vmem_limit_bytes=VMEM_LIMIT),
         name="split_noise",
-    )(place, noise, observed, scale)
+    )(place, noise, data)
 
 
 def select_noise_kernel(starts_ref, place_ref, near_ref, far_ref, out_ref, wide_ref, rows_ref):
@@ -413,19 +410,15 @@
     state_ref, held_ref, arrived, left,
 ):
     members, cells = held_ref.shape
-    tiles = arrived.shape[0]
+    tiles = left.shape[0]
     tile = cells // tiles
     parts = [pl.ds(i * tile, tile) for i in range(tiles)]
-    reads = [
-        pltpu.make_async_copy(slab_ref.at[:, part], held_ref.at[:, part], arrived.at[i])
-        for i, part in enumerate(parts)
-    ]
     writes = [
         pltpu.make_async_copy(held_ref.at[:, part], out_ref.at[:, part], left.at[i])
         for i, part in enumerate(parts)
     ]
-    for read in reads:
-        read.start()
+    read = pltpu.make_async_copy(slab_ref, held_ref, arrived)
+    read.start()
 
     total = mine_ref[0:members, :] + other_ref[0:members, :]
     misfit_ref[...] = (
@@ -463,14 +456,15 @@
     spread = ((full - center) * (1.0 / math.sqrt(members - 1))).T[0:members, 0:members]
     high = spread.astype(jnp.bfloat16)
     rest = spread - high.astype(jnp.float32)
-    middle = rest.astype(jnp.bfloat16)
-    low = (rest - middle.astype(jnp.float32)).astype(jnp.bfloat16)
+    low = rest.astype(jnp.bfloat16).astype(jnp.float32)
+    over = jnp.sum(rest - low, axis=1, keepdims=True)
+    lane = lax.broadcasted_iota(jnp.int32, (members, members), 1)
+    low = (low + jnp.where(lane == 0, over, 0.0)).astype(jnp.bfloat16)
+    read.wait()
     for i in range(tiles):
-        reads[i].wait()
         for j in range(i * tile, (i + 1) * tile, 256):
             state = held_ref[:, j : j + 256]
             moved = jnp.dot(low, state, preferred_element_type=jnp.float32)
-            moved = moved + jnp.dot(middle, state, preferred_element_type=jnp.float32)
             moved = moved + jnp.dot(high, state, preferred_element_type=jnp.float32)
             held_ref[:, j : j + 256] = (state.astype(jnp.float32) + moved).astype(jnp.bfloat16)
         writes[i].start()
@@ -493,7 +487,7 @@
         scratch_shapes=[
             pltpu.VMEM((256, 512), jnp.float32),
             pltpu.VMEM(slab.shape, slab.dtype),
-            pltpu.SemaphoreType.DMA((tiles,)),
+            pltpu.SemaphoreType.DMA,
             pltpu.SemaphoreType.DMA((tiles,)),
         ],
         compiler_params=pltpu.CompilerParams(vmem_limit_bytes=SLAB_LIMIT),
@@ -516,24 +510,27 @@
     lists = jnp.stack([lists] + [swap(lists, delta) for delta in range(1, 4)])
 
     noise_keep, noise_send = split_noise(
-        me.reshape(1), perturbation.T, observed[None, :], error_scale[None, :]
+        me.reshape(1), perturbation.T, jnp.stack([observed, error_scale])
     )
     noise = jnp.stack([noise_keep, swap(noise_send, 1)])
     amplitude_maps, noise, lists = lax.optimization_barrier((amplitude_maps, noise, lists))
     lists = [lists] + [swap(lists, 4 * i) for i in range(1, devices // 4)]
-    noises = [noise] + [swap(noise, 4 * i) for i in range(1, devices // 4)]
+    near_z = swap(noise, 4)
 
     maps = by_row(amplitude_maps)
     table_w = jnp.asarray(dct_constant(map_width))
     table_h = table_w if map_height == map_width else jnp.asarray(dct_constant(map_height))
+    lists, near_z = lax.optimization_barrier((lists, near_z))
     keep_0, keep_1, send_0, send_1 = shares(lists, me.reshape(1), maps, table_w, table_h)
 
     share_1 = keep_1 + swap(send_1, 1)
     got_1 = swap(share_1, 2)
     share_0 = keep_0 + swap(send_0, 1)
     share = [share_0[i] + got_1[i] for i in range(devices // 4)]
-    share, noises = lax.optimization_barrier((share, noises))
-    near_noise = jnp.stack(noises)
+    noise = jnp.stack([noise, near_z])
+    far_z = swap(noise, 8)
+    share, far_z = lax.optimization_barrier((share, far_z))
+    near_noise = jnp.concatenate([noise, far_z])
     far_noise = swap(near_noise, 2)
     got = [swap(share[i], 4 * i) for i in range(1, devices // 4)]
     predicted = (share[0] + got[0] + got[1] + got[2]).astype(jnp.bfloat16)

time: 79.1 us -> 76.7 us (0.970)
  Pallas kernels: 23.5 us -> 20.3 us
  waiting for transfers between devices: 21.9 us -> 23.4 us
  starting transfers between devices: 28.3 us -> 27.5 us
    pallas_call x1, Pallas kernels: 11.1 us -> 7.91 us  [update(): pl.pallas_call(update_kernel, in_specs=[VMEM, VMEM, HBM], out_specs=[HBM,...]
    ppermute x25 -> x24, waiting for transfers between devices: 21.9 us -> 23.4 us  [swap(): return lax.ppermute(value, 'map', pairs)]
    broadcast_in_dim x2 -> x0, local copies, waits for them, and re-layouts: 1.32 us -> none  [the longest x1 0.66 us: sparse_body(): observed[None, :]]
    another operation x0 -> x2, local copies, waits for them, and re-layouts: none -> 1.32 us  [sparse_body(): jnp.stack([observed, error_scale])]
    ppermute x25 -> x24, starting transfers between devices: 28.3 us -> 27.5 us  [swap(): return lax.ppermute(value, 'map', pairs)]
  transfers between devices with their start and end apart: 25 -> 24, of which waited for: 12 -> 12; matrix products, arithmetic and copies ran while one was open for 3% -> 3% of each run, Pallas kernels for 6% -> 7%
where the time goes in v4:
time: 76.7 us; the launch traced here: 76.5 us
  starting transfers between devices  27.5 us (36%)
  waiting for transfers between devices  23.4 us (31%)
  Pallas kernels  20.3 us (26%)
  local copies, waits for them, and re-layouts  2.73 us (4%)
  other arithmetic  1.53 us (2%)
  between operations  0.99 us (1%)
    ppermute x24, starting transfers between devices, swap(): return lax.ppermute(value, 'map', pairs)  27.5 us
    ppermute x24, waiting for transfers between devices, swap(): return lax.ppermute(value, 'map', pairs)  23.4 us
    pallas_call x1, Pallas kernels, update(): pl.pallas_call(update_kernel, in_specs=[VMEM, VMEM, HBM], out_specs=[HBM,...  7.91 us
    pallas_call x1, Pallas kernels, shares(): pl.pallas_call(shares_kernel, in_specs=[SMEM] * 5 + [VMEM] * 3, out_specs...  5.4 us
    pallas_call x1, Pallas kernels, by_row(): pl.pallas_call(by_row_kernel, in_specs=[HBM], out_specs=VMEM, out_shape=j...  3.65 us
    pallas_call x1, Pallas kernels, gram(): pl.pallas_call(gram_kernel, in_specs=[SMEM] + [VMEM] * (2 + len(predicted...  1.9 us
  transfers between devices with their start and end apart: 24, of which 12 were waited for; matrix products, arithmetic and copies ran while one was open for 3% of the time, Pallas kernels for 7%

profile of v4, /device:TPU:0, one launch (start us, length us, event | category | flops | bytes accessed | tf_op | source)
XLA Modules:
  0.0 76.5 jit_solution(7786197312890831665)
XLA Ops:
  0.6 0.7 pad_add_fusion.2
  1.8 2.5 %collective-permute-start.2 = (s32[32]{0:T(128)S(1)}, s32[32]{0:T(128)S(1)}, u32[]{:S(2)}, u32[]{:S(2)}) collective-permute-start(s32[32]{0:T(128)S(1)} %pad_add_fusion.2), channel_id=1, source_target_pairs={{0,2},{1,3},{2,0},{3,1},{4,6},{5,7},{6,4},{7,5},{8,10},{9,11},{10,... | collective-permute-start | bytes 392 | tf_op jit(solution)/shard_map/ppermute | solution.py:146
  4.5 0.7 stack.42
  5.1 0.7 stack.43
  5.8 0.9 %copy-done.1 = bf16[256,200]{0,1:T(8,128)(2,1)S(1)} copy-done((bf16[256,200]{0,1:T(8,128)(2,1)S(1)}, bf16[256,200]{0,1:T(8,128)(2,1)}, u32[]{:S(2)}) %copy-start.1) | copy-done | bytes 102424
  7.4 0.8 %collective-permute-done = bf16[208,128]{1,0:T(8,128)(2,1)S(1)} collective-permute-done((bf16[208,128]{1,0:T(8,128)(2,1)S(1)}, bf16[208,128]{1,0:T(8,128)(2,1)S(1)}, u32[]{:S(2)}, u32[]{:S(2)}) %collective-permute-start) | collective-permute-done | bytes 53280 | tf_op jit(solution)/shard_map/ppermute | solution.py:146
  8.2 1.9 %collective-permute-start.7 = (bf16[2,208,128]{2,1,0:T(8,128)(2,1)S(1)}, bf16[2,208,128]{2,1,0:T(8,128)(2,1)S(1)}, u32[]{:S(2)}, u32[]{:S(2)}) collective-permute-start(bf16[2,208,128]{2,1,0:T(8,128)(2,1)S(1)} %pad_maximum_fusion.2), channel_id=1, source_target_pairs={{0,4},{1,5},{2,6},{3,7},{4,0},{5,1},{6,2},{7,3},{8,12},{9,13},{10,... | collective-permute-start | bytes 319496 | tf_op jit(solution)/shard_map/ppermute | solution.py:146
  10.3 2.8 %collective-permute-start.5 = (s32[4,32]{1,0:T(4,128)S(1)}, s32[4,32]{1,0:T(4,128)S(1)}, u32[]{:S(2)}, u32[]{:S(2)}) collective-permute-start(s32[4,32]{1,0:T(4,128)S(1)} %pad_add_fusion.1.list0_ref), channel_id=1, source_target_pairs={{0,8},{1,9},{2,10},{3,11},{4,12},{5,13},{6,14},{7,15},{8,0},{9,1},... | collective-permute-start | bytes 1544 | tf_op jit(solution)/shard_map/ppermute | solution.py:146
  13.1 1.4 %collective-permute-start.6 = (s32[4,32]{1,0:T(4,128)S(1)}, s32[4,32]{1,0:T(4,128)S(1)}, u32[]{:S(2)}, u32[]{:S(2)}) collective-permute-start(s32[4,32]{1,0:T(4,128)S(1)} %pad_add_fusion.1.list0_ref), channel_id=1, source_target_pairs={{0,12},{1,13},{2,14},{3,15},{4,8},{5,9},{6,10},{7,11},{8,4},{9,5},... | collective-permute-start | bytes 1544 | tf_op jit(solution)/shard_map/ppermute | solution.py:146
  14.5 3.7 %maps_by_row.1.maps_ref = bf16[32,200,512]{2,1,0:T(8,128)(2,1)S(1)} custom-call(bf16[200,32,512]{2,1,0:T(8,128)(2,1)} %maps_ref), custom_call_target="tpu_custom_call" | custom-call | bytes 13107200 | tf_op jit(solution)/shard_map/maps_by_row/pallas_call | solution.py:171
  18.5 5.4 %coefficient_shares.1 = (f32[4,200,128]{2,1,0:T(8,128)S(1)}, f32[4,200,128]{2,1,0:T(8,128)S(1)}, f32[4,200,128]{2,1,0:T(8,128)S(1)}, f32[4,200,128]{2,1,0:T(8,128)S(1)}) custom-call(s32[4,32]{1,0:T(4,128)S(1)} %pad_add_fusion.1.list0_ref, s32[4,32]{1,0:T(4,128)S(1)} %collective-permute-done.4.list1_ref, s32[4,32]{1,0:T(4,128)S(1)} %collective-permute-done.5.list2_ref, ...), custom_call_target="tpu_custom_call" | custom-call | flops 1677721600 | bytes 6553600 | tf_op jit(solution)/shard_map/coefficient_shares/pallas_call | solution.py:242
  24.5 1.2 %collective-permute-done.9 = f32[4,200,128]{2,1,0:T(8,128)S(1)} collective-permute-done((f32[4,200,128]{2,1,0:T(8,128)S(1)}, f32[4,200,128]{2,1,0:T(8,128)S(1)}, u32[]{:S(2)}, u32[]{:S(2)}) %collective-permute-start.9) | collective-permute-done | bytes 409632 | tf_op jit(solution)/shard_map/ppermute | solution.py:146
  25.8 1.6 %collective-permute-start.10 = (f32[4,200,128]{2,1,0:T(8,128)S(1)}, f32[4,200,128]{2,1,0:T(8,128)S(1)}, u32[]{:S(2)}, u32[]{:S(2)}) collective-permute-start(f32[4,200,128]{2,1,0:T(8,128)S(1)} %add.121), channel_id=1, source_target_pairs={{0,2},{1,3},{2,0},{3,1},{4,6},{5,7},{6,4},{7,5},{8,10},{9,11},{10,... | collective-permute-start | bytes 1228808 | tf_op jit(solution)/shard_map/ppermute | solution.py:146
  27.5 1.4 %collective-permute-start.11 = (bf16[2,2,208,128]{3,2,1,0:T(8,128)(2,1)S(1)}, bf16[2,2,208,128]{3,2,1,0:T(8,128)(2,1)S(1)}, u32[]{:S(2)}, u32[]{:S(2)}) collective-permute-start(bf16[2,2,208,128]{3,2,1,0:T(8,128)(2,1)S(1)} %pad_maximum_fusion.1), channel_id=1, source_target_pairs={{0,8},{1,9},{2,10},{3,11},{4,12},{5,13},{6,14},{7,15},{8,0},{9,1},... | collective-permute-start | bytes 638984 | tf_op jit(solution)/shard_map/ppermute | solution.py:146
  29.0 8.4 %collective-permute-done.10 = f32[4,200,128]{2,1,0:T(8,128)S(1)} collective-permute-done((f32[4,200,128]{2,1,0:T(8,128)S(1)}, f32[4,200,128]{2,1,0:T(8,128)S(1)}, u32[]{:S(2)}, u32[]{:S(2)}) %collective-permute-start.10) | collective-permute-done | bytes 409632 | tf_op jit(solution)/shard_map/ppermute | solution.py:146
  37.4 2.1 %collective-permute-done.11 = bf16[2,2,208,128]{3,2,1,0:T(8,128)(2,1)S(1)} collective-permute-done((bf16[2,2,208,128]{3,2,1,0:T(8,128)(2,1)S(1)}, bf16[2,2,208,128]{3,2,1,0:T(8,128)(2,1)S(1)}, u32[]{:S(2)}, u32[]{:S(2)}) %collective-permute-start.11) | collective-permute-done | bytes 213024 | tf_op jit(solution)/shard_map/ppermute | solution.py:146
  40.3 3.2 %collective-permute-start.13 = (f32[200,128]{1,0:T(8,128)S(1)}, f32[200,128]{1,0:T(8,128)S(1)}, u32[]{:S(2)}, u32[]{:S(2)}) collective-permute-start(f32[200,128]{1,0:T(8,128)S(1)} %get-tuple-element.44), channel_id=1, source_target_pairs={{0,8},{1,9},{2,10},{3,11},{4,12},{5,13},{6,14},{7,15},{8,0},{9,1},... | collective-permute-start | bytes 307208 | tf_op jit(solution)/shard_map/ppermute | solution.py:146
  43.5 1.2 %collective-permute-start.14 = (f32[200,128]{1,0:T(8,128)S(1)}, f32[200,128]{1,0:T(8,128)S(1)}, u32[]{:S(2)}, u32[]{:S(2)}) collective-permute-start(f32[200,128]{1,0:T(8,128)S(1)} %get-tuple-element.45), channel_id=1, source_target_pairs={{0,12},{1,13},{2,14},{3,15},{4,8},{5,9},{6,10},{7,11},{8,4},{9,5},... | collective-permute-start | bytes 307208 | tf_op jit(solution)/shard_map/ppermute | solution.py:146
  45.0 1.2 %collective-permute-done.12 = f32[200,128]{1,0:T(8,128)S(1)} collective-permute-done((f32[200,128]{1,0:T(8,128)S(1)}, f32[200,128]{1,0:T(8,128)S(1)}, u32[]{:S(2)}, u32[]{:S(2)}) %collective-permute-start.12) | collective-permute-done | bytes 102432 | tf_op jit(solution)/shard_map/ppermute | solution.py:146
  46.2 5.2 %collective-permute-done.13 = f32[200,128]{1,0:T(8,128)S(1)} collective-permute-done((f32[200,128]{1,0:T(8,128)S(1)}, f32[200,128]{1,0:T(8,128)S(1)}, u32[]{:S(2)}, u32[]{:S(2)}) %collective-permute-start.13) | collective-permute-done | bytes 102432 | tf_op jit(solution)/shard_map/ppermute | solution.py:146
  51.5 1.7 %collective-permute-start.17 = (bf16[200,128]{1,0:T(8,128)(2,1)S(1)}, bf16[200,128]{1,0:T(8,128)(2,1)S(1)}, u32[]{:S(2)}, u32[]{:S(2)}) collective-permute-start(bf16[200,128]{1,0:T(8,128)(2,1)S(1)} %add_convert_fusion.refs_0_), channel_id=1, source_target_pairs={{0,4},{1,5},{2,6},{3,7},{4,0},{5,1},{6,2},{7,3},{8,12},{9,13},{10,... | collective-permute-start | bytes 153608 | tf_op jit(solution)/shard_map/ppermute | solution.py:146
  53.2 1.3 %collective-permute-start.19 = (bf16[200,128]{1,0:T(8,128)(2,1)S(1)}, bf16[200,128]{1,0:T(8,128)(2,1)S(1)}, u32[]{:S(2)}, u32[]{:S(2)}) collective-permute-start(bf16[200,128]{1,0:T(8,128)(2,1)S(1)} %add_convert_fusion.refs_0_), channel_id=1, source_target_pairs={{0,8},{1,9},{2,10},{3,11},{4,12},{5,13},{6,14},{7,15},{8,0},{9,1},... | collective-permute-start | bytes 153608 | tf_op jit(solution)/shard_map/ppermute | solution.py:146
  54.5 1.4 %collective-permute-start.21 = (bf16[200,128]{1,0:T(8,128)(2,1)S(1)}, bf16[200,128]{1,0:T(8,128)(2,1)S(1)}, u32[]{:S(2)}, u32[]{:S(2)}) collective-permute-start(bf16[200,128]{1,0:T(8,128)(2,1)S(1)} %add_convert_fusion.refs_0_), channel_id=1, source_target_pairs={{0,12},{1,13},{2,14},{3,15},{4,8},{5,9},{6,10},{7,11},{8,4},{9,5},... | collective-permute-start | bytes 153608 | tf_op jit(solution)/shard_map/ppermute | solution.py:146
  56.3 1.6 %collective-permute-start.16 = (bf16[200,128]{1,0:T(8,128)(2,1)S(1)}, bf16[200,128]{1,0:T(8,128)(2,1)S(1)}, u32[]{:S(2)}, u32[]{:S(2)}) collective-permute-start(bf16[200,128]{1,0:T(8,128)(2,1)S(1)} %add_convert_fusion.refs_0_), channel_id=1, source_target_pairs={{0,2},{1,3},{2,0},{3,1},{4,6},{5,7},{6,4},{7,5},{8,10},{9,11},{10,... | collective-permute-start | bytes 153608 | tf_op jit(solution)/shard_map/ppermute | solution.py:146
  58.4 0.8 %collective-permute-done.19.refs_4_ = bf16[200,128]{1,0:T(8,128)(2,1)S(1)} collective-permute-done((bf16[200,128]{1,0:T(8,128)(2,1)S(1)}, bf16[200,128]{1,0:T(8,128)(2,1)S(1)}, u32[]{:S(2)}, u32[]{:S(2)}) %collective-permute-start.19) | collective-permute-done | bytes 51232 | tf_op jit(solution)/shard_map/ppermute | solution.py:146
  59.1 1.2 %collective-permute-start.20 = (bf16[200,128]{1,0:T(8,128)(2,1)S(1)}, bf16[200,128]{1,0:T(8,128)(2,1)S(1)}, u32[]{:S(2)}, u32[]{:S(2)}) collective-permute-start(bf16[200,128]{1,0:T(8,128)(2,1)S(1)} %collective-permute-done.19.refs_4_), channel_id=1, source_target_pairs={{0,2},{1,3},{2,0},{3,1},{4,6},{5,7},{6,4},{7,5},{8,10},{9,11},{10,... | collective-permute-start | bytes 153608 | tf_op jit(solution)/shard_map/ppermute | solution.py:146
  60.4 1.5 %collective-permute-start.22 = (bf16[200,128]{1,0:T(8,128)(2,1)S(1)}, bf16[200,128]{1,0:T(8,128)(2,1)S(1)}, u32[]{:S(2)}, u32[]{:S(2)}) collective-permute-start(bf16[200,128]{1,0:T(8,128)(2,1)S(1)} %collective-permute-done.21.refs_6_), channel_id=1, source_target_pairs={{0,2},{1,3},{2,0},{3,1},{4,6},{5,7},{6,4},{7,5},{8,10},{9,11},{10,... | collective-permute-start | bytes 153608 | tf_op jit(solution)/shard_map/ppermute | solution.py:146
  62.1 1.2 %select_noise.1.noise_ref = f32[8,208,128]{2,1,0:T(8,128)S(1)} custom-call(s32[128]{0:T(128)S(1)} %reshape.93.starts_ref, s32[1]{0:T(128)} %bitcast.place_ref, bf16[4,2,208,128]{3,2,1,0:T(8,128)(2,1)S(1)} %pad_maximum_fusion.near_ref, bf16[4,2,208,128]{3,2,1,0:T(8,128)(2,1)S(1)} %collective-permute-done.15.far_ref), custom_call_target="tpu_custom_call" | custom-call | tf_op jit(solution)/shard_map/select_noise/pallas_call | solution.py:323
  63.4 1.1 %collective-permute-done.22.refs_7_ = bf16[200,128]{1,0:T(8,128)(2,1)S(1)} collective-permute-done((bf16[200,128]{1,0:T(8,128)(2,1)S(1)}, bf16[200,128]{1,0:T(8,128)(2,1)S(1)}, u32[]{:S(2)}, u32[]{:S(2)}) %collective-permute-start.22) | collective-permute-done | bytes 51232 | tf_op jit(solution)/shard_map/ppermute | solution.py:146
  64.6 1.9 %gram_and_cross.1.mine_ref = f32[208,512]{1,0:T(8,128)S(1)} custom-call(s32[1]{0:T(128)} %bitcast.place_ref, s32[8,128,1]{2,1,0:T(8,128)S(1)} %broadcast_add_fusion.target_ref, f32[8,208,128]{2,1,0:T(8,128)S(1)} %select_noise.1.noise_ref, bf16[200,128]{1,0:T(8,128)(2,1)S(1)} %add_convert_fusion.refs_0_, ...), custom_call_target="tpu_custom_call" | custom-call | tf_op jit(solution)/shard_map/gram_and_cross/pallas_call | solution.py:392
  66.7 1.8 %collective-permute-done.23.other_ref = f32[208,512]{1,0:T(8,128)S(1)} collective-permute-done((f32[208,512]{1,0:T(8,128)S(1)}, f32[208,512]{1,0:T(8,128)S(1)}, u32[]{:S(2)}, u32[]{:S(2)}) %collective-permute-start.23) | collective-permute-done | bytes 426016 | tf_op jit(solution)/shard_map/ppermute | solution.py:146
  68.5 7.9 %solve_and_update.1 = (bf16[200,12288]{1,0:T(8,128)(2,1)}, f32[200,200]{1,0:T(8,128)}, f32[1,256]{1,0:T(1,128)}) custom-call(f32[208,512]{1,0:T(8,128)S(1)} %gram_and_cross.1.mine_ref, f32[208,512]{1,0:T(8,128)S(1)} %collective-permute-done.23.other_ref, bf16[200,12288]{1,0:T(8,128)(2,1)} %slab_ref.1), custom_call_target="tpu_custom_call" | custom-call | tf_op jit(solution)/shard_map/solve_and_update/pallas_call | solution.py:478
  (50 shorter events, 5.1 us)
Async XLA Ops:
  1.4 5.7 %collective-permute-start.1 = (s32[32]{0:T(128)S(1)}, s32[32]{0:T(128)S(1)}, u32[]{:S(2)}, u32[]{:S(2)}) collective-permute-start(s32[32]{0:T(128)S(1)} %pad_add_fusion.2), channel_id=1, source_target_pairs={{0,1},{1,0},{2,3},{3,2},{4,5},{5,4},{6,7},{7,6},{8,9},{9,8},{10,11... | collective-permute-start | bytes 392 | tf_op jit(solution)/shard_map/ppermute | solution.py:146
  1.8 5.3 %collective-permute-start.2 = (s32[32]{0:T(128)S(1)}, s32[32]{0:T(128)S(1)}, u32[]{:S(2)}, u32[]{:S(2)}) collective-permute-start(s32[32]{0:T(128)S(1)} %pad_add_fusion.2), channel_id=1, source_target_pairs={{0,2},{1,3},{2,0},{3,1},{4,6},{5,7},{6,4},{7,5},{8,10},{9,11},{10,... | collective-permute-start | bytes 392 | tf_op jit(solution)/shard_map/ppermute | solution.py:146
  4.4 3.0 %collective-permute-start.3 = (s32[32]{0:T(128)S(1)}, s32[32]{0:T(128)S(1)}, u32[]{:S(2)}, u32[]{:S(2)}) collective-permute-start(s32[32]{0:T(128)S(1)} %pad_add_fusion.2), channel_id=1, source_target_pairs={{0,3},{1,2},{2,1},{3,0},{4,7},{5,6},{6,5},{7,4},{8,11},{9,10},{10,... | collective-permute-start | bytes 392 | tf_op jit(solution)/shard_map/ppermute | solution.py:146
  5.8 0.9 %copy-start.1 = (bf16[256,200]{0,1:T(8,128)(2,1)S(1)}, bf16[256,200]{0,1:T(8,128)(2,1)}, u32[]{:S(2)}) copy-start(bf16[256,200]{0,1:T(8,128)(2,1)} %param.13) | copy-start | bytes 307204
  6.9 1.3 %collective-permute-start = (bf16[208,128]{1,0:T(8,128)(2,1)S(1)}, bf16[208,128]{1,0:T(8,128)(2,1)S(1)}, u32[]{:S(2)}, u32[]{:S(2)}) collective-permute-start(bf16[208,128]{1,0:T(8,128)(2,1)S(1)} %get-tuple-element.28), channel_id=1, source_target_pairs={{0,1},{1,0},{2,3},{3,2},{4,5},{5,4},{6,7},{7,6},{8,9},{9,8},{10,11... | collective-permute-start | bytes 159752 | tf_op jit(solution)/shard_map/ppermute | solution.py:146
  8.2 10.3 %copy-start = (bf16[512,512]{1,0:T(8,128)(2,1)S(1)}, bf16[512,512]{1,0:T(8,128)(2,1)}, u32[]{:S(2)}) copy-start(bf16[512,512]{1,0:T(8,128)(2,1)} %constant.8.clone.table_w_ref.table_h_ref) | copy-start | bytes 1572868
  8.2 10.3 %collective-permute-start.7 = (bf16[2,208,128]{2,1,0:T(8,128)(2,1)S(1)}, bf16[2,208,128]{2,1,0:T(8,128)(2,1)S(1)}, u32[]{:S(2)}, u32[]{:S(2)}) collective-permute-start(bf16[2,208,128]{2,1,0:T(8,128)(2,1)S(1)} %pad_maximum_fusion.2), channel_id=1, source_target_pairs={{0,4},{1,5},{2,6},{3,7},{4,0},{5,1},{6,2},{7,3},{8,12},{9,13},{10,... | collective-permute-start | bytes 319496 | tf_op jit(solution)/shard_map/ppermute | solution.py:146
  10.1 8.1 %collective-permute-start.4 = (s32[4,32]{1,0:T(4,128)S(1)}, s32[4,32]{1,0:T(4,128)S(1)}, u32[]{:S(2)}, u32[]{:S(2)}) collective-permute-start(s32[4,32]{1,0:T(4,128)S(1)} %pad_add_fusion.1.list0_ref), channel_id=1, source_target_pairs={{0,4},{1,5},{2,6},{3,7},{4,0},{5,1},{6,2},{7,3},{8,12},{9,13},{10,... | collective-permute-start | bytes 1544 | tf_op jit(solution)/shard_map/ppermute | solution.py:146
  10.3 7.8 %collective-permute-start.5 = (s32[4,32]{1,0:T(4,128)S(1)}, s32[4,32]{1,0:T(4,128)S(1)}, u32[]{:S(2)}, u32[]{:S(2)}) collective-permute-start(s32[4,32]{1,0:T(4,128)S(1)} %pad_add_fusion.1.list0_ref), channel_id=1, source_target_pairs={{0,8},{1,9},{2,10},{3,11},{4,12},{5,13},{6,14},{7,15},{8,0},{9,1},... | collective-permute-start | bytes 1544 | tf_op jit(solution)/shard_map/ppermute | solution.py:146
  13.1 5.4 %collective-permute-start.6 = (s32[4,32]{1,0:T(4,128)S(1)}, s32[4,32]{1,0:T(4,128)S(1)}, u32[]{:S(2)}, u32[]{:S(2)}) collective-permute-start(s32[4,32]{1,0:T(4,128)S(1)} %pad_add_fusion.1.list0_ref), channel_id=1, source_target_pairs={{0,12},{1,13},{2,14},{3,15},{4,8},{5,9},{6,10},{7,11},{8,4},{9,5},... | collective-permute-start | bytes 1544 | tf_op jit(solution)/shard_map/ppermute | solution.py:146
  23.9 1.8 %collective-permute-start.9 = (f32[4,200,128]{2,1,0:T(8,128)S(1)}, f32[4,200,128]{2,1,0:T(8,128)S(1)}, u32[]{:S(2)}, u32[]{:S(2)}) collective-permute-start(f32[4,200,128]{2,1,0:T(8,128)S(1)} %get-tuple-element.40), channel_id=1, source_target_pairs={{0,1},{1,0},{2,3},{3,2},{4,5},{5,4},{6,7},{7,6},{8,9},{9,8},{10,11... | collective-permute-start | bytes 1228808 | tf_op jit(solution)/shard_map/ppermute | solution.py:146
  24.0 4.9 %collective-permute-start.8 = (f32[4,200,128]{2,1,0:T(8,128)S(1)}, f32[4,200,128]{2,1,0:T(8,128)S(1)}, u32[]{:S(2)}, u32[]{:S(2)}) collective-permute-start(f32[4,200,128]{2,1,0:T(8,128)S(1)} %get-tuple-element.38), channel_id=1, source_target_pairs={{0,1},{1,0},{2,3},{3,2},{4,5},{5,4},{6,7},{7,6},{8,9},{9,8},{10,11... | collective-permute-start | bytes 1228808 | tf_op jit(solution)/shard_map/ppermute | solution.py:146
  25.8 11.6 %collective-permute-start.10 = (f32[4,200,128]{2,1,0:T(8,128)S(1)}, f32[4,200,128]{2,1,0:T(8,128)S(1)}, u32[]{:S(2)}, u32[]{:S(2)}) collective-permute-start(f32[4,200,128]{2,1,0:T(8,128)S(1)} %add.121), channel_id=1, source_target_pairs={{0,2},{1,3},{2,0},{3,1},{4,6},{5,7},{6,4},{7,5},{8,10},{9,11},{10,... | collective-permute-start | bytes 1228808 | tf_op jit(solution)/shard_map/ppermute | solution.py:146
  27.5 12.1 %collective-permute-start.11 = (bf16[2,2,208,128]{3,2,1,0:T(8,128)(2,1)S(1)}, bf16[2,2,208,128]{3,2,1,0:T(8,128)(2,1)S(1)}, u32[]{:S(2)}, u32[]{:S(2)}) collective-permute-start(bf16[2,2,208,128]{3,2,1,0:T(8,128)(2,1)S(1)} %pad_maximum_fusion.1), channel_id=1, source_target_pairs={{0,8},{1,9},{2,10},{3,11},{4,12},{5,13},{6,14},{7,15},{8,0},{9,1},... | collective-permute-start | bytes 638984 | tf_op jit(solution)/shard_map/ppermute | solution.py:146
  39.6 11.9 %collective-permute-start.15 = (bf16[4,2,208,128]{3,2,1,0:T(8,128)(2,1)S(1)}, bf16[4,2,208,128]{3,2,1,0:T(8,128)(2,1)S(1)}, u32[]{:S(2)}, u32[]{:S(2)}) collective-permute-start(bf16[4,2,208,128]{3,2,1,0:T(8,128)(2,1)S(1)} %pad_maximum_fusion.near_ref), channel_id=1, source_target_pairs={{0,2},{1,3},{2,0},{3,1},{4,6},{5,7},{6,4},{7,5},{8,10},{9,11},{10,... | collective-permute-start | bytes 1277960 | tf_op jit(solution)/shard_map/ppermute | solution.py:146
  40.3 5.9 %collective-permute-start.12 = (f32[200,128]{1,0:T(8,128)S(1)}, f32[200,128]{1,0:T(8,128)S(1)}, u32[]{:S(2)}, u32[]{:S(2)}) collective-permute-start(f32[200,128]{1,0:T(8,128)S(1)} %get-tuple-element.43), channel_id=1, source_target_pairs={{0,4},{1,5},{2,6},{3,7},{4,0},{5,1},{6,2},{7,3},{8,12},{9,13},{10,... | collective-permute-start | bytes 307208 | tf_op jit(solution)/shard_map/ppermute | solution.py:146
  40.3 11.1 %collective-permute-start.13 = (f32[200,128]{1,0:T(8,128)S(1)}, f32[200,128]{1,0:T(8,128)S(1)}, u32[]{:S(2)}, u32[]{:S(2)}) collective-permute-start(f32[200,128]{1,0:T(8,128)S(1)} %get-tuple-element.44), channel_id=1, source_target_pairs={{0,8},{1,9},{2,10},{3,11},{4,12},{5,13},{6,14},{7,15},{8,0},{9,1},... | collective-permute-start | bytes 307208 | tf_op jit(solution)/shard_map/ppermute | solution.py:146
  43.5 7.9 %collective-permute-start.14 = (f32[200,128]{1,0:T(8,128)S(1)}, f32[200,128]{1,0:T(8,128)S(1)}, u32[]{:S(2)}, u32[]{:S(2)}) collective-permute-start(f32[200,128]{1,0:T(8,128)S(1)} %get-tuple-element.45), channel_id=1, source_target_pairs={{0,12},{1,13},{2,14},{3,15},{4,8},{5,9},{6,10},{7,11},{8,4},{9,5},... | collective-permute-start | bytes 307208 | tf_op jit(solution)/shard_map/ppermute | solution.py:146
  51.5 6.4 %collective-permute-start.17 = (bf16[200,128]{1,0:T(8,128)(2,1)S(1)}, bf16[200,128]{1,0:T(8,128)(2,1)S(1)}, u32[]{:S(2)}, u32[]{:S(2)}) collective-permute-start(bf16[200,128]{1,0:T(8,128)(2,1)S(1)} %add_convert_fusion.refs_0_), channel_id=1, source_target_pairs={{0,4},{1,5},{2,6},{3,7},{4,0},{5,1},{6,2},{7,3},{8,12},{9,13},{10,... | collective-permute-start | bytes 153608 | tf_op jit(solution)/shard_map/ppermute | solution.py:146
  53.2 6.0 %collective-permute-start.19 = (bf16[200,128]{1,0:T(8,128)(2,1)S(1)}, bf16[200,128]{1,0:T(8,128)(2,1)S(1)}, u32[]{:S(2)}, u32[]{:S(2)}) collective-permute-start(bf16[200,128]{1,0:T(8,128)(2,1)S(1)} %add_convert_fusion.refs_0_), channel_id=1, source_target_pairs={{0,8},{1,9},{2,10},{3,11},{4,12},{5,13},{6,14},{7,15},{8,0},{9,1},... | collective-permute-start | bytes 153608 | tf_op jit(solution)/shard_map/ppermute | solution.py:146
  54.5 5.9 %collective-permute-start.21 = (bf16[200,128]{1,0:T(8,128)(2,1)S(1)}, bf16[200,128]{1,0:T(8,128)(2,1)S(1)}, u32[]{:S(2)}, u32[]{:S(2)}) collective-permute-start(bf16[200,128]{1,0:T(8,128)(2,1)S(1)} %add_convert_fusion.refs_0_), channel_id=1, source_target_pairs={{0,12},{1,13},{2,14},{3,15},{4,8},{5,9},{6,10},{7,11},{8,4},{9,5},... | collective-permute-start | bytes 153608 | tf_op jit(solution)/shard_map/ppermute | solution.py:146
  56.3 7.1 %collective-permute-start.16 = (bf16[200,128]{1,0:T(8,128)(2,1)S(1)}, bf16[200,128]{1,0:T(8,128)(2,1)S(1)}, u32[]{:S(2)}, u32[]{:S(2)}) collective-permute-start(bf16[200,128]{1,0:T(8,128)(2,1)S(1)} %add_convert_fusion.refs_0_), channel_id=1, source_target_pairs={{0,2},{1,3},{2,0},{3,1},{4,6},{5,7},{6,4},{7,5},{8,10},{9,11},{10,... | collective-permute-start | bytes 153608 | tf_op jit(solution)/shard_map/ppermute | solution.py:146
  57.8 5.6 %collective-permute-start.18 = (bf16[200,128]{1,0:T(8,128)(2,1)S(1)}, bf16[200,128]{1,0:T(8,128)(2,1)S(1)}, u32[]{:S(2)}, u32[]{:S(2)}) collective-permute-start(bf16[200,128]{1,0:T(8,128)(2,1)S(1)} %collective-permute-done.17.refs_2_), channel_id=1, source_target_pairs={{0,2},{1,3},{2,0},{3,1},{4,6},{5,7},{6,4},{7,5},{8,10},{9,11},{10,... | collective-permute-start | bytes 153608 | tf_op jit(solution)/shard_map/ppermute | solution.py:146
  59.1 4.3 %collective-permute-start.20 = (bf16[200,128]{1,0:T(8,128)(2,1)S(1)}, bf16[200,128]{1,0:T(8,128)(2,1)S(1)}, u32[]{:S(2)}, u32[]{:S(2)}) collective-permute-start(bf16[200,128]{1,0:T(8,128)(2,1)S(1)} %collective-permute-done.19.refs_4_), channel_id=1, source_target_pairs={{0,2},{1,3},{2,0},{3,1},{4,6},{5,7},{6,4},{7,5},{8,10},{9,11},{10,... | collective-permute-start | bytes 153608 | tf_op jit(solution)/shard_map/ppermute | solution.py:146
  60.4 4.1 %collective-permute-start.22 = (bf16[200,128]{1,0:T(8,128)(2,1)S(1)}, bf16[200,128]{1,0:T(8,128)(2,1)S(1)}, u32[]{:S(2)}, u32[]{:S(2)}) collective-permute-start(bf16[200,128]{1,0:T(8,128)(2,1)S(1)} %collective-permute-done.21.refs_6_), channel_id=1, source_target_pairs={{0,2},{1,3},{2,0},{3,1},{4,6},{5,7},{6,4},{7,5},{8,10},{9,11},{10,... | collective-permute-start | bytes 153608 | tf_op jit(solution)/shard_map/ppermute | solution.py:146
  66.5 2.0 %collective-permute-start.23 = (f32[208,512]{1,0:T(8,128)S(1)}, f32[208,512]{1,0:T(8,128)S(1)}, u32[]{:S(2)}, u32[]{:S(2)}) collective-permute-start(f32[208,512]{1,0:T(8,128)S(1)} %gram_and_cross.1.mine_ref), channel_id=1, source_target_pairs={{0,1},{1,0},{2,3},{3,2},{4,5},{5,4},{6,7},{7,6},{8,9},{9,8},{10,11... | collective-permute-start | bytes 1277960 | tf_op jit(solution)/shard_map/ppermute | solution.py:146

commit v5 on v4

--- a/solution.py
+++ b/solution.py
@@ -186,8 +186,9 @@
 
 
 def shares_kernel(
-    list0_ref, list1_ref, list2_ref, list3_ref, place_ref, maps_ref, table_w_ref, table_h_ref, k0_ref, k1_ref, s0_ref, s1_ref,
-    full_ref, pick_ref, row_ref, spread_ref,
+    list0_ref, list1_ref, list2_ref, list3_ref, maps_ref, table_w_ref, table_h_ref,
+    k0_ref, k1_ref, s0_ref, s1_ref,
+    lists_ref, arrived, full_ref, pick_ref, row_ref, spread_ref,
 ):
     rows, members, width = maps_ref.shape
     devices, depth, _ = row_ref.shape
@@ -195,23 +196,38 @@
     height = table_h_ref.shape[0]
     per_column = height // BLK
     columns_here = width // devices
-    me = place_ref[0]
-    list_refs = (list0_ref, list1_ref, list2_ref, list3_ref)
-
-    def block(delta, p):
-        return list_refs[delta // 4][delta % 4, p]
+    me = lax.axis_index("map")
+    copies = [
+        pltpu.make_async_copy(ref, lists_ref.at[i], arrived.at[i])
+        for i, ref in enumerate((list0_ref, list1_ref, list2_ref, list3_ref))
+    ]
+    for copy in copies:
+        copy.start()
+
+    def column_of(delta, p):
+        number = lists_ref[delta // 4, delta % 4, p]
+        if per_column & (per_column - 1) == 0:
+            return number >> per_column.bit_length() - 1
+        return lax.div(number, per_column)
+
+    def row_of(delta, p):
+        number = lists_ref[delta // 4, delta % 4, p]
+        if per_column & (per_column - 1) == 0:
+            return (number & per_column - 1) * BLK
+        return lax.rem(number, per_column) * BLK
 
     full_ref[...] = table_w_ref[...].astype(jnp.float32)
-    for delta in range(devices):
-        for p in range(keep):
-            column = (me ^ delta) * columns_here + block(delta, p) // per_column
-            pick_ref[pl.ds(delta * keep + p, 1), :] = full_ref[pl.ds(column, 1), :]
     sample = lax.broadcasted_iota(jnp.int32, (height, depth), 0) - me * rows
     held = lax.broadcasted_iota(jnp.int32, (height, depth), 1) // keep
     spread_ref[...] = jnp.dot(
         table_h_ref[...], (sample == held).astype(jnp.bfloat16), preferred_element_type=jnp.float32
     )
-
+    for copy in copies:
+        copy.wait()
+    for delta in range(devices):
+        for p in range(keep):
+            column = (me ^ delta) * columns_here + column_of(delta, p)
+            pick_ref[pl.ds(delta * keep + p, 1), :] = full_ref[pl.ds(column, 1), :]
     pick = pick_ref[...].astype(jnp.bfloat16)
     for row in range(rows):
         rowwise = lax.dot_general(
@@ -225,7 +241,7 @@
             delta = high * 4 + low
             wide = []
             for p in range(keep):
-                start = pl.multiple_of(block(delta, p) % per_column * BLK, BLK)
+                start = pl.multiple_of(row_of(delta, p), BLK)
                 wide.append(jnp.where(position == p, spread_ref[pl.ds(start, BLK), :], 0.0))
             wide = jnp.concatenate(wide, axis=0).astype(jnp.bfloat16)
             out_ref[high] = jnp.dot(
@@ -233,7 +249,7 @@
             ).T
 
 
-def shares(lists, place, maps, table_w, table_h):
+def shares(lists, maps, table_w, table_h):
     rows, members, width = maps.shape
     devices = sum(part.shape[0] for part in lists)
     keep = lists[0].shape[1] // 2
@@ -241,10 +257,12 @@
     out = jax.ShapeDtypeStruct((devices // 4, members, keep * BLK), jnp.float32)
     return pl.pallas_call(
         shares_kernel,
-        in_specs=[SMEM] * 5 + [VMEM] * 3,
+        in_specs=[VMEM] * 7,
         out_specs=[VMEM] * 4,
         out_shape=[out] * 4,
         scratch_shapes=[
+            pltpu.SMEM((len(lists),) + lists[0].shape, jnp.int32),
+            pltpu.SemaphoreType.DMA((len(lists),)),
             pltpu.VMEM(table_w.shape, jnp.float32),
             pltpu.VMEM((devices * keep, width), jnp.float32),
             pltpu.VMEM((devices, depth, members), jnp.bfloat16),
@@ -257,13 +275,13 @@
             transcendentals=0,
         ),
         name="coefficient_shares",
-    )(*lists, place, maps, table_w, table_h)
-
-
-def split_noise_kernel(place_ref, noise_ref, data_ref, keep_ref, send_ref):
+    )(*lists, maps, table_w, table_h)
+
+
+def split_noise_kernel(noise_ref, observed_ref, scale_ref, keep_ref, send_ref):
     members, slots = noise_ref.shape
     half = slots // 2
-    core = place_ref[0] & 1
+    core = lax.axis_index("map") & 1
     span = 2 * CAP * BLK // 2
     row = lax.broadcasted_iota(jnp.int32, (slots, slots), 0)
     lane = lax.broadcasted_iota(jnp.int32, (slots, slots), 1)
@@ -274,7 +292,8 @@
     value = jnp.concatenate(
         [
             noise_ref[...].astype(jnp.float32),
-            data_ref[...].astype(jnp.float32),
+            observed_ref[...].astype(jnp.float32).reshape(1, slots),
+            scale_ref[...].astype(jnp.float32).reshape(1, slots),
             extra,
         ],
         axis=0,
@@ -284,25 +303,25 @@
     send_ref[...] = moved[:, half:slots]
 
 
-def split_noise(place, noise, data):
+def split_noise(noise, observed, scale):
     members, slots = noise.shape
     rows = -(-(members + 2) // 16) * 16
     out = jax.ShapeDtypeStruct((rows, slots // 2), jnp.bfloat16)
     return pl.pallas_call(
         split_noise_kernel,
-        in_specs=[SMEM] + [VMEM] * 2,
+        in_specs=[VMEM] * 3,
         out_specs=[VMEM] * 2,
         out_shape=[out] * 2,
         compiler_params=pltpu.CompilerParams(vmem_limit_bytes=VMEM_LIMIT),
         name="split_noise",
-    )(place, noise, data)
-
-
-def select_noise_kernel(starts_ref, place_ref, near_ref, far_ref, out_ref, wide_ref, rows_ref):
+    )(noise, observed, scale)
+
+
+def select_noise_kernel(starts_ref, near_ref, far_ref, out_ref, wide_ref, rows_ref):
     rows, per = near_ref.shape[-2:]
     chips = out_ref.shape[0]
     keep = per // BLK
-    chip = place_ref[0]
+    chip = lax.axis_index("map") >> 1
     units = near_ref.shape[0] * near_ref.shape[1]
     wide_ref[:, rows:256] = jnp.zeros((wide_ref.shape[0], 256 - rows), jnp.float32)
     for i, ref in enumerate((near_ref, far_ref)):
@@ -317,12 +336,12 @@
         out_ref[chip ^ i] = rows_ref[...].T[0:rows]
 
 
-def select_noise(starts, place, near, far):
+def select_noise(starts, near, far):
     rows, per = near.shape[-2:]
     chips = starts.shape[0] * BLK // per
     return pl.pallas_call(
         select_noise_kernel,
-        in_specs=[SMEM, SMEM, VMEM, VMEM],
+        in_specs=[SMEM, VMEM, VMEM],
         out_specs=VMEM,
         out_shape=jax.ShapeDtypeStruct((chips, rows, per), jnp.float32),
         scratch_shapes=[
@@ -331,16 +350,16 @@
         ],
         compiler_params=pltpu.CompilerParams(vmem_limit_bytes=VMEM_LIMIT),
         name="select_noise",
-    )(starts, place, near, far)
-
-
-def gram_kernel(place_ref, target_ref, noise_ref, *refs):
+    )(starts, near, far)
+
+
+def gram_kernel(target_ref, noise_ref, *refs):
     predicted_refs = refs[:8]
     out_ref, predicted_ref, left_ref, right_ref, misfit_ref = refs[8:]
     groups, members, per = predicted_ref.shape
     coefficients = groups * per
     weight_scale = members / (2 * coefficients)
-    chip = place_ref[0]
+    chip = lax.axis_index("map") >> 1
     for i, ref in enumerate(predicted_refs):
         predicted_ref[chip ^ i] = ref[...].astype(jnp.float32)
     right_ref[...] = jnp.zeros_like(right_ref)
@@ -385,13 +404,13 @@
     )
 
 
-def gram(place, target, noise, predicted):
+def gram(target, noise, predicted):
     members, per = predicted[0].shape
     groups = len(predicted)
     coefficients = groups * per
     return pl.pallas_call(
         gram_kernel,
-        in_specs=[SMEM] + [VMEM] * (2 + len(predicted)),
+        in_specs=[VMEM] * (2 + len(predicted)),
         out_specs=VMEM,
         out_shape=jax.ShapeDtypeStruct((members + 8, 512), jnp.float32),
         scratch_shapes=[
@@ -402,7 +421,7 @@
         ],
         compiler_params=pltpu.CompilerParams(vmem_limit_bytes=VMEM_LIMIT),
         name="gram_and_cross",
-    )(place, target, noise, *predicted)
+    )(target, noise, *predicted)
 
 
 def update_kernel(
@@ -509,28 +528,26 @@
     lists = jnp.concatenate([kept_blocks, block_owner[:, 0]])
     lists = jnp.stack([lists] + [swap(lists, delta) for delta in range(1, 4)])
 
-    noise_keep, noise_send = split_noise(
-        me.reshape(1), perturbation.T, jnp.stack([observed, error_scale])
-    )
+    noise_keep, noise_send = split_noise(perturbation.T, observed, error_scale)
     noise = jnp.stack([noise_keep, swap(noise_send, 1)])
     amplitude_maps, noise, lists = lax.optimization_barrier((amplitude_maps, noise, lists))
     lists = [lists] + [swap(lists, 4 * i) for i in range(1, devices // 4)]
-    near_z = swap(noise, 4)
+    far_z = swap(noise, 8)
 
     maps = by_row(amplitude_maps)
     table_w = jnp.asarray(dct_constant(map_width))
     table_h = table_w if map_height == map_width else jnp.asarray(dct_constant(map_height))
-    lists, near_z = lax.optimization_barrier((lists, near_z))
-    keep_0, keep_1, send_0, send_1 = shares(lists, me.reshape(1), maps, table_w, table_h)
+    lists, far_z = lax.optimization_barrier((lists, far_z))
+    keep_0, keep_1, send_0, send_1 = shares(lists, maps, table_w, table_h)
 
     share_1 = keep_1 + swap(send_1, 1)
     got_1 = swap(share_1, 2)
     share_0 = keep_0 + swap(send_0, 1)
     share = [share_0[i] + got_1[i] for i in range(devices // 4)]
-    noise = jnp.stack([noise, near_z])
-    far_z = swap(noise, 8)
-    share, far_z = lax.optimization_barrier((share, far_z))
-    near_noise = jnp.concatenate([noise, far_z])
+    noise = jnp.stack([noise, far_z])
+    near_z = swap(noise, 4)
+    share, near_z = lax.optimization_barrier((share, near_z))
+    near_noise = jnp.concatenate([noise, near_z])
     far_noise = swap(near_noise, 2)
     got = [swap(share[i], 4 * i) for i in range(1, devices // 4)]
     predicted = (share[0] + got[0] + got[1] + got[2]).astype(jnp.bfloat16)
@@ -549,15 +566,15 @@
     rank = jnp.sum(earlier.astype(jnp.int32), axis=2)
     chips = chip ^ jnp.arange(devices // 2, dtype=jnp.int32)[:, None]
     away = owner ^ me
-    held = (away >> 1 & 1) * 8 + (away >> 2) * 2 + (away & 1)
+    held = (away >> 1 & 1) * 8 + (away >> 2 & 1) * 4 + (away >> 3) * 2 + (away & 1)
     noise_rows = held * (slots // 2) + chips * (CAP * BLK) + rank * BLK
     data_row = (chips * 2 + core) * (CAP * BLK) + rank * BLK
     target = jnp.where(away < 2, away * slots + data_row, -1024)
     target = (target[:, :, None] + jnp.arange(BLK, dtype=jnp.int32)).reshape(
         devices // 2, keep * BLK, 1
     )
-    noise = select_noise(noise_rows.reshape(-1), chip.reshape(1), near_noise, far_noise)
-    mine = gram(chip.reshape(1), target, noise, gathered)
+    noise = select_noise(noise_rows.reshape(-1), near_noise, far_noise)
+    mine = gram(target, noise, gathered)
     updated_slab, update_weights, data_misfit = update(mine, swap(mine, 1), model_slab)
     return (updated_slab, update_weights, data_misfit.reshape(-1))
 

time: 76.7 us -> 73.6 us (0.960)
  waiting for transfers between devices: 23.4 us -> 21.3 us
  Pallas kernels: 20.3 us -> 19.3 us
    ppermute x24, waiting for transfers between devices: 23.4 us -> 21.3 us  [swap(): return lax.ppermute(value, 'map', pairs)]
    another operation x2 -> x0, local copies, waits for them, and re-layouts: 1.32 us -> none  [sparse_body(): jnp.stack([observed, error_scale])]
    unnamed x4 -> x8, local copies, waits for them, and re-layouts: 0.89 us -> 2.21 us
    pallas_call x4, Pallas kernels: 8.74 us -> 7.6 us  [the longest x1 4.26 us: shares(): pl.pallas_call(shares_kernel, in_specs=[VMEM] * 7, out_specs=[VMEM] * 4,...]
  transfers between devices with their start and end apart: 24 -> 24, of which waited for: 12 -> 11; matrix products, arithmetic and copies ran while one was open for 3% -> 2% of each run, Pallas kernels for 7% -> 7%
where the time goes in v5:
time: 73.6 us; the launch traced here: 73.4 us
  starting transfers between devices  27.6 us (38%)
  waiting for transfers between devices  21.3 us (29%)
  Pallas kernels  19.3 us (26%)
  local copies, waits for them, and re-layouts  2.73 us (4%)
  other arithmetic  1.51 us (2%)
  between operations  1.01 us (1%)
    ppermute x24, starting transfers between devices, swap(): return lax.ppermute(value, 'map', pairs)  27.6 us
    ppermute x24, waiting for transfers between devices, swap(): return lax.ppermute(value, 'map', pairs)  21.3 us
    pallas_call x1, Pallas kernels, update(): pl.pallas_call(update_kernel, in_specs=[VMEM, VMEM, HBM], out_specs=[HBM,...  8.09 us
    pallas_call x1, Pallas kernels, shares(): pl.pallas_call(shares_kernel, in_specs=[VMEM] * 7, out_specs=[VMEM] * 4,...  4.26 us
    pallas_call x1, Pallas kernels, by_row(): pl.pallas_call(by_row_kernel, in_specs=[HBM], out_specs=VMEM, out_shape=j...  3.65 us
    unnamed x8, local copies, waits for them, and re-layouts  2.21 us
    pallas_call x1, Pallas kernels, gram(): pl.pallas_call(gram_kernel, in_specs=[VMEM] * (2 + len(predicted)), out_s...  1.89 us
  transfers between devices with their start and end apart: 24, of which 11 were waited for; matrix products, arithmetic and copies ran while one was open for 2% of the time, Pallas kernels for 7%

profile of v5, /device:TPU:0, one launch (start us, length us, event | category | flops | bytes accessed | tf_op | source)
XLA Modules:
  0.0 73.4 jit_solution(15412012105672327360)
XLA Ops:
  0.6 0.7 %pad_add_fusion.2 = s32[32]{0:T(128)S(1)} fusion(s32[16]{0:T(128)} %bitcast.31, s32[16]{0:T(128)} %param.9), kind=kLoop, calls=%fused_computation.19 | loop fusion | flops 32 | bytes 256 | tf_op jit(solution)/shard_map/concatenate | solution.py:528
  1.8 2.5 %collective-permute-start.2 = (s32[32]{0:T(128)S(1)}, s32[32]{0:T(128)S(1)}, u32[]{:S(2)}, u32[]{:S(2)}) collective-permute-start(s32[32]{0:T(128)S(1)} %pad_add_fusion.2), channel_id=1, source_target_pairs={{0,2},{1,3},{2,0},{3,1},{4,6},{5,7},{6,4},{7,5},{8,10},{9,11},{10,... | collective-permute-start | bytes 392 | tf_op jit(solution)/shard_map/ppermute | solution.py:146
  4.5 0.9 %copy-done.1 = bf16[256,200]{0,1:T(8,128)(2,1)S(1)} copy-done((bf16[256,200]{0,1:T(8,128)(2,1)S(1)}, bf16[256,200]{0,1:T(8,128)(2,1)}, u32[]{:S(2)}) %copy-start.1) | copy-done | bytes 102424
  5.4 0.7 copy-done.2
  6.0 0.7 copy-done.3
  7.4 0.8 %collective-permute-done = bf16[208,128]{1,0:T(8,128)(2,1)S(1)} collective-permute-done((bf16[208,128]{1,0:T(8,128)(2,1)S(1)}, bf16[208,128]{1,0:T(8,128)(2,1)S(1)}, u32[]{:S(2)}, u32[]{:S(2)}) %collective-permute-start) | collective-permute-done | bytes 53280 | tf_op jit(solution)/shard_map/ppermute | solution.py:146
  8.2 2.9 %collective-permute-start.7 = (bf16[2,208,128]{2,1,0:T(8,128)(2,1)S(1)}, bf16[2,208,128]{2,1,0:T(8,128)(2,1)S(1)}, u32[]{:S(2)}, u32[]{:S(2)}) collective-permute-start(bf16[2,208,128]{2,1,0:T(8,128)(2,1)S(1)} %pad_maximum_fusion.2), channel_id=1, source_target_pairs={{0,8},{1,9},{2,10},{3,11},{4,12},{5,13},{6,14},{7,15},{8,0},{9,1},... | collective-permute-start | bytes 319496 | tf_op jit(solution)/shard_map/ppermute | solution.py:146
  11.1 1.6 %collective-permute-start.4 = (s32[4,32]{1,0:T(4,128)S(1)}, s32[4,32]{1,0:T(4,128)S(1)}, u32[]{:S(2)}, u32[]{:S(2)}) collective-permute-start(s32[4,32]{1,0:T(4,128)S(1)} %pad_add_fusion.1.list0_ref), channel_id=1, source_target_pairs={{0,4},{1,5},{2,6},{3,7},{4,0},{5,1},{6,2},{7,3},{8,12},{9,13},{10,... | collective-permute-start | bytes 1544 | tf_op jit(solution)/shard_map/ppermute | solution.py:146
  13.0 2.5 %collective-permute-start.6 = (s32[4,32]{1,0:T(4,128)S(1)}, s32[4,32]{1,0:T(4,128)S(1)}, u32[]{:S(2)}, u32[]{:S(2)}) collective-permute-start(s32[4,32]{1,0:T(4,128)S(1)} %pad_add_fusion.1.list0_ref), channel_id=1, source_target_pairs={{0,12},{1,13},{2,14},{3,15},{4,8},{5,9},{6,10},{7,11},{8,4},{9,5},... | collective-permute-start | bytes 1544 | tf_op jit(solution)/shard_map/ppermute | solution.py:146
  15.5 3.7 %maps_by_row.1.maps_ref = bf16[32,200,512]{2,1,0:T(8,128)(2,1)S(1)} custom-call(bf16[200,32,512]{2,1,0:T(8,128)(2,1)} %maps_ref), custom_call_target="tpu_custom_call" | custom-call | bytes 13107200 | tf_op jit(solution)/shard_map/maps_by_row/pallas_call | solution.py:171
  19.2 4.3 %coefficient_shares.1 = (f32[4,200,128]{2,1,0:T(8,128)S(1)}, f32[4,200,128]{2,1,0:T(8,128)S(1)}, f32[4,200,128]{2,1,0:T(8,128)S(1)}, f32[4,200,128]{2,1,0:T(8,128)S(1)}) custom-call(s32[4,32]{1,0:T(4,128)S(1)} %pad_add_fusion.1.list0_ref, s32[4,32]{1,0:T(4,128)S(1)} %collective-permute-done.4.list1_ref, s32[4,32]{1,0:T(4,128)S(1)} %collective-permute-done.5.list2_ref, ...), custom_call_target="tpu_custom_call" | custom-call | flops 1677721600 | bytes 6553600 | tf_op jit(solution)/shard_map/coefficient_shares/pallas_call | solution.py:258
  24.0 1.2 %collective-permute-done.9 = f32[4,200,128]{2,1,0:T(8,128)S(1)} collective-permute-done((f32[4,200,128]{2,1,0:T(8,128)S(1)}, f32[4,200,128]{2,1,0:T(8,128)S(1)}, u32[]{:S(2)}, u32[]{:S(2)}) %collective-permute-start.9) | collective-permute-done | bytes 409632 | tf_op jit(solution)/shard_map/ppermute | solution.py:146
  25.3 1.6 %collective-permute-start.10 = (f32[4,200,128]{2,1,0:T(8,128)S(1)}, f32[4,200,128]{2,1,0:T(8,128)S(1)}, u32[]{:S(2)}, u32[]{:S(2)}) collective-permute-start(f32[4,200,128]{2,1,0:T(8,128)S(1)} %add.125), channel_id=1, source_target_pairs={{0,2},{1,3},{2,0},{3,1},{4,6},{5,7},{6,4},{7,5},{8,10},{9,11},{10,... | collective-permute-start | bytes 1228808 | tf_op jit(solution)/shard_map/ppermute | solution.py:146
  27.0 0.7 %collective-permute-start.11 = (bf16[2,2,208,128]{3,2,1,0:T(8,128)(2,1)S(1)}, bf16[2,2,208,128]{3,2,1,0:T(8,128)(2,1)S(1)}, u32[]{:S(2)}, u32[]{:S(2)}) collective-permute-start(bf16[2,2,208,128]{3,2,1,0:T(8,128)(2,1)S(1)} %pad_maximum_fusion.1), channel_id=1, source_target_pairs={{0,4},{1,5},{2,6},{3,7},{4,0},{5,1},{6,2},{7,3},{8,12},{9,13},{10,... | collective-permute-start | bytes 638984 | tf_op jit(solution)/shard_map/ppermute | solution.py:146
  27.8 9.1 %collective-permute-done.10 = f32[4,200,128]{2,1,0:T(8,128)S(1)} collective-permute-done((f32[4,200,128]{2,1,0:T(8,128)S(1)}, f32[4,200,128]{2,1,0:T(8,128)S(1)}, u32[]{:S(2)}, u32[]{:S(2)}) %collective-permute-start.10) | collective-permute-done | bytes 409632 | tf_op jit(solution)/shard_map/ppermute | solution.py:146
  37.0 1.6 %collective-permute-start.15 = (bf16[4,2,208,128]{3,2,1,0:T(8,128)(2,1)S(1)}, bf16[4,2,208,128]{3,2,1,0:T(8,128)(2,1)S(1)}, u32[]{:S(2)}, u32[]{:S(2)}) collective-permute-start(bf16[4,2,208,128]{3,2,1,0:T(8,128)(2,1)S(1)} %pad_maximum_fusion.near_ref), channel_id=1, source_target_pairs={{0,2},{1,3},{2,0},{3,1},{4,6},{5,7},{6,4},{7,5},{8,10},{9,11},{10,... | collective-permute-start | bytes 1277960 | tf_op jit(solution)/shard_map/ppermute | solution.py:146
  38.7 0.7 collective-permute-start.12
  39.3 1.6 %collective-permute-start.13 = (f32[200,128]{1,0:T(8,128)S(1)}, f32[200,128]{1,0:T(8,128)S(1)}, u32[]{:S(2)}, u32[]{:S(2)}) collective-permute-start(f32[200,128]{1,0:T(8,128)S(1)} %get-tuple-element.44), channel_id=1, source_target_pairs={{0,8},{1,9},{2,10},{3,11},{4,12},{5,13},{6,14},{7,15},{8,0},{9,1},... | collective-permute-start | bytes 307208 | tf_op jit(solution)/shard_map/ppermute | solution.py:146
  40.9 2.1 %collective-permute-start.14 = (f32[200,128]{1,0:T(8,128)S(1)}, f32[200,128]{1,0:T(8,128)S(1)}, u32[]{:S(2)}, u32[]{:S(2)}) collective-permute-start(f32[200,128]{1,0:T(8,128)S(1)} %get-tuple-element.45), channel_id=1, source_target_pairs={{0,12},{1,13},{2,14},{3,15},{4,8},{5,9},{6,10},{7,11},{8,4},{9,5},... | collective-permute-start | bytes 307208 | tf_op jit(solution)/shard_map/ppermute | solution.py:146
  43.8 5.5 %collective-permute-done.13 = f32[200,128]{1,0:T(8,128)S(1)} collective-permute-done((f32[200,128]{1,0:T(8,128)S(1)}, f32[200,128]{1,0:T(8,128)S(1)}, u32[]{:S(2)}, u32[]{:S(2)}) %collective-permute-start.13) | collective-permute-done | bytes 102432 | tf_op jit(solution)/shard_map/ppermute | solution.py:146
  49.3 1.7 %collective-permute-start.17 = (bf16[200,128]{1,0:T(8,128)(2,1)S(1)}, bf16[200,128]{1,0:T(8,128)(2,1)S(1)}, u32[]{:S(2)}, u32[]{:S(2)}) collective-permute-start(bf16[200,128]{1,0:T(8,128)(2,1)S(1)} %add_convert_fusion.refs_0_), channel_id=1, source_target_pairs={{0,4},{1,5},{2,6},{3,7},{4,0},{5,1},{6,2},{7,3},{8,12},{9,13},{10,... | collective-permute-start | bytes 153608 | tf_op jit(solution)/shard_map/ppermute | solution.py:146
  51.4 2.4 %collective-permute-start.21 = (bf16[200,128]{1,0:T(8,128)(2,1)S(1)}, bf16[200,128]{1,0:T(8,128)(2,1)S(1)}, u32[]{:S(2)}, u32[]{:S(2)}) collective-permute-start(bf16[200,128]{1,0:T(8,128)(2,1)S(1)} %add_convert_fusion.refs_0_), channel_id=1, source_target_pairs={{0,12},{1,13},{2,14},{3,15},{4,8},{5,9},{6,10},{7,11},{8,4},{9,5},... | collective-permute-start | bytes 153608 | tf_op jit(solution)/shard_map/ppermute | solution.py:146
  54.1 0.6 collective-permute-start.16
  54.7 1.5 %collective-permute-start.18 = (bf16[200,128]{1,0:T(8,128)(2,1)S(1)}, bf16[200,128]{1,0:T(8,128)(2,1)S(1)}, u32[]{:S(2)}, u32[]{:S(2)}) collective-permute-start(bf16[200,128]{1,0:T(8,128)(2,1)S(1)} %collective-permute-done.17.refs_2_), channel_id=1, source_target_pairs={{0,2},{1,3},{2,0},{3,1},{4,6},{5,7},{6,4},{7,5},{8,10},{9,11},{10,... | collective-permute-start | bytes 153608 | tf_op jit(solution)/shard_map/ppermute | solution.py:146
  56.4 0.5 collective-permute-start.20
  57.4 1.1 %collective-permute-start.22 = (bf16[200,128]{1,0:T(8,128)(2,1)S(1)}, bf16[200,128]{1,0:T(8,128)(2,1)S(1)}, u32[]{:S(2)}, u32[]{:S(2)}) collective-permute-start(bf16[200,128]{1,0:T(8,128)(2,1)S(1)} %collective-permute-done.21.refs_6_), channel_id=1, source_target_pairs={{0,2},{1,3},{2,0},{3,1},{4,6},{5,7},{6,4},{7,5},{8,10},{9,11},{10,... | collective-permute-start | bytes 153608 | tf_op jit(solution)/shard_map/ppermute | solution.py:146
  58.6 1.2 %select_noise.1.noise_ref = f32[8,208,128]{2,1,0:T(8,128)S(1)} custom-call(s32[128]{0:T(128)S(1)} %reshape.83.starts_ref, bf16[4,2,208,128]{3,2,1,0:T(8,128)(2,1)S(1)} %pad_maximum_fusion.near_ref, bf16[4,2,208,128]{3,2,1,0:T(8,128)(2,1)S(1)} %collective-permute-done.15.far_ref), custom_call_target="tpu_custom_call" | custom-call | tf_op jit(solution)/shard_map/select_noise/pallas_call | solution.py:342
  59.9 0.6 collective-permute-done.20.refs_5_
  60.5 1.0 %collective-permute-done.22.refs_7_ = bf16[200,128]{1,0:T(8,128)(2,1)S(1)} collective-permute-done((bf16[200,128]{1,0:T(8,128)(2,1)S(1)}, bf16[200,128]{1,0:T(8,128)(2,1)S(1)}, u32[]{:S(2)}, u32[]{:S(2)}) %collective-permute-start.22) | collective-permute-done | bytes 51232 | tf_op jit(solution)/shard_map/ppermute | solution.py:146
  61.5 1.9 %gram_and_cross.1.mine_ref = f32[208,512]{1,0:T(8,128)S(1)} custom-call(s32[8,128,1]{2,1,0:T(8,128)S(1)} %broadcast_add_fusion.target_ref, f32[8,208,128]{2,1,0:T(8,128)S(1)} %select_noise.1.noise_ref, bf16[200,128]{1,0:T(8,128)(2,1)S(1)} %add_convert_fusion.refs_0_, bf16[200,128]{1,0:T(8,128)(2,1)S(1)} %collective-permute-done.16.refs_1_, ...), custom_call_target="tpu_custom_call" | custom-call | tf_op jit(solution)/shard_map/gram_and_cross/pallas_call | solution.py:411
  63.4 1.8 %collective-permute-done.23.other_ref = f32[208,512]{1,0:T(8,128)S(1)} collective-permute-done((f32[208,512]{1,0:T(8,128)S(1)}, f32[208,512]{1,0:T(8,128)S(1)}, u32[]{:S(2)}, u32[]{:S(2)}) %collective-permute-start.23) | collective-permute-done | bytes 426016 | tf_op jit(solution)/shard_map/ppermute | solution.py:146
  65.2 8.1 %solve_and_update.1 = (bf16[200,12288]{1,0:T(8,128)(2,1)}, f32[200,200]{1,0:T(8,128)}, f32[1,256]{1,0:T(1,128)}) custom-call(f32[208,512]{1,0:T(8,128)S(1)} %gram_and_cross.1.mine_ref, f32[208,512]{1,0:T(8,128)S(1)} %collective-permute-done.23.other_ref, bf16[200,12288]{1,0:T(8,128)(2,1)} %slab_ref.1), custom_call_target="tpu_custom_call" | custom-call | tf_op jit(solution)/shard_map/solve_and_update/pallas_call | solution.py:497
  (51 shorter events, 4.9 us)
Async XLA Ops:
  1.4 5.7 %collective-permute-start.1 = (s32[32]{0:T(128)S(1)}, s32[32]{0:T(128)S(1)}, u32[]{:S(2)}, u32[]{:S(2)}) collective-permute-start(s32[32]{0:T(128)S(1)} %pad_add_fusion.2), channel_id=1, source_target_pairs={{0,1},{1,0},{2,3},{3,2},{4,5},{5,4},{6,7},{7,6},{8,9},{9,8},{10,11... | collective-permute-start | bytes 392 | tf_op jit(solution)/shard_map/ppermute | solution.py:146
  1.8 5.2 %collective-permute-start.2 = (s32[32]{0:T(128)S(1)}, s32[32]{0:T(128)S(1)}, u32[]{:S(2)}, u32[]{:S(2)}) collective-permute-start(s32[32]{0:T(128)S(1)} %pad_add_fusion.2), channel_id=1, source_target_pairs={{0,2},{1,3},{2,0},{3,1},{4,6},{5,7},{6,4},{7,5},{8,10},{9,11},{10,... | collective-permute-start | bytes 392 | tf_op jit(solution)/shard_map/ppermute | solution.py:146
  4.4 3.0 %collective-permute-start.3 = (s32[32]{0:T(128)S(1)}, s32[32]{0:T(128)S(1)}, u32[]{:S(2)}, u32[]{:S(2)}) collective-permute-start(s32[32]{0:T(128)S(1)} %pad_add_fusion.2), channel_id=1, source_target_pairs={{0,3},{1,2},{2,1},{3,0},{4,7},{5,6},{6,5},{7,4},{8,11},{9,10},{10,... | collective-permute-start | bytes 392 | tf_op jit(solution)/shard_map/ppermute | solution.py:146
  4.5 0.9 %copy-start.1 = (bf16[256,200]{0,1:T(8,128)(2,1)S(1)}, bf16[256,200]{0,1:T(8,128)(2,1)}, u32[]{:S(2)}) copy-start(bf16[256,200]{0,1:T(8,128)(2,1)} %param.13) | copy-start | bytes 307204
  5.4 0.7 copy-start.2
  6.0 0.7 copy-start.3
  6.9 1.3 %collective-permute-start = (bf16[208,128]{1,0:T(8,128)(2,1)S(1)}, bf16[208,128]{1,0:T(8,128)(2,1)S(1)}, u32[]{:S(2)}, u32[]{:S(2)}) collective-permute-start(bf16[208,128]{1,0:T(8,128)(2,1)S(1)} %get-tuple-element.28), channel_id=1, source_target_pairs={{0,1},{1,0},{2,3},{3,2},{4,5},{5,4},{6,7},{7,6},{8,9},{9,8},{10,11... | collective-permute-start | bytes 159752 | tf_op jit(solution)/shard_map/ppermute | solution.py:146
  8.2 11.0 %copy-start = (bf16[512,512]{1,0:T(8,128)(2,1)S(1)}, bf16[512,512]{1,0:T(8,128)(2,1)}, u32[]{:S(2)}) copy-start(bf16[512,512]{1,0:T(8,128)(2,1)} %constant.10.clone.table_w_ref.table_h_ref) | copy-start | bytes 1572868
  8.2 11.0 %collective-permute-start.7 = (bf16[2,208,128]{2,1,0:T(8,128)(2,1)S(1)}, bf16[2,208,128]{2,1,0:T(8,128)(2,1)S(1)}, u32[]{:S(2)}, u32[]{:S(2)}) collective-permute-start(bf16[2,208,128]{2,1,0:T(8,128)(2,1)S(1)} %pad_maximum_fusion.2), channel_id=1, source_target_pairs={{0,8},{1,9},{2,10},{3,11},{4,12},{5,13},{6,14},{7,15},{8,0},{9,1},... | collective-permute-start | bytes 319496 | tf_op jit(solution)/shard_map/ppermute | solution.py:146
  11.1 8.1 %collective-permute-start.4 = (s32[4,32]{1,0:T(4,128)S(1)}, s32[4,32]{1,0:T(4,128)S(1)}, u32[]{:S(2)}, u32[]{:S(2)}) collective-permute-start(s32[4,32]{1,0:T(4,128)S(1)} %pad_add_fusion.1.list0_ref), channel_id=1, source_target_pairs={{0,4},{1,5},{2,6},{3,7},{4,0},{5,1},{6,2},{7,3},{8,12},{9,13},{10,... | collective-permute-start | bytes 1544 | tf_op jit(solution)/shard_map/ppermute | solution.py:146
  12.7 6.5 %collective-permute-start.5 = (s32[4,32]{1,0:T(4,128)S(1)}, s32[4,32]{1,0:T(4,128)S(1)}, u32[]{:S(2)}, u32[]{:S(2)}) collective-permute-start(s32[4,32]{1,0:T(4,128)S(1)} %pad_add_fusion.1.list0_ref), channel_id=1, source_target_pairs={{0,8},{1,9},{2,10},{3,11},{4,12},{5,13},{6,14},{7,15},{8,0},{9,1},... | collective-permute-start | bytes 1544 | tf_op jit(solution)/shard_map/ppermute | solution.py:146
  13.0 6.2 %collective-permute-start.6 = (s32[4,32]{1,0:T(4,128)S(1)}, s32[4,32]{1,0:T(4,128)S(1)}, u32[]{:S(2)}, u32[]{:S(2)}) collective-permute-start(s32[4,32]{1,0:T(4,128)S(1)} %pad_add_fusion.1.list0_ref), channel_id=1, source_target_pairs={{0,12},{1,13},{2,14},{3,15},{4,8},{5,9},{6,10},{7,11},{8,4},{9,5},... | collective-permute-start | bytes 1544 | tf_op jit(solution)/shard_map/ppermute | solution.py:146
  23.5 1.8 %collective-permute-start.9 = (f32[4,200,128]{2,1,0:T(8,128)S(1)}, f32[4,200,128]{2,1,0:T(8,128)S(1)}, u32[]{:S(2)}, u32[]{:S(2)}) collective-permute-start(f32[4,200,128]{2,1,0:T(8,128)S(1)} %get-tuple-element.40), channel_id=1, source_target_pairs={{0,1},{1,0},{2,3},{3,2},{4,5},{5,4},{6,7},{7,6},{8,9},{9,8},{10,11... | collective-permute-start | bytes 1228808 | tf_op jit(solution)/shard_map/ppermute | solution.py:146
  23.5 4.2 %collective-permute-start.8 = (f32[4,200,128]{2,1,0:T(8,128)S(1)}, f32[4,200,128]{2,1,0:T(8,128)S(1)}, u32[]{:S(2)}, u32[]{:S(2)}) collective-permute-start(f32[4,200,128]{2,1,0:T(8,128)S(1)} %get-tuple-element.38), channel_id=1, source_target_pairs={{0,1},{1,0},{2,3},{3,2},{4,5},{5,4},{6,7},{7,6},{8,9},{9,8},{10,11... | collective-permute-start | bytes 1228808 | tf_op jit(solution)/shard_map/ppermute | solution.py:146
  25.3 11.6 %collective-permute-start.10 = (f32[4,200,128]{2,1,0:T(8,128)S(1)}, f32[4,200,128]{2,1,0:T(8,128)S(1)}, u32[]{:S(2)}, u32[]{:S(2)}) collective-permute-start(f32[4,200,128]{2,1,0:T(8,128)S(1)} %add.125), channel_id=1, source_target_pairs={{0,2},{1,3},{2,0},{3,1},{4,6},{5,7},{6,4},{7,5},{8,10},{9,11},{10,... | collective-permute-start | bytes 1228808 | tf_op jit(solution)/shard_map/ppermute | solution.py:146
  27.0 9.9 %collective-permute-start.11 = (bf16[2,2,208,128]{3,2,1,0:T(8,128)(2,1)S(1)}, bf16[2,2,208,128]{3,2,1,0:T(8,128)(2,1)S(1)}, u32[]{:S(2)}, u32[]{:S(2)}) collective-permute-start(bf16[2,2,208,128]{3,2,1,0:T(8,128)(2,1)S(1)} %pad_maximum_fusion.1), channel_id=1, source_target_pairs={{0,4},{1,5},{2,6},{3,7},{4,0},{5,1},{6,2},{7,3},{8,12},{9,13},{10,... | collective-permute-start | bytes 638984 | tf_op jit(solution)/shard_map/ppermute | solution.py:146
  37.0 12.3 %collective-permute-start.15 = (bf16[4,2,208,128]{3,2,1,0:T(8,128)(2,1)S(1)}, bf16[4,2,208,128]{3,2,1,0:T(8,128)(2,1)S(1)}, u32[]{:S(2)}, u32[]{:S(2)}) collective-permute-start(bf16[4,2,208,128]{3,2,1,0:T(8,128)(2,1)S(1)} %pad_maximum_fusion.near_ref), channel_id=1, source_target_pairs={{0,2},{1,3},{2,0},{3,1},{4,6},{5,7},{6,4},{7,5},{8,10},{9,11},{10,... | collective-permute-start | bytes 1277960 | tf_op jit(solution)/shard_map/ppermute | solution.py:146
  38.7 5.1 %collective-permute-start.12 = (f32[200,128]{1,0:T(8,128)S(1)}, f32[200,128]{1,0:T(8,128)S(1)}, u32[]{:S(2)}, u32[]{:S(2)}) collective-permute-start(f32[200,128]{1,0:T(8,128)S(1)} %get-tuple-element.43), channel_id=1, source_target_pairs={{0,4},{1,5},{2,6},{3,7},{4,0},{5,1},{6,2},{7,3},{8,12},{9,13},{10,... | collective-permute-start | bytes 307208 | tf_op jit(solution)/shard_map/ppermute | solution.py:146
  39.3 9.9 %collective-permute-start.13 = (f32[200,128]{1,0:T(8,128)S(1)}, f32[200,128]{1,0:T(8,128)S(1)}, u32[]{:S(2)}, u32[]{:S(2)}) collective-permute-start(f32[200,128]{1,0:T(8,128)S(1)} %get-tuple-element.44), channel_id=1, source_target_pairs={{0,8},{1,9},{2,10},{3,11},{4,12},{5,13},{6,14},{7,15},{8,0},{9,1},... | collective-permute-start | bytes 307208 | tf_op jit(solution)/shard_map/ppermute | solution.py:146
  40.9 8.4 %collective-permute-start.14 = (f32[200,128]{1,0:T(8,128)S(1)}, f32[200,128]{1,0:T(8,128)S(1)}, u32[]{:S(2)}, u32[]{:S(2)}) collective-permute-start(f32[200,128]{1,0:T(8,128)S(1)} %get-tuple-element.45), channel_id=1, source_target_pairs={{0,12},{1,13},{2,14},{3,15},{4,8},{5,9},{6,10},{7,11},{8,4},{9,5},... | collective-permute-start | bytes 307208 | tf_op jit(solution)/shard_map/ppermute | solution.py:146
  49.3 5.4 %collective-permute-start.17 = (bf16[200,128]{1,0:T(8,128)(2,1)S(1)}, bf16[200,128]{1,0:T(8,128)(2,1)S(1)}, u32[]{:S(2)}, u32[]{:S(2)}) collective-permute-start(bf16[200,128]{1,0:T(8,128)(2,1)S(1)} %add_convert_fusion.refs_0_), channel_id=1, source_target_pairs={{0,4},{1,5},{2,6},{3,7},{4,0},{5,1},{6,2},{7,3},{8,12},{9,13},{10,... | collective-permute-start | bytes 153608 | tf_op jit(solution)/shard_map/ppermute | solution.py:146
  51.0 5.4 %collective-permute-start.19 = (bf16[200,128]{1,0:T(8,128)(2,1)S(1)}, bf16[200,128]{1,0:T(8,128)(2,1)S(1)}, u32[]{:S(2)}, u32[]{:S(2)}) collective-permute-start(bf16[200,128]{1,0:T(8,128)(2,1)S(1)} %add_convert_fusion.refs_0_), channel_id=1, source_target_pairs={{0,8},{1,9},{2,10},{3,11},{4,12},{5,13},{6,14},{7,15},{8,0},{9,1},... | collective-permute-start | bytes 153608 | tf_op jit(solution)/shard_map/ppermute | solution.py:146
  51.4 6.0 %collective-permute-start.21 = (bf16[200,128]{1,0:T(8,128)(2,1)S(1)}, bf16[200,128]{1,0:T(8,128)(2,1)S(1)}, u32[]{:S(2)}, u32[]{:S(2)}) collective-permute-start(bf16[200,128]{1,0:T(8,128)(2,1)S(1)} %add_convert_fusion.refs_0_), channel_id=1, source_target_pairs={{0,12},{1,13},{2,14},{3,15},{4,8},{5,9},{6,10},{7,11},{8,4},{9,5},... | collective-permute-start | bytes 153608 | tf_op jit(solution)/shard_map/ppermute | solution.py:146
  54.1 5.8 %collective-permute-start.16 = (bf16[200,128]{1,0:T(8,128)(2,1)S(1)}, bf16[200,128]{1,0:T(8,128)(2,1)S(1)}, u32[]{:S(2)}, u32[]{:S(2)}) collective-permute-start(bf16[200,128]{1,0:T(8,128)(2,1)S(1)} %add_convert_fusion.refs_0_), channel_id=1, source_target_pairs={{0,2},{1,3},{2,0},{3,1},{4,6},{5,7},{6,4},{7,5},{8,10},{9,11},{10,... | collective-permute-start | bytes 153608 | tf_op jit(solution)/shard_map/ppermute | solution.py:146
  54.7 5.2 %collective-permute-start.18 = (bf16[200,128]{1,0:T(8,128)(2,1)S(1)}, bf16[200,128]{1,0:T(8,128)(2,1)S(1)}, u32[]{:S(2)}, u32[]{:S(2)}) collective-permute-start(bf16[200,128]{1,0:T(8,128)(2,1)S(1)} %collective-permute-done.17.refs_2_), channel_id=1, source_target_pairs={{0,2},{1,3},{2,0},{3,1},{4,6},{5,7},{6,4},{7,5},{8,10},{9,11},{10,... | collective-permute-start | bytes 153608 | tf_op jit(solution)/shard_map/ppermute | solution.py:146
  56.4 4.1 %collective-permute-start.20 = (bf16[200,128]{1,0:T(8,128)(2,1)S(1)}, bf16[200,128]{1,0:T(8,128)(2,1)S(1)}, u32[]{:S(2)}, u32[]{:S(2)}) collective-permute-start(bf16[200,128]{1,0:T(8,128)(2,1)S(1)} %collective-permute-done.19.refs_4_), channel_id=1, source_target_pairs={{0,2},{1,3},{2,0},{3,1},{4,6},{5,7},{6,4},{7,5},{8,10},{9,11},{10,... | collective-permute-start | bytes 153608 | tf_op jit(solution)/shard_map/ppermute | solution.py:146
  57.4 4.1 %collective-permute-start.22 = (bf16[200,128]{1,0:T(8,128)(2,1)S(1)}, bf16[200,128]{1,0:T(8,128)(2,1)S(1)}, u32[]{:S(2)}, u32[]{:S(2)}) collective-permute-start(bf16[200,128]{1,0:T(8,128)(2,1)S(1)} %collective-permute-done.21.refs_6_), channel_id=1, source_target_pairs={{0,2},{1,3},{2,0},{3,1},{4,6},{5,7},{6,4},{7,5},{8,10},{9,11},{10,... | collective-permute-start | bytes 153608 | tf_op jit(solution)/shard_map/ppermute | solution.py:146
  63.4 1.8 %collective-permute-start.23 = (f32[208,512]{1,0:T(8,128)S(1)}, f32[208,512]{1,0:T(8,128)S(1)}, u32[]{:S(2)}, u32[]{:S(2)}) collective-permute-start(f32[208,512]{1,0:T(8,128)S(1)} %gram_and_cross.1.mine_ref), channel_id=1, source_target_pairs={{0,1},{1,0},{2,3},{3,2},{4,5},{5,4},{6,7},{7,6},{8,9},{9,8},{10,11... | collective-permute-start | bytes 1277960 | tf_op jit(solution)/shard_map/ppermute | solution.py:146

commit v6 on v5

--- a/solution.py
+++ b/solution.py
@@ -457,14 +457,14 @@
         return carry[0] > 2.0**-24
 
     def double(carry):
-        power = state_ref[:, 0:256]
+        power = state_ref[0:members, 0:256]
         size = jnp.sum(power * power)
         moved = jnp.dot(
             power, state_ref[...], precision=lax.Precision.HIGHEST,
             preferred_element_type=jnp.float32,
         )
-        state_ref[:, 0:256] = moved[:, 0:256]
-        state_ref[:, 256:512] = state_ref[:, 256:512] + moved[:, 256:512]
+        state_ref[0:members, 0:256] = moved[:, 0:256]
+        state_ref[0:members, 256:512] = state_ref[0:members, 256:512] + moved[:, 256:512]
         return (size,)
 
     lax.while_loop(more, double, (jnp.float32(1.0),))
@@ -548,12 +548,13 @@
     near_z = swap(noise, 4)
     share, near_z = lax.optimization_barrier((share, near_z))
     near_noise = jnp.concatenate([noise, near_z])
+    got = [swap(share[i], 4 * i) for i in range(1, devices // 4)]
+    got[0], near_noise = lax.optimization_barrier((got[0], near_noise))
     far_noise = swap(near_noise, 2)
-    got = [swap(share[i], 4 * i) for i in range(1, devices // 4)]
     predicted = (share[0] + got[0] + got[1] + got[2]).astype(jnp.bfloat16)
-    predicted, far_noise = lax.optimization_barrier((predicted, far_noise))
 
     near = [predicted] + [swap(predicted, 4 * i) for i in range(1, devices // 4)]
+    near[3], far_noise = lax.optimization_barrier((near[3], far_noise))
     gathered = []
     for value in near:
         gathered += [value, swap(value, 2)]

time: 73.6 us -> 73.2 us (level)
  waiting for transfers between devices: 21.3 us -> 19.5 us
  starting transfers between devices: 27.6 us -> 28.8 us
    ppermute x24, waiting for transfers between devices: 21.3 us -> 19.5 us  [swap(): return lax.ppermute(value, 'map', pairs)]
    ppermute x24, starting transfers between devices: 27.6 us -> 28.8 us  [swap(): return lax.ppermute(value, 'map', pairs)]
  transfers between devices with their start and end apart: 24 -> 24, of which waited for: 11 -> 9; matrix products, arithmetic and copies ran while one was open for 2% -> 2% of each run, Pallas kernels for 7% -> 7%
where the time goes in v6:
time: 73.2 us; the launch traced here: 73 us
  starting transfers between devices  28.8 us (39%)
  waiting for transfers between devices  19.5 us (27%)
  Pallas kernels  19.4 us (27%)
  local copies, waits for them, and re-layouts  2.73 us (4%)
  other arithmetic  1.51 us (2%)
  between operations  1.01 us (1%)
    ppermute x24, starting transfers between devices, swap(): return lax.ppermute(value, 'map', pairs)  28.8 us
    ppermute x24, waiting for transfers between devices, swap(): return lax.ppermute(value, 'map', pairs)  19.5 us
    pallas_call x1, Pallas kernels, update(): pl.pallas_call(update_kernel, in_specs=[VMEM, VMEM, HBM], out_specs=[HBM,...  8.18 us
    pallas_call x1, Pallas kernels, shares(): pl.pallas_call(shares_kernel, in_specs=[VMEM] * 7, out_specs=[VMEM] * 4,...  4.26 us
    pallas_call x1, Pallas kernels, by_row(): pl.pallas_call(by_row_kernel, in_specs=[HBM], out_specs=VMEM, out_shape=j...  3.65 us
    unnamed x8, local copies, waits for them, and re-layouts  2.21 us
    pallas_call x1, Pallas kernels, gram(): pl.pallas_call(gram_kernel, in_specs=[VMEM] * (2 + len(predicted)), out_s...  1.89 us
  transfers between devices with their start and end apart: 24, of which 9 were waited for; matrix products, arithmetic and copies ran while one was open for 2% of the time, Pallas kernels for 7%

profile of v6, /device:TPU:0, one launch (start us, length us, event | category | flops | bytes accessed | tf_op | source)
XLA Modules:
  0.0 73.0 jit_solution(6409675355900637935)
XLA Ops:
  0.6 0.7 %pad_add_fusion.2 = s32[32]{0:T(128)S(1)} fusion(s32[16]{0:T(128)} %bitcast.31, s32[16]{0:T(128)} %param.9), kind=kLoop, calls=%fused_computation.19 | loop fusion | flops 32 | bytes 256 | tf_op jit(solution)/shard_map/concatenate | solution.py:528
  1.8 2.5 %collective-permute-start.2 = (s32[32]{0:T(128)S(1)}, s32[32]{0:T(128)S(1)}, u32[]{:S(2)}, u32[]{:S(2)}) collective-permute-start(s32[32]{0:T(128)S(1)} %pad_add_fusion.2), channel_id=1, source_target_pairs={{0,2},{1,3},{2,0},{3,1},{4,6},{5,7},{6,4},{7,5},{8,10},{9,11},{10,... | collective-permute-start | bytes 392 | tf_op jit(solution)/shard_map/ppermute | solution.py:146
  4.5 0.9 %copy-done.1 = bf16[256,200]{0,1:T(8,128)(2,1)S(1)} copy-done((bf16[256,200]{0,1:T(8,128)(2,1)S(1)}, bf16[256,200]{0,1:T(8,128)(2,1)}, u32[]{:S(2)}) %copy-start.1) | copy-done | bytes 102424
  6.0 0.7 copy-done.3
  7.4 0.8 %collective-permute-done = bf16[208,128]{1,0:T(8,128)(2,1)S(1)} collective-permute-done((bf16[208,128]{1,0:T(8,128)(2,1)S(1)}, bf16[208,128]{1,0:T(8,128)(2,1)S(1)}, u32[]{:S(2)}, u32[]{:S(2)}) %collective-permute-start) | collective-permute-done | bytes 53280 | tf_op jit(solution)/shard_map/ppermute | solution.py:146
  8.2 2.9 %collective-permute-start.7 = (bf16[2,208,128]{2,1,0:T(8,128)(2,1)S(1)}, bf16[2,208,128]{2,1,0:T(8,128)(2,1)S(1)}, u32[]{:S(2)}, u32[]{:S(2)}) collective-permute-start(bf16[2,208,128]{2,1,0:T(8,128)(2,1)S(1)} %pad_maximum_fusion.2), channel_id=1, source_target_pairs={{0,8},{1,9},{2,10},{3,11},{4,12},{5,13},{6,14},{7,15},{8,0},{9,1},... | collective-permute-start | bytes 319496 | tf_op jit(solution)/shard_map/ppermute | solution.py:146
  11.1 1.6 %collective-permute-start.4 = (s32[4,32]{1,0:T(4,128)S(1)}, s32[4,32]{1,0:T(4,128)S(1)}, u32[]{:S(2)}, u32[]{:S(2)}) collective-permute-start(s32[4,32]{1,0:T(4,128)S(1)} %pad_add_fusion.1.list0_ref), channel_id=1, source_target_pairs={{0,4},{1,5},{2,6},{3,7},{4,0},{5,1},{6,2},{7,3},{8,12},{9,13},{10,... | collective-permute-start | bytes 1544 | tf_op jit(solution)/shard_map/ppermute | solution.py:146
  13.0 2.5 %collective-permute-start.6 = (s32[4,32]{1,0:T(4,128)S(1)}, s32[4,32]{1,0:T(4,128)S(1)}, u32[]{:S(2)}, u32[]{:S(2)}) collective-permute-start(s32[4,32]{1,0:T(4,128)S(1)} %pad_add_fusion.1.list0_ref), channel_id=1, source_target_pairs={{0,12},{1,13},{2,14},{3,15},{4,8},{5,9},{6,10},{7,11},{8,4},{9,5},... | collective-permute-start | bytes 1544 | tf_op jit(solution)/shard_map/ppermute | solution.py:146
  15.5 3.7 %maps_by_row.1.maps_ref = bf16[32,200,512]{2,1,0:T(8,128)(2,1)S(1)} custom-call(bf16[200,32,512]{2,1,0:T(8,128)(2,1)} %maps_ref), custom_call_target="tpu_custom_call" | custom-call | bytes 13107200 | tf_op jit(solution)/shard_map/maps_by_row/pallas_call | solution.py:171
  19.2 4.3 %coefficient_shares.1 = (f32[4,200,128]{2,1,0:T(8,128)S(1)}, f32[4,200,128]{2,1,0:T(8,128)S(1)}, f32[4,200,128]{2,1,0:T(8,128)S(1)}, f32[4,200,128]{2,1,0:T(8,128)S(1)}) custom-call(s32[4,32]{1,0:T(4,128)S(1)} %pad_add_fusion.1.list0_ref, s32[4,32]{1,0:T(4,128)S(1)} %collective-permute-done.4.list1_ref, s32[4,32]{1,0:T(4,128)S(1)} %collective-permute-done.5.list2_ref, ...), custom_call_target="tpu_custom_call" | custom-call | flops 1677721600 | bytes 6553600 | tf_op jit(solution)/shard_map/coefficient_shares/pallas_call | solution.py:258
  24.2 1.1 %collective-permute-done.9 = f32[4,200,128]{2,1,0:T(8,128)S(1)} collective-permute-done((f32[4,200,128]{2,1,0:T(8,128)S(1)}, f32[4,200,128]{2,1,0:T(8,128)S(1)}, u32[]{:S(2)}, u32[]{:S(2)}) %collective-permute-start.9) | collective-permute-done | bytes 409632 | tf_op jit(solution)/shard_map/ppermute | solution.py:146
  25.3 1.6 %collective-permute-start.10 = (f32[4,200,128]{2,1,0:T(8,128)S(1)}, f32[4,200,128]{2,1,0:T(8,128)S(1)}, u32[]{:S(2)}, u32[]{:S(2)}) collective-permute-start(f32[4,200,128]{2,1,0:T(8,128)S(1)} %add.125), channel_id=1, source_target_pairs={{0,2},{1,3},{2,0},{3,1},{4,6},{5,7},{6,4},{7,5},{8,10},{9,11},{10,... | collective-permute-start | bytes 1228808 | tf_op jit(solution)/shard_map/ppermute | solution.py:146
  26.9 0.7 %collective-permute-start.11 = (bf16[2,2,208,128]{3,2,1,0:T(8,128)(2,1)S(1)}, bf16[2,2,208,128]{3,2,1,0:T(8,128)(2,1)S(1)}, u32[]{:S(2)}, u32[]{:S(2)}) collective-permute-start(bf16[2,2,208,128]{3,2,1,0:T(8,128)(2,1)S(1)} %pad_maximum_fusion.1), channel_id=1, source_target_pairs={{0,4},{1,5},{2,6},{3,7},{4,0},{5,1},{6,2},{7,3},{8,12},{9,13},{10,... | collective-permute-start | bytes 638984 | tf_op jit(solution)/shard_map/ppermute | solution.py:146
  28.1 8.8 %collective-permute-done.10 = f32[4,200,128]{2,1,0:T(8,128)S(1)} collective-permute-done((f32[4,200,128]{2,1,0:T(8,128)S(1)}, f32[4,200,128]{2,1,0:T(8,128)S(1)}, u32[]{:S(2)}, u32[]{:S(2)}) %collective-permute-start.10) | collective-permute-done | bytes 409632 | tf_op jit(solution)/shard_map/ppermute | solution.py:146
  37.0 0.7 %collective-permute-start.12 = (f32[200,128]{1,0:T(8,128)S(1)}, f32[200,128]{1,0:T(8,128)S(1)}, u32[]{:S(2)}, u32[]{:S(2)}) collective-permute-start(f32[200,128]{1,0:T(8,128)S(1)} %get-tuple-element.43), channel_id=1, source_target_pairs={{0,4},{1,5},{2,6},{3,7},{4,0},{5,1},{6,2},{7,3},{8,12},{9,13},{10,... | collective-permute-start | bytes 307208 | tf_op jit(solution)/shard_map/ppermute | solution.py:146
  37.7 1.6 %collective-permute-start.13 = (f32[200,128]{1,0:T(8,128)S(1)}, f32[200,128]{1,0:T(8,128)S(1)}, u32[]{:S(2)}, u32[]{:S(2)}) collective-permute-start(f32[200,128]{1,0:T(8,128)S(1)} %get-tuple-element.48), channel_id=1, source_target_pairs={{0,8},{1,9},{2,10},{3,11},{4,12},{5,13},{6,14},{7,15},{8,0},{9,1},... | collective-permute-start | bytes 307208 | tf_op jit(solution)/shard_map/ppermute | solution.py:146
  39.3 2.2 %collective-permute-start.14 = (f32[200,128]{1,0:T(8,128)S(1)}, f32[200,128]{1,0:T(8,128)S(1)}, u32[]{:S(2)}, u32[]{:S(2)}) collective-permute-start(f32[200,128]{1,0:T(8,128)S(1)} %get-tuple-element.49), channel_id=1, source_target_pairs={{0,12},{1,13},{2,14},{3,15},{4,8},{5,9},{6,10},{7,11},{8,4},{9,5},... | collective-permute-start | bytes 307208 | tf_op jit(solution)/shard_map/ppermute | solution.py:146
  41.5 1.0 %collective-permute-done.12 = f32[200,128]{1,0:T(8,128)S(1)} collective-permute-done((f32[200,128]{1,0:T(8,128)S(1)}, f32[200,128]{1,0:T(8,128)S(1)}, u32[]{:S(2)}, u32[]{:S(2)}) %collective-permute-start.12) | collective-permute-done | bytes 102432 | tf_op jit(solution)/shard_map/ppermute | solution.py:146
  42.4 1.5 %collective-permute-start.16 = (bf16[4,2,208,128]{3,2,1,0:T(8,128)(2,1)S(1)}, bf16[4,2,208,128]{3,2,1,0:T(8,128)(2,1)S(1)}, u32[]{:S(2)}, u32[]{:S(2)}) collective-permute-start(bf16[4,2,208,128]{3,2,1,0:T(8,128)(2,1)S(1)} %pad_maximum_fusion.near_ref), channel_id=1, source_target_pairs={{0,2},{1,3},{2,0},{3,1},{4,6},{5,7},{6,4},{7,5},{8,10},{9,11},{10,... | collective-permute-start | bytes 1277960 | tf_op jit(solution)/shard_map/ppermute | solution.py:146
  43.9 4.0 %collective-permute-done.13 = f32[200,128]{1,0:T(8,128)S(1)} collective-permute-done((f32[200,128]{1,0:T(8,128)S(1)}, f32[200,128]{1,0:T(8,128)S(1)}, u32[]{:S(2)}, u32[]{:S(2)}) %collective-permute-start.13) | collective-permute-done | bytes 102432 | tf_op jit(solution)/shard_map/ppermute | solution.py:146
  47.9 1.5 %collective-permute-start.15 = (bf16[200,128]{1,0:T(8,128)(2,1)S(1)}, bf16[200,128]{1,0:T(8,128)(2,1)S(1)}, u32[]{:S(2)}, u32[]{:S(2)}) collective-permute-start(bf16[200,128]{1,0:T(8,128)(2,1)S(1)} %add_convert_fusion.refs_0_), channel_id=1, source_target_pairs={{0,12},{1,13},{2,14},{3,15},{4,8},{5,9},{6,10},{7,11},{8,4},{9,5},... | collective-permute-start | bytes 153608 | tf_op jit(solution)/shard_map/ppermute | solution.py:146
  49.4 0.9 %collective-permute-start.18 = (bf16[200,128]{1,0:T(8,128)(2,1)S(1)}, bf16[200,128]{1,0:T(8,128)(2,1)S(1)}, u32[]{:S(2)}, u32[]{:S(2)}) collective-permute-start(bf16[200,128]{1,0:T(8,128)(2,1)S(1)} %add_convert_fusion.refs_0_), channel_id=1, source_target_pairs={{0,4},{1,5},{2,6},{3,7},{4,0},{5,1},{6,2},{7,3},{8,12},{9,13},{10,... | collective-permute-start | bytes 153608 | tf_op jit(solution)/shard_map/ppermute | solution.py:146
  50.3 2.1 %collective-permute-start.20 = (bf16[200,128]{1,0:T(8,128)(2,1)S(1)}, bf16[200,128]{1,0:T(8,128)(2,1)S(1)}, u32[]{:S(2)}, u32[]{:S(2)}) collective-permute-start(bf16[200,128]{1,0:T(8,128)(2,1)S(1)} %add_convert_fusion.refs_0_), channel_id=1, source_target_pairs={{0,8},{1,9},{2,10},{3,11},{4,12},{5,13},{6,14},{7,15},{8,0},{9,1},... | collective-permute-start | bytes 153608 | tf_op jit(solution)/shard_map/ppermute | solution.py:146
  52.7 1.6 %collective-permute-start.17 = (bf16[200,128]{1,0:T(8,128)(2,1)S(1)}, bf16[200,128]{1,0:T(8,128)(2,1)S(1)}, u32[]{:S(2)}, u32[]{:S(2)}) collective-permute-start(bf16[200,128]{1,0:T(8,128)(2,1)S(1)} %add_convert_fusion.refs_0_), channel_id=1, source_target_pairs={{0,2},{1,3},{2,0},{3,1},{4,6},{5,7},{6,4},{7,5},{8,10},{9,11},{10,... | collective-permute-start | bytes 153608 | tf_op jit(solution)/shard_map/ppermute | solution.py:146
  54.3 1.3 %collective-permute-start.19 = (bf16[200,128]{1,0:T(8,128)(2,1)S(1)}, bf16[200,128]{1,0:T(8,128)(2,1)S(1)}, u32[]{:S(2)}, u32[]{:S(2)}) collective-permute-start(bf16[200,128]{1,0:T(8,128)(2,1)S(1)} %collective-permute-done.18.refs_2_), channel_id=1, source_target_pairs={{0,2},{1,3},{2,0},{3,1},{4,6},{5,7},{6,4},{7,5},{8,10},{9,11},{10,... | collective-permute-start | bytes 153608 | tf_op jit(solution)/shard_map/ppermute | solution.py:146
  55.6 1.2 %collective-permute-start.21 = (bf16[200,128]{1,0:T(8,128)(2,1)S(1)}, bf16[200,128]{1,0:T(8,128)(2,1)S(1)}, u32[]{:S(2)}, u32[]{:S(2)}) collective-permute-start(bf16[200,128]{1,0:T(8,128)(2,1)S(1)} %collective-permute-done.20.refs_4_), channel_id=1, source_target_pairs={{0,2},{1,3},{2,0},{3,1},{4,6},{5,7},{6,4},{7,5},{8,10},{9,11},{10,... | collective-permute-start | bytes 153608 | tf_op jit(solution)/shard_map/ppermute | solution.py:146
  56.8 0.9 %collective-permute-start.22 = (bf16[200,128]{1,0:T(8,128)(2,1)S(1)}, bf16[200,128]{1,0:T(8,128)(2,1)S(1)}, u32[]{:S(2)}, u32[]{:S(2)}) collective-permute-start(bf16[200,128]{1,0:T(8,128)(2,1)S(1)} %collective-permute-done.15.refs_6_), channel_id=1, source_target_pairs={{0,2},{1,3},{2,0},{3,1},{4,6},{5,7},{6,4},{7,5},{8,10},{9,11},{10,... | collective-permute-start | bytes 153608 | tf_op jit(solution)/shard_map/ppermute | solution.py:146
  57.9 1.2 %select_noise.1.noise_ref = f32[8,208,128]{2,1,0:T(8,128)S(1)} custom-call(s32[128]{0:T(128)S(1)} %reshape.83.starts_ref, bf16[4,2,208,128]{3,2,1,0:T(8,128)(2,1)S(1)} %pad_maximum_fusion.near_ref, bf16[4,2,208,128]{3,2,1,0:T(8,128)(2,1)S(1)} %collective-permute-done.16.far_ref), custom_call_target="tpu_custom_call" | custom-call | tf_op jit(solution)/shard_map/select_noise/pallas_call | solution.py:342
  59.8 1.2 %collective-permute-done.22.refs_7_ = bf16[200,128]{1,0:T(8,128)(2,1)S(1)} collective-permute-done((bf16[200,128]{1,0:T(8,128)(2,1)S(1)}, bf16[200,128]{1,0:T(8,128)(2,1)S(1)}, u32[]{:S(2)}, u32[]{:S(2)}) %collective-permute-start.22) | collective-permute-done | bytes 51232 | tf_op jit(solution)/shard_map/ppermute | solution.py:146
  60.9 1.9 %gram_and_cross.1.mine_ref = f32[208,512]{1,0:T(8,128)S(1)} custom-call(s32[8,128,1]{2,1,0:T(8,128)S(1)} %broadcast_add_fusion.target_ref, f32[8,208,128]{2,1,0:T(8,128)S(1)} %select_noise.1.noise_ref, bf16[200,128]{1,0:T(8,128)(2,1)S(1)} %add_convert_fusion.refs_0_, bf16[200,128]{1,0:T(8,128)(2,1)S(1)} %collective-permute-done.17.refs_1_, ...), custom_call_target="tpu_custom_call" | custom-call | tf_op jit(solution)/shard_map/gram_and_cross/pallas_call | solution.py:411
  62.9 1.8 %collective-permute-done.23.other_ref = f32[208,512]{1,0:T(8,128)S(1)} collective-permute-done((f32[208,512]{1,0:T(8,128)S(1)}, f32[208,512]{1,0:T(8,128)S(1)}, u32[]{:S(2)}, u32[]{:S(2)}) %collective-permute-start.23) | collective-permute-done | bytes 426016 | tf_op jit(solution)/shard_map/ppermute | solution.py:146
  64.6 8.2 %solve_and_update.1 = (bf16[200,12288]{1,0:T(8,128)(2,1)}, f32[200,200]{1,0:T(8,128)}, f32[1,256]{1,0:T(1,128)}) custom-call(f32[208,512]{1,0:T(8,128)S(1)} %gram_and_cross.1.mine_ref, f32[208,512]{1,0:T(8,128)S(1)} %collective-permute-done.23.other_ref, bf16[200,12288]{1,0:T(8,128)(2,1)} %slab_ref.1), custom_call_target="tpu_custom_call" | custom-call | tf_op jit(solution)/shard_map/solve_and_update/pallas_call | solution.py:497
  (51 shorter events, 4.8 us)
Async XLA Ops:
  1.4 5.7 %collective-permute-start.1 = (s32[32]{0:T(128)S(1)}, s32[32]{0:T(128)S(1)}, u32[]{:S(2)}, u32[]{:S(2)}) collective-permute-start(s32[32]{0:T(128)S(1)} %pad_add_fusion.2), channel_id=1, source_target_pairs={{0,1},{1,0},{2,3},{3,2},{4,5},{5,4},{6,7},{7,6},{8,9},{9,8},{10,11... | collective-permute-start | bytes 392 | tf_op jit(solution)/shard_map/ppermute | solution.py:146
  1.8 5.2 %collective-permute-start.2 = (s32[32]{0:T(128)S(1)}, s32[32]{0:T(128)S(1)}, u32[]{:S(2)}, u32[]{:S(2)}) collective-permute-start(s32[32]{0:T(128)S(1)} %pad_add_fusion.2), channel_id=1, source_target_pairs={{0,2},{1,3},{2,0},{3,1},{4,6},{5,7},{6,4},{7,5},{8,10},{9,11},{10,... | collective-permute-start | bytes 392 | tf_op jit(solution)/shard_map/ppermute | solution.py:146
  4.4 3.0 %collective-permute-start.3 = (s32[32]{0:T(128)S(1)}, s32[32]{0:T(128)S(1)}, u32[]{:S(2)}, u32[]{:S(2)}) collective-permute-start(s32[32]{0:T(128)S(1)} %pad_add_fusion.2), channel_id=1, source_target_pairs={{0,3},{1,2},{2,1},{3,0},{4,7},{5,6},{6,5},{7,4},{8,11},{9,10},{10,... | collective-permute-start | bytes 392 | tf_op jit(solution)/shard_map/ppermute | solution.py:146
  4.5 0.9 %copy-start.1 = (bf16[256,200]{0,1:T(8,128)(2,1)S(1)}, bf16[256,200]{0,1:T(8,128)(2,1)}, u32[]{:S(2)}) copy-start(bf16[256,200]{0,1:T(8,128)(2,1)} %param.13) | copy-start | bytes 307204
  5.4 0.7 copy-start.2
  6.0 0.7 copy-start.3
  6.9 1.3 %collective-permute-start = (bf16[208,128]{1,0:T(8,128)(2,1)S(1)}, bf16[208,128]{1,0:T(8,128)(2,1)S(1)}, u32[]{:S(2)}, u32[]{:S(2)}) collective-permute-start(bf16[208,128]{1,0:T(8,128)(2,1)S(1)} %get-tuple-element.30), channel_id=1, source_target_pairs={{0,1},{1,0},{2,3},{3,2},{4,5},{5,4},{6,7},{7,6},{8,9},{9,8},{10,11... | collective-permute-start | bytes 159752 | tf_op jit(solution)/shard_map/ppermute | solution.py:146
  8.2 11.0 %copy-start = (bf16[512,512]{1,0:T(8,128)(2,1)S(1)}, bf16[512,512]{1,0:T(8,128)(2,1)}, u32[]{:S(2)}) copy-start(bf16[512,512]{1,0:T(8,128)(2,1)} %constant.10.clone.table_w_ref.table_h_ref) | copy-start | bytes 1572868
  8.2 11.0 %collective-permute-start.7 = (bf16[2,208,128]{2,1,0:T(8,128)(2,1)S(1)}, bf16[2,208,128]{2,1,0:T(8,128)(2,1)S(1)}, u32[]{:S(2)}, u32[]{:S(2)}) collective-permute-start(bf16[2,208,128]{2,1,0:T(8,128)(2,1)S(1)} %pad_maximum_fusion.2), channel_id=1, source_target_pairs={{0,8},{1,9},{2,10},{3,11},{4,12},{5,13},{6,14},{7,15},{8,0},{9,1},... | collective-permute-start | bytes 319496 | tf_op jit(solution)/shard_map/ppermute | solution.py:146
  11.1 8.1 %collective-permute-start.4 = (s32[4,32]{1,0:T(4,128)S(1)}, s32[4,32]{1,0:T(4,128)S(1)}, u32[]{:S(2)}, u32[]{:S(2)}) collective-permute-start(s32[4,32]{1,0:T(4,128)S(1)} %pad_add_fusion.1.list0_ref), channel_id=1, source_target_pairs={{0,4},{1,5},{2,6},{3,7},{4,0},{5,1},{6,2},{7,3},{8,12},{9,13},{10,... | collective-permute-start | bytes 1544 | tf_op jit(solution)/shard_map/ppermute | solution.py:146
  12.7 6.5 %collective-permute-start.5 = (s32[4,32]{1,0:T(4,128)S(1)}, s32[4,32]{1,0:T(4,128)S(1)}, u32[]{:S(2)}, u32[]{:S(2)}) collective-permute-start(s32[4,32]{1,0:T(4,128)S(1)} %pad_add_fusion.1.list0_ref), channel_id=1, source_target_pairs={{0,8},{1,9},{2,10},{3,11},{4,12},{5,13},{6,14},{7,15},{8,0},{9,1},... | collective-permute-start | bytes 1544 | tf_op jit(solution)/shard_map/ppermute | solution.py:146
  13.0 6.2 %collective-permute-start.6 = (s32[4,32]{1,0:T(4,128)S(1)}, s32[4,32]{1,0:T(4,128)S(1)}, u32[]{:S(2)}, u32[]{:S(2)}) collective-permute-start(s32[4,32]{1,0:T(4,128)S(1)} %pad_add_fusion.1.list0_ref), channel_id=1, source_target_pairs={{0,12},{1,13},{2,14},{3,15},{4,8},{5,9},{6,10},{7,11},{8,4},{9,5},... | collective-permute-start | bytes 1544 | tf_op jit(solution)/shard_map/ppermute | solution.py:146
  23.5 1.8 %collective-permute-start.9 = (f32[4,200,128]{2,1,0:T(8,128)S(1)}, f32[4,200,128]{2,1,0:T(8,128)S(1)}, u32[]{:S(2)}, u32[]{:S(2)}) collective-permute-start(f32[4,200,128]{2,1,0:T(8,128)S(1)} %get-tuple-element.41), channel_id=1, source_target_pairs={{0,1},{1,0},{2,3},{3,2},{4,5},{5,4},{6,7},{7,6},{8,9},{9,8},{10,11... | collective-permute-start | bytes 1228808 | tf_op jit(solution)/shard_map/ppermute | solution.py:146
  23.6 4.4 %collective-permute-start.8 = (f32[4,200,128]{2,1,0:T(8,128)S(1)}, f32[4,200,128]{2,1,0:T(8,128)S(1)}, u32[]{:S(2)}, u32[]{:S(2)}) collective-permute-start(f32[4,200,128]{2,1,0:T(8,128)S(1)} %get-tuple-element.39), channel_id=1, source_target_pairs={{0,1},{1,0},{2,3},{3,2},{4,5},{5,4},{6,7},{7,6},{8,9},{9,8},{10,11... | collective-permute-start | bytes 1228808 | tf_op jit(solution)/shard_map/ppermute | solution.py:146
  25.3 11.6 %collective-permute-start.10 = (f32[4,200,128]{2,1,0:T(8,128)S(1)}, f32[4,200,128]{2,1,0:T(8,128)S(1)}, u32[]{:S(2)}, u32[]{:S(2)}) collective-permute-start(f32[4,200,128]{2,1,0:T(8,128)S(1)} %add.125), channel_id=1, source_target_pairs={{0,2},{1,3},{2,0},{3,1},{4,6},{5,7},{6,4},{7,5},{8,10},{9,11},{10,... | collective-permute-start | bytes 1228808 | tf_op jit(solution)/shard_map/ppermute | solution.py:146
  26.9 10.1 %collective-permute-start.11 = (bf16[2,2,208,128]{3,2,1,0:T(8,128)(2,1)S(1)}, bf16[2,2,208,128]{3,2,1,0:T(8,128)(2,1)S(1)}, u32[]{:S(2)}, u32[]{:S(2)}) collective-permute-start(bf16[2,2,208,128]{3,2,1,0:T(8,128)(2,1)S(1)} %pad_maximum_fusion.1), channel_id=1, source_target_pairs={{0,4},{1,5},{2,6},{3,7},{4,0},{5,1},{6,2},{7,3},{8,12},{9,13},{10,... | collective-permute-start | bytes 638984 | tf_op jit(solution)/shard_map/ppermute | solution.py:146
  37.0 5.5 %collective-permute-start.12 = (f32[200,128]{1,0:T(8,128)S(1)}, f32[200,128]{1,0:T(8,128)S(1)}, u32[]{:S(2)}, u32[]{:S(2)}) collective-permute-start(f32[200,128]{1,0:T(8,128)S(1)} %get-tuple-element.43), channel_id=1, source_target_pairs={{0,4},{1,5},{2,6},{3,7},{4,0},{5,1},{6,2},{7,3},{8,12},{9,13},{10,... | collective-permute-start | bytes 307208 | tf_op jit(solution)/shard_map/ppermute | solution.py:146
  37.7 10.2 %collective-permute-start.13 = (f32[200,128]{1,0:T(8,128)S(1)}, f32[200,128]{1,0:T(8,128)S(1)}, u32[]{:S(2)}, u32[]{:S(2)}) collective-permute-start(f32[200,128]{1,0:T(8,128)S(1)} %get-tuple-element.48), channel_id=1, source_target_pairs={{0,8},{1,9},{2,10},{3,11},{4,12},{5,13},{6,14},{7,15},{8,0},{9,1},... | collective-permute-start | bytes 307208 | tf_op jit(solution)/shard_map/ppermute | solution.py:146
  39.3 8.6 %collective-permute-start.14 = (f32[200,128]{1,0:T(8,128)S(1)}, f32[200,128]{1,0:T(8,128)S(1)}, u32[]{:S(2)}, u32[]{:S(2)}) collective-permute-start(f32[200,128]{1,0:T(8,128)S(1)} %get-tuple-element.49), channel_id=1, source_target_pairs={{0,12},{1,13},{2,14},{3,15},{4,8},{5,9},{6,10},{7,11},{8,4},{9,5},... | collective-permute-start | bytes 307208 | tf_op jit(solution)/shard_map/ppermute | solution.py:146
  42.4 14.4 %collective-permute-start.16 = (bf16[4,2,208,128]{3,2,1,0:T(8,128)(2,1)S(1)}, bf16[4,2,208,128]{3,2,1,0:T(8,128)(2,1)S(1)}, u32[]{:S(2)}, u32[]{:S(2)}) collective-permute-start(bf16[4,2,208,128]{3,2,1,0:T(8,128)(2,1)S(1)} %pad_maximum_fusion.near_ref), channel_id=1, source_target_pairs={{0,2},{1,3},{2,0},{3,1},{4,6},{5,7},{6,4},{7,5},{8,10},{9,11},{10,... | collective-permute-start | bytes 1277960 | tf_op jit(solution)/shard_map/ppermute | solution.py:146
  47.9 8.9 %collective-permute-start.15 = (bf16[200,128]{1,0:T(8,128)(2,1)S(1)}, bf16[200,128]{1,0:T(8,128)(2,1)S(1)}, u32[]{:S(2)}, u32[]{:S(2)}) collective-permute-start(bf16[200,128]{1,0:T(8,128)(2,1)S(1)} %add_convert_fusion.refs_0_), channel_id=1, source_target_pairs={{0,12},{1,13},{2,14},{3,15},{4,8},{5,9},{6,10},{7,11},{8,4},{9,5},... | collective-permute-start | bytes 153608 | tf_op jit(solution)/shard_map/ppermute | solution.py:146
  49.4 4.9 %collective-permute-start.18 = (bf16[200,128]{1,0:T(8,128)(2,1)S(1)}, bf16[200,128]{1,0:T(8,128)(2,1)S(1)}, u32[]{:S(2)}, u32[]{:S(2)}) collective-permute-start(bf16[200,128]{1,0:T(8,128)(2,1)S(1)} %add_convert_fusion.refs_0_), channel_id=1, source_target_pairs={{0,4},{1,5},{2,6},{3,7},{4,0},{5,1},{6,2},{7,3},{8,12},{9,13},{10,... | collective-permute-start | bytes 153608 | tf_op jit(solution)/shard_map/ppermute | solution.py:146
  50.3 5.3 %collective-permute-start.20 = (bf16[200,128]{1,0:T(8,128)(2,1)S(1)}, bf16[200,128]{1,0:T(8,128)(2,1)S(1)}, u32[]{:S(2)}, u32[]{:S(2)}) collective-permute-start(bf16[200,128]{1,0:T(8,128)(2,1)S(1)} %add_convert_fusion.refs_0_), channel_id=1, source_target_pairs={{0,8},{1,9},{2,10},{3,11},{4,12},{5,13},{6,14},{7,15},{8,0},{9,1},... | collective-permute-start | bytes 153608 | tf_op jit(solution)/shard_map/ppermute | solution.py:146
  52.7 6.4 %collective-permute-start.17 = (bf16[200,128]{1,0:T(8,128)(2,1)S(1)}, bf16[200,128]{1,0:T(8,128)(2,1)S(1)}, u32[]{:S(2)}, u32[]{:S(2)}) collective-permute-start(bf16[200,128]{1,0:T(8,128)(2,1)S(1)} %add_convert_fusion.refs_0_), channel_id=1, source_target_pairs={{0,2},{1,3},{2,0},{3,1},{4,6},{5,7},{6,4},{7,5},{8,10},{9,11},{10,... | collective-permute-start | bytes 153608 | tf_op jit(solution)/shard_map/ppermute | solution.py:146
  54.3 4.8 %collective-permute-start.19 = (bf16[200,128]{1,0:T(8,128)(2,1)S(1)}, bf16[200,128]{1,0:T(8,128)(2,1)S(1)}, u32[]{:S(2)}, u32[]{:S(2)}) collective-permute-start(bf16[200,128]{1,0:T(8,128)(2,1)S(1)} %collective-permute-done.18.refs_2_), channel_id=1, source_target_pairs={{0,2},{1,3},{2,0},{3,1},{4,6},{5,7},{6,4},{7,5},{8,10},{9,11},{10,... | collective-permute-start | bytes 153608 | tf_op jit(solution)/shard_map/ppermute | solution.py:146
  55.6 4.1 %collective-permute-start.21 = (bf16[200,128]{1,0:T(8,128)(2,1)S(1)}, bf16[200,128]{1,0:T(8,128)(2,1)S(1)}, u32[]{:S(2)}, u32[]{:S(2)}) collective-permute-start(bf16[200,128]{1,0:T(8,128)(2,1)S(1)} %collective-permute-done.20.refs_4_), channel_id=1, source_target_pairs={{0,2},{1,3},{2,0},{3,1},{4,6},{5,7},{6,4},{7,5},{8,10},{9,11},{10,... | collective-permute-start | bytes 153608 | tf_op jit(solution)/shard_map/ppermute | solution.py:146
  56.8 4.1 %collective-permute-start.22 = (bf16[200,128]{1,0:T(8,128)(2,1)S(1)}, bf16[200,128]{1,0:T(8,128)(2,1)S(1)}, u32[]{:S(2)}, u32[]{:S(2)}) collective-permute-start(bf16[200,128]{1,0:T(8,128)(2,1)S(1)} %collective-permute-done.15.refs_6_), channel_id=1, source_target_pairs={{0,2},{1,3},{2,0},{3,1},{4,6},{5,7},{6,4},{7,5},{8,10},{9,11},{10,... | collective-permute-start | bytes 153608 | tf_op jit(solution)/shard_map/ppermute | solution.py:146
  62.8 1.8 %collective-permute-start.23 = (f32[208,512]{1,0:T(8,128)S(1)}, f32[208,512]{1,0:T(8,128)S(1)}, u32[]{:S(2)}, u32[]{:S(2)}) collective-permute-start(f32[208,512]{1,0:T(8,128)S(1)} %gram_and_cross.1.mine_ref), channel_id=1, source_target_pairs={{0,1},{1,0},{2,3},{3,2},{4,5},{5,4},{6,7},{7,6},{8,9},{9,8},{10,11... | collective-permute-start | bytes 1277960 | tf_op jit(solution)/shard_map/ppermute | solution.py:146

commit v7 on v6

--- a/solution.py
+++ b/solution.py
@@ -14,6 +14,7 @@
 
 inflation = 4.0
 epsilon = 1e-06
+well_conditioned = 128.0
 
 VMEM_LIMIT = 24 * 1024 * 1024
 MAPS_LIMIT = 44 * 1024 * 1024
@@ -467,7 +468,29 @@
         state_ref[0:members, 256:512] = state_ref[0:members, 256:512] + moved[:, 256:512]
         return (size,)
 
-    lax.while_loop(more, double, (jnp.float32(1.0),))
+    well = jnp.max(bound) <= well_conditioned * inflation
+    lax.while_loop(more, double, (jnp.where(well, 1.0, 0.0),))
+
+    @pl.when(jnp.logical_not(well))
+    def _():
+        state_ref[0:members, 0:256] = matrix
+        state_ref[0:members, 256:512] = total[:, 256:512]
+
+        def eliminate(k, carry):
+            rows = state_ref[0:members, :]
+            pivot_row = state_ref[pl.ds(k, 1), :]
+            pivot = jnp.sum(
+                jnp.where(lane[0:1] == k, pivot_row[:, 0:256], 0.0), axis=1, keepdims=True
+            )
+            column = jnp.sum(jnp.where(lane == k, rows[:, 0:256], 0.0), axis=1, keepdims=True)
+            pivot_row = pivot_row / pivot
+            state_ref[0:members, :] = jnp.where(
+                row[:, 0:1] == k, pivot_row, rows - column * pivot_row
+            )
+            return carry
+
+        lax.fori_loop(0, members, eliminate, 0)
+
     weights_ref[...] = state_ref[0:members, 256 : 256 + members]
 
     full = state_ref[:, 256:512]

time: 73.2 us -> 72.9 us (level)
  no operation moved by 1% of the time
where the time goes in v7:
time: 72.9 us; the launch traced here: 72.5 us
  starting transfers between devices  28.8 us (40%)
  waiting for transfers between devices  19.5 us (27%)
  Pallas kernels  18.9 us (26%)
  local copies, waits for them, and re-layouts  2.73 us (4%)
  other arithmetic  1.51 us (2%)
  between operations  1.01 us (1%)
    ppermute x24, starting transfers between devices, swap(): return lax.ppermute(value, 'map', pairs)  28.8 us
    ppermute x24, waiting for transfers between devices, swap(): return lax.ppermute(value, 'map', pairs)  19.5 us
    pallas_call x1, Pallas kernels, update(): pl.pallas_call(update_kernel, in_specs=[VMEM, VMEM, HBM], out_specs=[HBM,...  7.67 us
    pallas_call x1, Pallas kernels, shares(): pl.pallas_call(shares_kernel, in_specs=[VMEM] * 7, out_specs=[VMEM] * 4,...  4.26 us
    pallas_call x1, Pallas kernels, by_row(): pl.pallas_call(by_row_kernel, in_specs=[HBM], out_specs=VMEM, out_shape=j...  3.65 us
    unnamed x8, local copies, waits for them, and re-layouts  2.21 us
    pallas_call x1, Pallas kernels, gram(): pl.pallas_call(gram_kernel, in_specs=[VMEM] * (2 + len(predicted)), out_s...  1.89 us
  transfers between devices with their start and end apart: 24, of which 9 were waited for; matrix products, arithmetic and copies ran while one was open for 2% of the time, Pallas kernels for 7%

profile of v7, /device:TPU:0, one launch (start us, length us, event | category | flops | bytes accessed | tf_op | source)
XLA Modules:
  0.0 72.5 jit_solution(6390241364032490616)
XLA Ops:
  0.6 0.7 %pad_add_fusion.2 = s32[32]{0:T(128)S(1)} fusion(s32[16]{0:T(128)} %bitcast.31, s32[16]{0:T(128)} %param.9), kind=kLoop, calls=%fused_computation.19 | loop fusion | flops 32 | bytes 256 | tf_op jit(solution)/shard_map/concatenate | solution.py:551
  1.8 2.5 %collective-permute-start.2 = (s32[32]{0:T(128)S(1)}, s32[32]{0:T(128)S(1)}, u32[]{:S(2)}, u32[]{:S(2)}) collective-permute-start(s32[32]{0:T(128)S(1)} %pad_add_fusion.2), channel_id=1, source_target_pairs={{0,2},{1,3},{2,0},{3,1},{4,6},{5,7},{6,4},{7,5},{8,10},{9,11},{10,... | collective-permute-start | bytes 392 | tf_op jit(solution)/shard_map/ppermute | solution.py:147
  4.5 0.9 %copy-done.1 = bf16[256,200]{0,1:T(8,128)(2,1)S(1)} copy-done((bf16[256,200]{0,1:T(8,128)(2,1)S(1)}, bf16[256,200]{0,1:T(8,128)(2,1)}, u32[]{:S(2)}) %copy-start.1) | copy-done | bytes 102424
  6.0 0.7 copy-done.3
  7.4 0.8 %collective-permute-done = bf16[208,128]{1,0:T(8,128)(2,1)S(1)} collective-permute-done((bf16[208,128]{1,0:T(8,128)(2,1)S(1)}, bf16[208,128]{1,0:T(8,128)(2,1)S(1)}, u32[]{:S(2)}, u32[]{:S(2)}) %collective-permute-start) | collective-permute-done | bytes 53280 | tf_op jit(solution)/shard_map/ppermute | solution.py:147
  8.2 2.9 %collective-permute-start.7 = (bf16[2,208,128]{2,1,0:T(8,128)(2,1)S(1)}, bf16[2,208,128]{2,1,0:T(8,128)(2,1)S(1)}, u32[]{:S(2)}, u32[]{:S(2)}) collective-permute-start(bf16[2,208,128]{2,1,0:T(8,128)(2,1)S(1)} %pad_maximum_fusion.2), channel_id=1, source_target_pairs={{0,8},{1,9},{2,10},{3,11},{4,12},{5,13},{6,14},{7,15},{8,0},{9,1},... | collective-permute-start | bytes 319496 | tf_op jit(solution)/shard_map/ppermute | solution.py:147
  11.1 1.6 %collective-permute-start.4 = (s32[4,32]{1,0:T(4,128)S(1)}, s32[4,32]{1,0:T(4,128)S(1)}, u32[]{:S(2)}, u32[]{:S(2)}) collective-permute-start(s32[4,32]{1,0:T(4,128)S(1)} %pad_add_fusion.1.list0_ref), channel_id=1, source_target_pairs={{0,4},{1,5},{2,6},{3,7},{4,0},{5,1},{6,2},{7,3},{8,12},{9,13},{10,... | collective-permute-start | bytes 1544 | tf_op jit(solution)/shard_map/ppermute | solution.py:147
  13.0 2.5 %collective-permute-start.6 = (s32[4,32]{1,0:T(4,128)S(1)}, s32[4,32]{1,0:T(4,128)S(1)}, u32[]{:S(2)}, u32[]{:S(2)}) collective-permute-start(s32[4,32]{1,0:T(4,128)S(1)} %pad_add_fusion.1.list0_ref), channel_id=1, source_target_pairs={{0,12},{1,13},{2,14},{3,15},{4,8},{5,9},{6,10},{7,11},{8,4},{9,5},... | collective-permute-start | bytes 1544 | tf_op jit(solution)/shard_map/ppermute | solution.py:147
  15.5 3.7 %maps_by_row.1.maps_ref = bf16[32,200,512]{2,1,0:T(8,128)(2,1)S(1)} custom-call(bf16[200,32,512]{2,1,0:T(8,128)(2,1)} %maps_ref), custom_call_target="tpu_custom_call" | custom-call | bytes 13107200 | tf_op jit(solution)/shard_map/maps_by_row/pallas_call | solution.py:172
  19.2 4.3 %coefficient_shares.1 = (f32[4,200,128]{2,1,0:T(8,128)S(1)}, f32[4,200,128]{2,1,0:T(8,128)S(1)}, f32[4,200,128]{2,1,0:T(8,128)S(1)}, f32[4,200,128]{2,1,0:T(8,128)S(1)}) custom-call(s32[4,32]{1,0:T(4,128)S(1)} %pad_add_fusion.1.list0_ref, s32[4,32]{1,0:T(4,128)S(1)} %collective-permute-done.4.list1_ref, s32[4,32]{1,0:T(4,128)S(1)} %collective-permute-done.5.list2_ref, ...), custom_call_target="tpu_custom_call" | custom-call | flops 1677721600 | bytes 6553600 | tf_op jit(solution)/shard_map/coefficient_shares/pallas_call | solution.py:259
  24.2 1.1 %collective-permute-done.9 = f32[4,200,128]{2,1,0:T(8,128)S(1)} collective-permute-done((f32[4,200,128]{2,1,0:T(8,128)S(1)}, f32[4,200,128]{2,1,0:T(8,128)S(1)}, u32[]{:S(2)}, u32[]{:S(2)}) %collective-permute-start.9) | collective-permute-done | bytes 409632 | tf_op jit(solution)/shard_map/ppermute | solution.py:147
  25.3 1.6 %collective-permute-start.10 = (f32[4,200,128]{2,1,0:T(8,128)S(1)}, f32[4,200,128]{2,1,0:T(8,128)S(1)}, u32[]{:S(2)}, u32[]{:S(2)}) collective-permute-start(f32[4,200,128]{2,1,0:T(8,128)S(1)} %add.125), channel_id=1, source_target_pairs={{0,2},{1,3},{2,0},{3,1},{4,6},{5,7},{6,4},{7,5},{8,10},{9,11},{10,... | collective-permute-start | bytes 1228808 | tf_op jit(solution)/shard_map/ppermute | solution.py:147
  26.9 0.7 %collective-permute-start.11 = (bf16[2,2,208,128]{3,2,1,0:T(8,128)(2,1)S(1)}, bf16[2,2,208,128]{3,2,1,0:T(8,128)(2,1)S(1)}, u32[]{:S(2)}, u32[]{:S(2)}) collective-permute-start(bf16[2,2,208,128]{3,2,1,0:T(8,128)(2,1)S(1)} %pad_maximum_fusion.1), channel_id=1, source_target_pairs={{0,4},{1,5},{2,6},{3,7},{4,0},{5,1},{6,2},{7,3},{8,12},{9,13},{10,... | collective-permute-start | bytes 638984 | tf_op jit(solution)/shard_map/ppermute | solution.py:147
  28.1 8.8 %collective-permute-done.10 = f32[4,200,128]{2,1,0:T(8,128)S(1)} collective-permute-done((f32[4,200,128]{2,1,0:T(8,128)S(1)}, f32[4,200,128]{2,1,0:T(8,128)S(1)}, u32[]{:S(2)}, u32[]{:S(2)}) %collective-permute-start.10) | collective-permute-done | bytes 409632 | tf_op jit(solution)/shard_map/ppermute | solution.py:147
  37.0 0.7 %collective-permute-start.12 = (f32[200,128]{1,0:T(8,128)S(1)}, f32[200,128]{1,0:T(8,128)S(1)}, u32[]{:S(2)}, u32[]{:S(2)}) collective-permute-start(f32[200,128]{1,0:T(8,128)S(1)} %get-tuple-element.43), channel_id=1, source_target_pairs={{0,4},{1,5},{2,6},{3,7},{4,0},{5,1},{6,2},{7,3},{8,12},{9,13},{10,... | collective-permute-start | bytes 307208 | tf_op jit(solution)/shard_map/ppermute | solution.py:147
  37.7 1.6 %collective-permute-start.13 = (f32[200,128]{1,0:T(8,128)S(1)}, f32[200,128]{1,0:T(8,128)S(1)}, u32[]{:S(2)}, u32[]{:S(2)}) collective-permute-start(f32[200,128]{1,0:T(8,128)S(1)} %get-tuple-element.48), channel_id=1, source_target_pairs={{0,8},{1,9},{2,10},{3,11},{4,12},{5,13},{6,14},{7,15},{8,0},{9,1},... | collective-permute-start | bytes 307208 | tf_op jit(solution)/shard_map/ppermute | solution.py:147
  39.3 2.2 %collective-permute-start.14 = (f32[200,128]{1,0:T(8,128)S(1)}, f32[200,128]{1,0:T(8,128)S(1)}, u32[]{:S(2)}, u32[]{:S(2)}) collective-permute-start(f32[200,128]{1,0:T(8,128)S(1)} %get-tuple-element.49), channel_id=1, source_target_pairs={{0,12},{1,13},{2,14},{3,15},{4,8},{5,9},{6,10},{7,11},{8,4},{9,5},... | collective-permute-start | bytes 307208 | tf_op jit(solution)/shard_map/ppermute | solution.py:147
  41.5 1.0 %collective-permute-done.12 = f32[200,128]{1,0:T(8,128)S(1)} collective-permute-done((f32[200,128]{1,0:T(8,128)S(1)}, f32[200,128]{1,0:T(8,128)S(1)}, u32[]{:S(2)}, u32[]{:S(2)}) %collective-permute-start.12) | collective-permute-done | bytes 102432 | tf_op jit(solution)/shard_map/ppermute | solution.py:147
  42.4 1.5 %collective-permute-start.16 = (bf16[4,2,208,128]{3,2,1,0:T(8,128)(2,1)S(1)}, bf16[4,2,208,128]{3,2,1,0:T(8,128)(2,1)S(1)}, u32[]{:S(2)}, u32[]{:S(2)}) collective-permute-start(bf16[4,2,208,128]{3,2,1,0:T(8,128)(2,1)S(1)} %pad_maximum_fusion.near_ref), channel_id=1, source_target_pairs={{0,2},{1,3},{2,0},{3,1},{4,6},{5,7},{6,4},{7,5},{8,10},{9,11},{10,... | collective-permute-start | bytes 1277960 | tf_op jit(solution)/shard_map/ppermute | solution.py:147
  43.9 4.0 %collective-permute-done.13 = f32[200,128]{1,0:T(8,128)S(1)} collective-permute-done((f32[200,128]{1,0:T(8,128)S(1)}, f32[200,128]{1,0:T(8,128)S(1)}, u32[]{:S(2)}, u32[]{:S(2)}) %collective-permute-start.13) | collective-permute-done | bytes 102432 | tf_op jit(solution)/shard_map/ppermute | solution.py:147
  47.9 1.5 %collective-permute-start.15 = (bf16[200,128]{1,0:T(8,128)(2,1)S(1)}, bf16[200,128]{1,0:T(8,128)(2,1)S(1)}, u32[]{:S(2)}, u32[]{:S(2)}) collective-permute-start(bf16[200,128]{1,0:T(8,128)(2,1)S(1)} %add_convert_fusion.refs_0_), channel_id=1, source_target_pairs={{0,12},{1,13},{2,14},{3,15},{4,8},{5,9},{6,10},{7,11},{8,4},{9,5},... | collective-permute-start | bytes 153608 | tf_op jit(solution)/shard_map/ppermute | solution.py:147
  49.4 0.9 %collective-permute-start.18 = (bf16[200,128]{1,0:T(8,128)(2,1)S(1)}, bf16[200,128]{1,0:T(8,128)(2,1)S(1)}, u32[]{:S(2)}, u32[]{:S(2)}) collective-permute-start(bf16[200,128]{1,0:T(8,128)(2,1)S(1)} %add_convert_fusion.refs_0_), channel_id=1, source_target_pairs={{0,4},{1,5},{2,6},{3,7},{4,0},{5,1},{6,2},{7,3},{8,12},{9,13},{10,... | collective-permute-start | bytes 153608 | tf_op jit(solution)/shard_map/ppermute | solution.py:147
  50.3 2.1 %collective-permute-start.20 = (bf16[200,128]{1,0:T(8,128)(2,1)S(1)}, bf16[200,128]{1,0:T(8,128)(2,1)S(1)}, u32[]{:S(2)}, u32[]{:S(2)}) collective-permute-start(bf16[200,128]{1,0:T(8,128)(2,1)S(1)} %add_convert_fusion.refs_0_), channel_id=1, source_target_pairs={{0,8},{1,9},{2,10},{3,11},{4,12},{5,13},{6,14},{7,15},{8,0},{9,1},... | collective-permute-start | bytes 153608 | tf_op jit(solution)/shard_map/ppermute | solution.py:147
  52.7 1.6 %collective-permute-start.17 = (bf16[200,128]{1,0:T(8,128)(2,1)S(1)}, bf16[200,128]{1,0:T(8,128)(2,1)S(1)}, u32[]{:S(2)}, u32[]{:S(2)}) collective-permute-start(bf16[200,128]{1,0:T(8,128)(2,1)S(1)} %add_convert_fusion.refs_0_), channel_id=1, source_target_pairs={{0,2},{1,3},{2,0},{3,1},{4,6},{5,7},{6,4},{7,5},{8,10},{9,11},{10,... | collective-permute-start | bytes 153608 | tf_op jit(solution)/shard_map/ppermute | solution.py:147
  54.3 1.3 %collective-permute-start.19 = (bf16[200,128]{1,0:T(8,128)(2,1)S(1)}, bf16[200,128]{1,0:T(8,128)(2,1)S(1)}, u32[]{:S(2)}, u32[]{:S(2)}) collective-permute-start(bf16[200,128]{1,0:T(8,128)(2,1)S(1)} %collective-permute-done.18.refs_2_), channel_id=1, source_target_pairs={{0,2},{1,3},{2,0},{3,1},{4,6},{5,7},{6,4},{7,5},{8,10},{9,11},{10,... | collective-permute-start | bytes 153608 | tf_op jit(solution)/shard_map/ppermute | solution.py:147
  55.6 1.2 %collective-permute-start.21 = (bf16[200,128]{1,0:T(8,128)(2,1)S(1)}, bf16[200,128]{1,0:T(8,128)(2,1)S(1)}, u32[]{:S(2)}, u32[]{:S(2)}) collective-permute-start(bf16[200,128]{1,0:T(8,128)(2,1)S(1)} %collective-permute-done.20.refs_4_), channel_id=1, source_target_pairs={{0,2},{1,3},{2,0},{3,1},{4,6},{5,7},{6,4},{7,5},{8,10},{9,11},{10,... | collective-permute-start | bytes 153608 | tf_op jit(solution)/shard_map/ppermute | solution.py:147
  56.8 0.9 %collective-permute-start.22 = (bf16[200,128]{1,0:T(8,128)(2,1)S(1)}, bf16[200,128]{1,0:T(8,128)(2,1)S(1)}, u32[]{:S(2)}, u32[]{:S(2)}) collective-permute-start(bf16[200,128]{1,0:T(8,128)(2,1)S(1)} %collective-permute-done.15.refs_6_), channel_id=1, source_target_pairs={{0,2},{1,3},{2,0},{3,1},{4,6},{5,7},{6,4},{7,5},{8,10},{9,11},{10,... | collective-permute-start | bytes 153608 | tf_op jit(solution)/shard_map/ppermute | solution.py:147
  57.9 1.2 %select_noise.1.noise_ref = f32[8,208,128]{2,1,0:T(8,128)S(1)} custom-call(s32[128]{0:T(128)S(1)} %reshape.83.starts_ref, bf16[4,2,208,128]{3,2,1,0:T(8,128)(2,1)S(1)} %pad_maximum_fusion.near_ref, bf16[4,2,208,128]{3,2,1,0:T(8,128)(2,1)S(1)} %collective-permute-done.16.far_ref), custom_call_target="tpu_custom_call" | custom-call | tf_op jit(solution)/shard_map/select_noise/pallas_call | solution.py:343
  59.8 1.2 %collective-permute-done.22.refs_7_ = bf16[200,128]{1,0:T(8,128)(2,1)S(1)} collective-permute-done((bf16[200,128]{1,0:T(8,128)(2,1)S(1)}, bf16[200,128]{1,0:T(8,128)(2,1)S(1)}, u32[]{:S(2)}, u32[]{:S(2)}) %collective-permute-start.22) | collective-permute-done | bytes 51232 | tf_op jit(solution)/shard_map/ppermute | solution.py:147
  60.9 1.9 %gram_and_cross.1.mine_ref = f32[208,512]{1,0:T(8,128)S(1)} custom-call(s32[8,128,1]{2,1,0:T(8,128)S(1)} %broadcast_add_fusion.target_ref, f32[8,208,128]{2,1,0:T(8,128)S(1)} %select_noise.1.noise_ref, bf16[200,128]{1,0:T(8,128)(2,1)S(1)} %add_convert_fusion.refs_0_, bf16[200,128]{1,0:T(8,128)(2,1)S(1)} %collective-permute-done.17.refs_1_, ...), custom_call_target="tpu_custom_call" | custom-call | tf_op jit(solution)/shard_map/gram_and_cross/pallas_call | solution.py:412
  62.9 1.8 %collective-permute-done.23.other_ref = f32[208,512]{1,0:T(8,128)S(1)} collective-permute-done((f32[208,512]{1,0:T(8,128)S(1)}, f32[208,512]{1,0:T(8,128)S(1)}, u32[]{:S(2)}, u32[]{:S(2)}) %collective-permute-start.23) | collective-permute-done | bytes 426016 | tf_op jit(solution)/shard_map/ppermute | solution.py:147
  64.6 7.7 %solve_and_update.1 = (bf16[200,12288]{1,0:T(8,128)(2,1)}, f32[200,200]{1,0:T(8,128)}, f32[1,256]{1,0:T(1,128)}) custom-call(f32[208,512]{1,0:T(8,128)S(1)} %gram_and_cross.1.mine_ref, f32[208,512]{1,0:T(8,128)S(1)} %collective-permute-done.23.other_ref, bf16[200,12288]{1,0:T(8,128)(2,1)} %slab_ref.1), custom_call_target="tpu_custom_call" | custom-call | tf_op jit(solution)/shard_map/solve_and_update/pallas_call | solution.py:520
  (51 shorter events, 4.8 us)
Async XLA Ops:
  1.4 5.7 %collective-permute-start.1 = (s32[32]{0:T(128)S(1)}, s32[32]{0:T(128)S(1)}, u32[]{:S(2)}, u32[]{:S(2)}) collective-permute-start(s32[32]{0:T(128)S(1)} %pad_add_fusion.2), channel_id=1, source_target_pairs={{0,1},{1,0},{2,3},{3,2},{4,5},{5,4},{6,7},{7,6},{8,9},{9,8},{10,11... | collective-permute-start | bytes 392 | tf_op jit(solution)/shard_map/ppermute | solution.py:147
  1.8 5.2 %collective-permute-start.2 = (s32[32]{0:T(128)S(1)}, s32[32]{0:T(128)S(1)}, u32[]{:S(2)}, u32[]{:S(2)}) collective-permute-start(s32[32]{0:T(128)S(1)} %pad_add_fusion.2), channel_id=1, source_target_pairs={{0,2},{1,3},{2,0},{3,1},{4,6},{5,7},{6,4},{7,5},{8,10},{9,11},{10,... | collective-permute-start | bytes 392 | tf_op jit(solution)/shard_map/ppermute | solution.py:147
  4.4 3.0 %collective-permute-start.3 = (s32[32]{0:T(128)S(1)}, s32[32]{0:T(128)S(1)}, u32[]{:S(2)}, u32[]{:S(2)}) collective-permute-start(s32[32]{0:T(128)S(1)} %pad_add_fusion.2), channel_id=1, source_target_pairs={{0,3},{1,2},{2,1},{3,0},{4,7},{5,6},{6,5},{7,4},{8,11},{9,10},{10,... | collective-permute-start | bytes 392 | tf_op jit(solution)/shard_map/ppermute | solution.py:147
  4.5 0.9 %copy-start.1 = (bf16[256,200]{0,1:T(8,128)(2,1)S(1)}, bf16[256,200]{0,1:T(8,128)(2,1)}, u32[]{:S(2)}) copy-start(bf16[256,200]{0,1:T(8,128)(2,1)} %param.13) | copy-start | bytes 307204
  5.4 0.7 copy-start.2
  6.0 0.7 copy-start.3
  6.9 1.3 %collective-permute-start = (bf16[208,128]{1,0:T(8,128)(2,1)S(1)}, bf16[208,128]{1,0:T(8,128)(2,1)S(1)}, u32[]{:S(2)}, u32[]{:S(2)}) collective-permute-start(bf16[208,128]{1,0:T(8,128)(2,1)S(1)} %get-tuple-element.30), channel_id=1, source_target_pairs={{0,1},{1,0},{2,3},{3,2},{4,5},{5,4},{6,7},{7,6},{8,9},{9,8},{10,11... | collective-permute-start | bytes 159752 | tf_op jit(solution)/shard_map/ppermute | solution.py:147
  8.2 11.0 %copy-start = (bf16[512,512]{1,0:T(8,128)(2,1)S(1)}, bf16[512,512]{1,0:T(8,128)(2,1)}, u32[]{:S(2)}) copy-start(bf16[512,512]{1,0:T(8,128)(2,1)} %constant.10.clone.table_w_ref.table_h_ref) | copy-start | bytes 1572868
  8.2 11.0 %collective-permute-start.7 = (bf16[2,208,128]{2,1,0:T(8,128)(2,1)S(1)}, bf16[2,208,128]{2,1,0:T(8,128)(2,1)S(1)}, u32[]{:S(2)}, u32[]{:S(2)}) collective-permute-start(bf16[2,208,128]{2,1,0:T(8,128)(2,1)S(1)} %pad_maximum_fusion.2), channel_id=1, source_target_pairs={{0,8},{1,9},{2,10},{3,11},{4,12},{5,13},{6,14},{7,15},{8,0},{9,1},... | collective-permute-start | bytes 319496 | tf_op jit(solution)/shard_map/ppermute | solution.py:147
  11.1 8.1 %collective-permute-start.4 = (s32[4,32]{1,0:T(4,128)S(1)}, s32[4,32]{1,0:T(4,128)S(1)}, u32[]{:S(2)}, u32[]{:S(2)}) collective-permute-start(s32[4,32]{1,0:T(4,128)S(1)} %pad_add_fusion.1.list0_ref), channel_id=1, source_target_pairs={{0,4},{1,5},{2,6},{3,7},{4,0},{5,1},{6,2},{7,3},{8,12},{9,13},{10,... | collective-permute-start | bytes 1544 | tf_op jit(solution)/shard_map/ppermute | solution.py:147
  12.7 6.5 %collective-permute-start.5 = (s32[4,32]{1,0:T(4,128)S(1)}, s32[4,32]{1,0:T(4,128)S(1)}, u32[]{:S(2)}, u32[]{:S(2)}) collective-permute-start(s32[4,32]{1,0:T(4,128)S(1)} %pad_add_fusion.1.list0_ref), channel_id=1, source_target_pairs={{0,8},{1,9},{2,10},{3,11},{4,12},{5,13},{6,14},{7,15},{8,0},{9,1},... | collective-permute-start | bytes 1544 | tf_op jit(solution)/shard_map/ppermute | solution.py:147
  13.0 6.2 %collective-permute-start.6 = (s32[4,32]{1,0:T(4,128)S(1)}, s32[4,32]{1,0:T(4,128)S(1)}, u32[]{:S(2)}, u32[]{:S(2)}) collective-permute-start(s32[4,32]{1,0:T(4,128)S(1)} %pad_add_fusion.1.list0_ref), channel_id=1, source_target_pairs={{0,12},{1,13},{2,14},{3,15},{4,8},{5,9},{6,10},{7,11},{8,4},{9,5},... | collective-permute-start | bytes 1544 | tf_op jit(solution)/shard_map/ppermute | solution.py:147
  23.5 1.8 %collective-permute-start.9 = (f32[4,200,128]{2,1,0:T(8,128)S(1)}, f32[4,200,128]{2,1,0:T(8,128)S(1)}, u32[]{:S(2)}, u32[]{:S(2)}) collective-permute-start(f32[4,200,128]{2,1,0:T(8,128)S(1)} %get-tuple-element.41), channel_id=1, source_target_pairs={{0,1},{1,0},{2,3},{3,2},{4,5},{5,4},{6,7},{7,6},{8,9},{9,8},{10,11... | collective-permute-start | bytes 1228808 | tf_op jit(solution)/shard_map/ppermute | solution.py:147
  23.6 4.4 %collective-permute-start.8 = (f32[4,200,128]{2,1,0:T(8,128)S(1)}, f32[4,200,128]{2,1,0:T(8,128)S(1)}, u32[]{:S(2)}, u32[]{:S(2)}) collective-permute-start(f32[4,200,128]{2,1,0:T(8,128)S(1)} %get-tuple-element.39), channel_id=1, source_target_pairs={{0,1},{1,0},{2,3},{3,2},{4,5},{5,4},{6,7},{7,6},{8,9},{9,8},{10,11... | collective-permute-start | bytes 1228808 | tf_op jit(solution)/shard_map/ppermute | solution.py:147
  25.3 11.6 %collective-permute-start.10 = (f32[4,200,128]{2,1,0:T(8,128)S(1)}, f32[4,200,128]{2,1,0:T(8,128)S(1)}, u32[]{:S(2)}, u32[]{:S(2)}) collective-permute-start(f32[4,200,128]{2,1,0:T(8,128)S(1)} %add.125), channel_id=1, source_target_pairs={{0,2},{1,3},{2,0},{3,1},{4,6},{5,7},{6,4},{7,5},{8,10},{9,11},{10,... | collective-permute-start | bytes 1228808 | tf_op jit(solution)/shard_map/ppermute | solution.py:147
  26.9 10.1 %collective-permute-start.11 = (bf16[2,2,208,128]{3,2,1,0:T(8,128)(2,1)S(1)}, bf16[2,2,208,128]{3,2,1,0:T(8,128)(2,1)S(1)}, u32[]{:S(2)}, u32[]{:S(2)}) collective-permute-start(bf16[2,2,208,128]{3,2,1,0:T(8,128)(2,1)S(1)} %pad_maximum_fusion.1), channel_id=1, source_target_pairs={{0,4},{1,5},{2,6},{3,7},{4,0},{5,1},{6,2},{7,3},{8,12},{9,13},{10,... | collective-permute-start | bytes 638984 | tf_op jit(solution)/shard_map/ppermute | solution.py:147
  37.0 5.5 %collective-permute-start.12 = (f32[200,128]{1,0:T(8,128)S(1)}, f32[200,128]{1,0:T(8,128)S(1)}, u32[]{:S(2)}, u32[]{:S(2)}) collective-permute-start(f32[200,128]{1,0:T(8,128)S(1)} %get-tuple-element.43), channel_id=1, source_target_pairs={{0,4},{1,5},{2,6},{3,7},{4,0},{5,1},{6,2},{7,3},{8,12},{9,13},{10,... | collective-permute-start | bytes 307208 | tf_op jit(solution)/shard_map/ppermute | solution.py:147
  37.7 10.2 %collective-permute-start.13 = (f32[200,128]{1,0:T(8,128)S(1)}, f32[200,128]{1,0:T(8,128)S(1)}, u32[]{:S(2)}, u32[]{:S(2)}) collective-permute-start(f32[200,128]{1,0:T(8,128)S(1)} %get-tuple-element.48), channel_id=1, source_target_pairs={{0,8},{1,9},{2,10},{3,11},{4,12},{5,13},{6,14},{7,15},{8,0},{9,1},... | collective-permute-start | bytes 307208 | tf_op jit(solution)/shard_map/ppermute | solution.py:147
  39.3 8.6 %collective-permute-start.14 = (f32[200,128]{1,0:T(8,128)S(1)}, f32[200,128]{1,0:T(8,128)S(1)}, u32[]{:S(2)}, u32[]{:S(2)}) collective-permute-start(f32[200,128]{1,0:T(8,128)S(1)} %get-tuple-element.49), channel_id=1, source_target_pairs={{0,12},{1,13},{2,14},{3,15},{4,8},{5,9},{6,10},{7,11},{8,4},{9,5},... | collective-permute-start | bytes 307208 | tf_op jit(solution)/shard_map/ppermute | solution.py:147
  42.4 14.4 %collective-permute-start.16 = (bf16[4,2,208,128]{3,2,1,0:T(8,128)(2,1)S(1)}, bf16[4,2,208,128]{3,2,1,0:T(8,128)(2,1)S(1)}, u32[]{:S(2)}, u32[]{:S(2)}) collective-permute-start(bf16[4,2,208,128]{3,2,1,0:T(8,128)(2,1)S(1)} %pad_maximum_fusion.near_ref), channel_id=1, source_target_pairs={{0,2},{1,3},{2,0},{3,1},{4,6},{5,7},{6,4},{7,5},{8,10},{9,11},{10,... | collective-permute-start | bytes 1277960 | tf_op jit(solution)/shard_map/ppermute | solution.py:147
  47.9 8.9 %collective-permute-start.15 = (bf16[200,128]{1,0:T(8,128)(2,1)S(1)}, bf16[200,128]{1,0:T(8,128)(2,1)S(1)}, u32[]{:S(2)}, u32[]{:S(2)}) collective-permute-start(bf16[200,128]{1,0:T(8,128)(2,1)S(1)} %add_convert_fusion.refs_0_), channel_id=1, source_target_pairs={{0,12},{1,13},{2,14},{3,15},{4,8},{5,9},{6,10},{7,11},{8,4},{9,5},... | collective-permute-start | bytes 153608 | tf_op jit(solution)/shard_map/ppermute | solution.py:147
  49.4 4.9 %collective-permute-start.18 = (bf16[200,128]{1,0:T(8,128)(2,1)S(1)}, bf16[200,128]{1,0:T(8,128)(2,1)S(1)}, u32[]{:S(2)}, u32[]{:S(2)}) collective-permute-start(bf16[200,128]{1,0:T(8,128)(2,1)S(1)} %add_convert_fusion.refs_0_), channel_id=1, source_target_pairs={{0,4},{1,5},{2,6},{3,7},{4,0},{5,1},{6,2},{7,3},{8,12},{9,13},{10,... | collective-permute-start | bytes 153608 | tf_op jit(solution)/shard_map/ppermute | solution.py:147
  50.3 5.3 %collective-permute-start.20 = (bf16[200,128]{1,0:T(8,128)(2,1)S(1)}, bf16[200,128]{1,0:T(8,128)(2,1)S(1)}, u32[]{:S(2)}, u32[]{:S(2)}) collective-permute-start(bf16[200,128]{1,0:T(8,128)(2,1)S(1)} %add_convert_fusion.refs_0_), channel_id=1, source_target_pairs={{0,8},{1,9},{2,10},{3,11},{4,12},{5,13},{6,14},{7,15},{8,0},{9,1},... | collective-permute-start | bytes 153608 | tf_op jit(solution)/shard_map/ppermute | solution.py:147
  52.7 6.4 %collective-permute-start.17 = (bf16[200,128]{1,0:T(8,128)(2,1)S(1)}, bf16[200,128]{1,0:T(8,128)(2,1)S(1)}, u32[]{:S(2)}, u32[]{:S(2)}) collective-permute-start(bf16[200,128]{1,0:T(8,128)(2,1)S(1)} %add_convert_fusion.refs_0_), channel_id=1, source_target_pairs={{0,2},{1,3},{2,0},{3,1},{4,6},{5,7},{6,4},{7,5},{8,10},{9,11},{10,... | collective-permute-start | bytes 153608 | tf_op jit(solution)/shard_map/ppermute | solution.py:147
  54.3 4.8 %collective-permute-start.19 = (bf16[200,128]{1,0:T(8,128)(2,1)S(1)}, bf16[200,128]{1,0:T(8,128)(2,1)S(1)}, u32[]{:S(2)}, u32[]{:S(2)}) collective-permute-start(bf16[200,128]{1,0:T(8,128)(2,1)S(1)} %collective-permute-done.18.refs_2_), channel_id=1, source_target_pairs={{0,2},{1,3},{2,0},{3,1},{4,6},{5,7},{6,4},{7,5},{8,10},{9,11},{10,... | collective-permute-start | bytes 153608 | tf_op jit(solution)/shard_map/ppermute | solution.py:147
  55.6 4.1 %collective-permute-start.21 = (bf16[200,128]{1,0:T(8,128)(2,1)S(1)}, bf16[200,128]{1,0:T(8,128)(2,1)S(1)}, u32[]{:S(2)}, u32[]{:S(2)}) collective-permute-start(bf16[200,128]{1,0:T(8,128)(2,1)S(1)} %collective-permute-done.20.refs_4_), channel_id=1, source_target_pairs={{0,2},{1,3},{2,0},{3,1},{4,6},{5,7},{6,4},{7,5},{8,10},{9,11},{10,... | collective-permute-start | bytes 153608 | tf_op jit(solution)/shard_map/ppermute | solution.py:147
  56.8 4.1 %collective-permute-start.22 = (bf16[200,128]{1,0:T(8,128)(2,1)S(1)}, bf16[200,128]{1,0:T(8,128)(2,1)S(1)}, u32[]{:S(2)}, u32[]{:S(2)}) collective-permute-start(bf16[200,128]{1,0:T(8,128)(2,1)S(1)} %collective-permute-done.15.refs_6_), channel_id=1, source_target_pairs={{0,2},{1,3},{2,0},{3,1},{4,6},{5,7},{6,4},{7,5},{8,10},{9,11},{10,... | collective-permute-start | bytes 153608 | tf_op jit(solution)/shard_map/ppermute | solution.py:147
  62.8 1.8 %collective-permute-start.23 = (f32[208,512]{1,0:T(8,128)S(1)}, f32[208,512]{1,0:T(8,128)S(1)}, u32[]{:S(2)}, u32[]{:S(2)}) collective-permute-start(f32[208,512]{1,0:T(8,128)S(1)} %gram_and_cross.1.mine_ref), channel_id=1, source_target_pairs={{0,1},{1,0},{2,3},{3,2},{4,5},{5,4},{6,7},{7,6},{8,9},{9,8},{10,11... | collective-permute-start | bytes 1277960 | tf_op jit(solution)/shard_map/ppermute | solution.py:147

commit v8 on v7

--- a/solution.py
+++ b/solution.py
@@ -363,7 +363,9 @@
     chip = lax.axis_index("map") >> 1
     for i, ref in enumerate(predicted_refs):
         predicted_ref[chip ^ i] = ref[...].astype(jnp.float32)
-    right_ref[...] = jnp.zeros_like(right_ref)
+    padding = jnp.zeros((256 - members, coefficients), jnp.float32)
+    right_ref[members:256, :] = padding
+    right_ref[256 + members : 512, :] = padding
     for g in range(groups):
         noise = noise_ref[g]
         observed = noise[members : members + 1]

time: 72.9 us -> 72.6 us (level)
  no operation moved by 1% of the time
where the time goes in v8:
time: 72.6 us; the launch traced here: 72.5 us
  starting transfers between devices  28.8 us (40%)
  waiting for transfers between devices  19.5 us (27%)
  Pallas kernels  18.9 us (26%)
  local copies, waits for them, and re-layouts  2.73 us (4%)
  other arithmetic  1.51 us (2%)
  between operations  1.01 us (1%)
    ppermute x24, starting transfers between devices, swap(): return lax.ppermute(value, 'map', pairs)  28.8 us
    ppermute x24, waiting for transfers between devices, swap(): return lax.ppermute(value, 'map', pairs)  19.5 us
    pallas_call x1, Pallas kernels, update(): pl.pallas_call(update_kernel, in_specs=[VMEM, VMEM, HBM], out_specs=[HBM,...  7.67 us
    pallas_call x1, Pallas kernels, shares(): pl.pallas_call(shares_kernel, in_specs=[VMEM] * 7, out_specs=[VMEM] * 4,...  4.26 us
    pallas_call x1, Pallas kernels, by_row(): pl.pallas_call(by_row_kernel, in_specs=[HBM], out_specs=VMEM, out_shape=j...  3.65 us
    unnamed x8, local copies, waits for them, and re-layouts  2.21 us
    pallas_call x1, Pallas kernels, gram(): pl.pallas_call(gram_kernel, in_specs=[VMEM] * (2 + len(predicted)), out_s...  1.89 us
  transfers between devices with their start and end apart: 24, of which 9 were waited for; matrix products, arithmetic and copies ran while one was open for 2% of the time, Pallas kernels for 7%

profile of v8, /device:TPU:0, one launch (start us, length us, event | category | flops | bytes accessed | tf_op | source)
XLA Modules:
  0.0 72.5 jit_solution(6390241364032490616)
XLA Ops:
  0.6 0.7 %pad_add_fusion.2 = s32[32]{0:T(128)S(1)} fusion(s32[16]{0:T(128)} %bitcast.31, s32[16]{0:T(128)} %param.9), kind=kLoop, calls=%fused_computation.19 | loop fusion | flops 32 | bytes 256 | tf_op jit(solution)/shard_map/concatenate | solution.py:553
  1.8 2.5 %collective-permute-start.2 = (s32[32]{0:T(128)S(1)}, s32[32]{0:T(128)S(1)}, u32[]{:S(2)}, u32[]{:S(2)}) collective-permute-start(s32[32]{0:T(128)S(1)} %pad_add_fusion.2), channel_id=1, source_target_pairs={{0,2},{1,3},{2,0},{3,1},{4,6},{5,7},{6,4},{7,5},{8,10},{9,11},{10,... | collective-permute-start | bytes 392 | tf_op jit(solution)/shard_map/ppermute | solution.py:147
  4.5 0.9 %copy-done.1 = bf16[256,200]{0,1:T(8,128)(2,1)S(1)} copy-done((bf16[256,200]{0,1:T(8,128)(2,1)S(1)}, bf16[256,200]{0,1:T(8,128)(2,1)}, u32[]{:S(2)}) %copy-start.1) | copy-done | bytes 102424
  5.4 0.7 copy-done.2
  7.4 0.8 %collective-permute-done = bf16[208,128]{1,0:T(8,128)(2,1)S(1)} collective-permute-done((bf16[208,128]{1,0:T(8,128)(2,1)S(1)}, bf16[208,128]{1,0:T(8,128)(2,1)S(1)}, u32[]{:S(2)}, u32[]{:S(2)}) %collective-permute-start) | collective-permute-done | bytes 53280 | tf_op jit(solution)/shard_map/ppermute | solution.py:147
  8.2 2.9 %collective-permute-start.7 = (bf16[2,208,128]{2,1,0:T(8,128)(2,1)S(1)}, bf16[2,208,128]{2,1,0:T(8,128)(2,1)S(1)}, u32[]{:S(2)}, u32[]{:S(2)}) collective-permute-start(bf16[2,208,128]{2,1,0:T(8,128)(2,1)S(1)} %pad_maximum_fusion.2), channel_id=1, source_target_pairs={{0,8},{1,9},{2,10},{3,11},{4,12},{5,13},{6,14},{7,15},{8,0},{9,1},... | collective-permute-start | bytes 319496 | tf_op jit(solution)/shard_map/ppermute | solution.py:147
  11.1 1.6 %collective-permute-start.4 = (s32[4,32]{1,0:T(4,128)S(1)}, s32[4,32]{1,0:T(4,128)S(1)}, u32[]{:S(2)}, u32[]{:S(2)}) collective-permute-start(s32[4,32]{1,0:T(4,128)S(1)} %pad_add_fusion.1.list0_ref), channel_id=1, source_target_pairs={{0,4},{1,5},{2,6},{3,7},{4,0},{5,1},{6,2},{7,3},{8,12},{9,13},{10,... | collective-permute-start | bytes 1544 | tf_op jit(solution)/shard_map/ppermute | solution.py:147
  13.0 2.5 %collective-permute-start.6 = (s32[4,32]{1,0:T(4,128)S(1)}, s32[4,32]{1,0:T(4,128)S(1)}, u32[]{:S(2)}, u32[]{:S(2)}) collective-permute-start(s32[4,32]{1,0:T(4,128)S(1)} %pad_add_fusion.1.list0_ref), channel_id=1, source_target_pairs={{0,12},{1,13},{2,14},{3,15},{4,8},{5,9},{6,10},{7,11},{8,4},{9,5},... | collective-permute-start | bytes 1544 | tf_op jit(solution)/shard_map/ppermute | solution.py:147
  15.5 3.7 %maps_by_row.1.maps_ref = bf16[32,200,512]{2,1,0:T(8,128)(2,1)S(1)} custom-call(bf16[200,32,512]{2,1,0:T(8,128)(2,1)} %maps_ref), custom_call_target="tpu_custom_call" | custom-call | bytes 13107200 | tf_op jit(solution)/shard_map/maps_by_row/pallas_call | solution.py:172
  19.2 4.3 %coefficient_shares.1 = (f32[4,200,128]{2,1,0:T(8,128)S(1)}, f32[4,200,128]{2,1,0:T(8,128)S(1)}, f32[4,200,128]{2,1,0:T(8,128)S(1)}, f32[4,200,128]{2,1,0:T(8,128)S(1)}) custom-call(s32[4,32]{1,0:T(4,128)S(1)} %pad_add_fusion.1.list0_ref, s32[4,32]{1,0:T(4,128)S(1)} %collective-permute-done.4.list1_ref, s32[4,32]{1,0:T(4,128)S(1)} %collective-permute-done.5.list2_ref, ...), custom_call_target="tpu_custom_call" | custom-call | flops 1677721600 | bytes 6553600 | tf_op jit(solution)/shard_map/coefficient_shares/pallas_call | solution.py:259
  24.2 1.1 %collective-permute-done.9 = f32[4,200,128]{2,1,0:T(8,128)S(1)} collective-permute-done((f32[4,200,128]{2,1,0:T(8,128)S(1)}, f32[4,200,128]{2,1,0:T(8,128)S(1)}, u32[]{:S(2)}, u32[]{:S(2)}) %collective-permute-start.9) | collective-permute-done | bytes 409632 | tf_op jit(solution)/shard_map/ppermute | solution.py:147
  25.3 1.6 %collective-permute-start.10 = (f32[4,200,128]{2,1,0:T(8,128)S(1)}, f32[4,200,128]{2,1,0:T(8,128)S(1)}, u32[]{:S(2)}, u32[]{:S(2)}) collective-permute-start(f32[4,200,128]{2,1,0:T(8,128)S(1)} %add.125), channel_id=1, source_target_pairs={{0,2},{1,3},{2,0},{3,1},{4,6},{5,7},{6,4},{7,5},{8,10},{9,11},{10,... | collective-permute-start | bytes 1228808 | tf_op jit(solution)/shard_map/ppermute | solution.py:147
  26.9 0.7 %collective-permute-start.11 = (bf16[2,2,208,128]{3,2,1,0:T(8,128)(2,1)S(1)}, bf16[2,2,208,128]{3,2,1,0:T(8,128)(2,1)S(1)}, u32[]{:S(2)}, u32[]{:S(2)}) collective-permute-start(bf16[2,2,208,128]{3,2,1,0:T(8,128)(2,1)S(1)} %pad_maximum_fusion.1), channel_id=1, source_target_pairs={{0,4},{1,5},{2,6},{3,7},{4,0},{5,1},{6,2},{7,3},{8,12},{9,13},{10,... | collective-permute-start | bytes 638984 | tf_op jit(solution)/shard_map/ppermute | solution.py:147
  28.1 8.8 %collective-permute-done.10 = f32[4,200,128]{2,1,0:T(8,128)S(1)} collective-permute-done((f32[4,200,128]{2,1,0:T(8,128)S(1)}, f32[4,200,128]{2,1,0:T(8,128)S(1)}, u32[]{:S(2)}, u32[]{:S(2)}) %collective-permute-start.10) | collective-permute-done | bytes 409632 | tf_op jit(solution)/shard_map/ppermute | solution.py:147
  37.0 0.7 %collective-permute-start.12 = (f32[200,128]{1,0:T(8,128)S(1)}, f32[200,128]{1,0:T(8,128)S(1)}, u32[]{:S(2)}, u32[]{:S(2)}) collective-permute-start(f32[200,128]{1,0:T(8,128)S(1)} %get-tuple-element.43), channel_id=1, source_target_pairs={{0,4},{1,5},{2,6},{3,7},{4,0},{5,1},{6,2},{7,3},{8,12},{9,13},{10,... | collective-permute-start | bytes 307208 | tf_op jit(solution)/shard_map/ppermute | solution.py:147
  37.7 1.6 %collective-permute-start.13 = (f32[200,128]{1,0:T(8,128)S(1)}, f32[200,128]{1,0:T(8,128)S(1)}, u32[]{:S(2)}, u32[]{:S(2)}) collective-permute-start(f32[200,128]{1,0:T(8,128)S(1)} %get-tuple-element.48), channel_id=1, source_target_pairs={{0,8},{1,9},{2,10},{3,11},{4,12},{5,13},{6,14},{7,15},{8,0},{9,1},... | collective-permute-start | bytes 307208 | tf_op jit(solution)/shard_map/ppermute | solution.py:147
  39.3 2.2 %collective-permute-start.14 = (f32[200,128]{1,0:T(8,128)S(1)}, f32[200,128]{1,0:T(8,128)S(1)}, u32[]{:S(2)}, u32[]{:S(2)}) collective-permute-start(f32[200,128]{1,0:T(8,128)S(1)} %get-tuple-element.49), channel_id=1, source_target_pairs={{0,12},{1,13},{2,14},{3,15},{4,8},{5,9},{6,10},{7,11},{8,4},{9,5},... | collective-permute-start | bytes 307208 | tf_op jit(solution)/shard_map/ppermute | solution.py:147
  41.5 1.0 %collective-permute-done.12 = f32[200,128]{1,0:T(8,128)S(1)} collective-permute-done((f32[200,128]{1,0:T(8,128)S(1)}, f32[200,128]{1,0:T(8,128)S(1)}, u32[]{:S(2)}, u32[]{:S(2)}) %collective-permute-start.12) | collective-permute-done | bytes 102432 | tf_op jit(solution)/shard_map/ppermute | solution.py:147
  42.4 1.5 %collective-permute-start.16 = (bf16[4,2,208,128]{3,2,1,0:T(8,128)(2,1)S(1)}, bf16[4,2,208,128]{3,2,1,0:T(8,128)(2,1)S(1)}, u32[]{:S(2)}, u32[]{:S(2)}) collective-permute-start(bf16[4,2,208,128]{3,2,1,0:T(8,128)(2,1)S(1)} %pad_maximum_fusion.near_ref), channel_id=1, source_target_pairs={{0,2},{1,3},{2,0},{3,1},{4,6},{5,7},{6,4},{7,5},{8,10},{9,11},{10,... | collective-permute-start | bytes 1277960 | tf_op jit(solution)/shard_map/ppermute | solution.py:147
  43.9 4.0 %collective-permute-done.13 = f32[200,128]{1,0:T(8,128)S(1)} collective-permute-done((f32[200,128]{1,0:T(8,128)S(1)}, f32[200,128]{1,0:T(8,128)S(1)}, u32[]{:S(2)}, u32[]{:S(2)}) %collective-permute-start.13) | collective-permute-done | bytes 102432 | tf_op jit(solution)/shard_map/ppermute | solution.py:147
  47.9 1.5 %collective-permute-start.15 = (bf16[200,128]{1,0:T(8,128)(2,1)S(1)}, bf16[200,128]{1,0:T(8,128)(2,1)S(1)}, u32[]{:S(2)}, u32[]{:S(2)}) collective-permute-start(bf16[200,128]{1,0:T(8,128)(2,1)S(1)} %add_convert_fusion.refs_0_), channel_id=1, source_target_pairs={{0,12},{1,13},{2,14},{3,15},{4,8},{5,9},{6,10},{7,11},{8,4},{9,5},... | collective-permute-start | bytes 153608 | tf_op jit(solution)/shard_map/ppermute | solution.py:147
  49.4 0.9 %collective-permute-start.18 = (bf16[200,128]{1,0:T(8,128)(2,1)S(1)}, bf16[200,128]{1,0:T(8,128)(2,1)S(1)}, u32[]{:S(2)}, u32[]{:S(2)}) collective-permute-start(bf16[200,128]{1,0:T(8,128)(2,1)S(1)} %add_convert_fusion.refs_0_), channel_id=1, source_target_pairs={{0,4},{1,5},{2,6},{3,7},{4,0},{5,1},{6,2},{7,3},{8,12},{9,13},{10,... | collective-permute-start | bytes 153608 | tf_op jit(solution)/shard_map/ppermute | solution.py:147
  50.3 2.1 %collective-permute-start.20 = (bf16[200,128]{1,0:T(8,128)(2,1)S(1)}, bf16[200,128]{1,0:T(8,128)(2,1)S(1)}, u32[]{:S(2)}, u32[]{:S(2)}) collective-permute-start(bf16[200,128]{1,0:T(8,128)(2,1)S(1)} %add_convert_fusion.refs_0_), channel_id=1, source_target_pairs={{0,8},{1,9},{2,10},{3,11},{4,12},{5,13},{6,14},{7,15},{8,0},{9,1},... | collective-permute-start | bytes 153608 | tf_op jit(solution)/shard_map/ppermute | solution.py:147
  52.7 1.6 %collective-permute-start.17 = (bf16[200,128]{1,0:T(8,128)(2,1)S(1)}, bf16[200,128]{1,0:T(8,128)(2,1)S(1)}, u32[]{:S(2)}, u32[]{:S(2)}) collective-permute-start(bf16[200,128]{1,0:T(8,128)(2,1)S(1)} %add_convert_fusion.refs_0_), channel_id=1, source_target_pairs={{0,2},{1,3},{2,0},{3,1},{4,6},{5,7},{6,4},{7,5},{8,10},{9,11},{10,... | collective-permute-start | bytes 153608 | tf_op jit(solution)/shard_map/ppermute | solution.py:147
  54.3 1.3 %collective-permute-start.19 = (bf16[200,128]{1,0:T(8,128)(2,1)S(1)}, bf16[200,128]{1,0:T(8,128)(2,1)S(1)}, u32[]{:S(2)}, u32[]{:S(2)}) collective-permute-start(bf16[200,128]{1,0:T(8,128)(2,1)S(1)} %collective-permute-done.18.refs_2_), channel_id=1, source_target_pairs={{0,2},{1,3},{2,0},{3,1},{4,6},{5,7},{6,4},{7,5},{8,10},{9,11},{10,... | collective-permute-start | bytes 153608 | tf_op jit(solution)/shard_map/ppermute | solution.py:147
  55.6 1.2 %collective-permute-start.21 = (bf16[200,128]{1,0:T(8,128)(2,1)S(1)}, bf16[200,128]{1,0:T(8,128)(2,1)S(1)}, u32[]{:S(2)}, u32[]{:S(2)}) collective-permute-start(bf16[200,128]{1,0:T(8,128)(2,1)S(1)} %collective-permute-done.20.refs_4_), channel_id=1, source_target_pairs={{0,2},{1,3},{2,0},{3,1},{4,6},{5,7},{6,4},{7,5},{8,10},{9,11},{10,... | collective-permute-start | bytes 153608 | tf_op jit(solution)/shard_map/ppermute | solution.py:147
  56.8 0.9 %collective-permute-start.22 = (bf16[200,128]{1,0:T(8,128)(2,1)S(1)}, bf16[200,128]{1,0:T(8,128)(2,1)S(1)}, u32[]{:S(2)}, u32[]{:S(2)}) collective-permute-start(bf16[200,128]{1,0:T(8,128)(2,1)S(1)} %collective-permute-done.15.refs_6_), channel_id=1, source_target_pairs={{0,2},{1,3},{2,0},{3,1},{4,6},{5,7},{6,4},{7,5},{8,10},{9,11},{10,... | collective-permute-start | bytes 153608 | tf_op jit(solution)/shard_map/ppermute | solution.py:147
  57.9 1.2 %select_noise.1.noise_ref = f32[8,208,128]{2,1,0:T(8,128)S(1)} custom-call(s32[128]{0:T(128)S(1)} %reshape.83.starts_ref, bf16[4,2,208,128]{3,2,1,0:T(8,128)(2,1)S(1)} %pad_maximum_fusion.near_ref, bf16[4,2,208,128]{3,2,1,0:T(8,128)(2,1)S(1)} %collective-permute-done.16.far_ref), custom_call_target="tpu_custom_call" | custom-call | tf_op jit(solution)/shard_map/select_noise/pallas_call | solution.py:343
  59.8 1.2 %collective-permute-done.22.refs_7_ = bf16[200,128]{1,0:T(8,128)(2,1)S(1)} collective-permute-done((bf16[200,128]{1,0:T(8,128)(2,1)S(1)}, bf16[200,128]{1,0:T(8,128)(2,1)S(1)}, u32[]{:S(2)}, u32[]{:S(2)}) %collective-permute-start.22) | collective-permute-done | bytes 51232 | tf_op jit(solution)/shard_map/ppermute | solution.py:147
  60.9 1.9 %gram_and_cross.1.mine_ref = f32[208,512]{1,0:T(8,128)S(1)} custom-call(s32[8,128,1]{2,1,0:T(8,128)S(1)} %broadcast_add_fusion.target_ref, f32[8,208,128]{2,1,0:T(8,128)S(1)} %select_noise.1.noise_ref, bf16[200,128]{1,0:T(8,128)(2,1)S(1)} %add_convert_fusion.refs_0_, bf16[200,128]{1,0:T(8,128)(2,1)S(1)} %collective-permute-done.17.refs_1_, ...), custom_call_target="tpu_custom_call" | custom-call | tf_op jit(solution)/shard_map/gram_and_cross/pallas_call | solution.py:414
  62.9 1.8 %collective-permute-done.23.other_ref = f32[208,512]{1,0:T(8,128)S(1)} collective-permute-done((f32[208,512]{1,0:T(8,128)S(1)}, f32[208,512]{1,0:T(8,128)S(1)}, u32[]{:S(2)}, u32[]{:S(2)}) %collective-permute-start.23) | collective-permute-done | bytes 426016 | tf_op jit(solution)/shard_map/ppermute | solution.py:147
  64.6 7.7 %solve_and_update.1 = (bf16[200,12288]{1,0:T(8,128)(2,1)}, f32[200,200]{1,0:T(8,128)}, f32[1,256]{1,0:T(1,128)}) custom-call(f32[208,512]{1,0:T(8,128)S(1)} %gram_and_cross.1.mine_ref, f32[208,512]{1,0:T(8,128)S(1)} %collective-permute-done.23.other_ref, bf16[200,12288]{1,0:T(8,128)(2,1)} %slab_ref.1), custom_call_target="tpu_custom_call" | custom-call | tf_op jit(solution)/shard_map/solve_and_update/pallas_call | solution.py:522
  (51 shorter events, 4.8 us)
Async XLA Ops:
  1.4 5.7 %collective-permute-start.1 = (s32[32]{0:T(128)S(1)}, s32[32]{0:T(128)S(1)}, u32[]{:S(2)}, u32[]{:S(2)}) collective-permute-start(s32[32]{0:T(128)S(1)} %pad_add_fusion.2), channel_id=1, source_target_pairs={{0,1},{1,0},{2,3},{3,2},{4,5},{5,4},{6,7},{7,6},{8,9},{9,8},{10,11... | collective-permute-start | bytes 392 | tf_op jit(solution)/shard_map/ppermute | solution.py:147
  1.8 5.2 %collective-permute-start.2 = (s32[32]{0:T(128)S(1)}, s32[32]{0:T(128)S(1)}, u32[]{:S(2)}, u32[]{:S(2)}) collective-permute-start(s32[32]{0:T(128)S(1)} %pad_add_fusion.2), channel_id=1, source_target_pairs={{0,2},{1,3},{2,0},{3,1},{4,6},{5,7},{6,4},{7,5},{8,10},{9,11},{10,... | collective-permute-start | bytes 392 | tf_op jit(solution)/shard_map/ppermute | solution.py:147
  4.4 3.0 %collective-permute-start.3 = (s32[32]{0:T(128)S(1)}, s32[32]{0:T(128)S(1)}, u32[]{:S(2)}, u32[]{:S(2)}) collective-permute-start(s32[32]{0:T(128)S(1)} %pad_add_fusion.2), channel_id=1, source_target_pairs={{0,3},{1,2},{2,1},{3,0},{4,7},{5,6},{6,5},{7,4},{8,11},{9,10},{10,... | collective-permute-start | bytes 392 | tf_op jit(solution)/shard_map/ppermute | solution.py:147
  4.5 0.9 %copy-start.1 = (bf16[256,200]{0,1:T(8,128)(2,1)S(1)}, bf16[256,200]{0,1:T(8,128)(2,1)}, u32[]{:S(2)}) copy-start(bf16[256,200]{0,1:T(8,128)(2,1)} %param.13) | copy-start | bytes 307204
  5.4 0.7 copy-start.2
  6.0 0.7 copy-start.3
  6.9 1.3 %collective-permute-start = (bf16[208,128]{1,0:T(8,128)(2,1)S(1)}, bf16[208,128]{1,0:T(8,128)(2,1)S(1)}, u32[]{:S(2)}, u32[]{:S(2)}) collective-permute-start(bf16[208,128]{1,0:T(8,128)(2,1)S(1)} %get-tuple-element.30), channel_id=1, source_target_pairs={{0,1},{1,0},{2,3},{3,2},{4,5},{5,4},{6,7},{7,6},{8,9},{9,8},{10,11... | collective-permute-start | bytes 159752 | tf_op jit(solution)/shard_map/ppermute | solution.py:147
  8.2 11.0 %copy-start = (bf16[512,512]{1,0:T(8,128)(2,1)S(1)}, bf16[512,512]{1,0:T(8,128)(2,1)}, u32[]{:S(2)}) copy-start(bf16[512,512]{1,0:T(8,128)(2,1)} %constant.10.clone.table_w_ref.table_h_ref) | copy-start | bytes 1572868
  8.2 11.0 %collective-permute-start.7 = (bf16[2,208,128]{2,1,0:T(8,128)(2,1)S(1)}, bf16[2,208,128]{2,1,0:T(8,128)(2,1)S(1)}, u32[]{:S(2)}, u32[]{:S(2)}) collective-permute-start(bf16[2,208,128]{2,1,0:T(8,128)(2,1)S(1)} %pad_maximum_fusion.2), channel_id=1, source_target_pairs={{0,8},{1,9},{2,10},{3,11},{4,12},{5,13},{6,14},{7,15},{8,0},{9,1},... | collective-permute-start | bytes 319496 | tf_op jit(solution)/shard_map/ppermute | solution.py:147
  11.1 8.1 %collective-permute-start.4 = (s32[4,32]{1,0:T(4,128)S(1)}, s32[4,32]{1,0:T(4,128)S(1)}, u32[]{:S(2)}, u32[]{:S(2)}) collective-permute-start(s32[4,32]{1,0:T(4,128)S(1)} %pad_add_fusion.1.list0_ref), channel_id=1, source_target_pairs={{0,4},{1,5},{2,6},{3,7},{4,0},{5,1},{6,2},{7,3},{8,12},{9,13},{10,... | collective-permute-start | bytes 1544 | tf_op jit(solution)/shard_map/ppermute | solution.py:147
  12.7 6.5 %collective-permute-start.5 = (s32[4,32]{1,0:T(4,128)S(1)}, s32[4,32]{1,0:T(4,128)S(1)}, u32[]{:S(2)}, u32[]{:S(2)}) collective-permute-start(s32[4,32]{1,0:T(4,128)S(1)} %pad_add_fusion.1.list0_ref), channel_id=1, source_target_pairs={{0,8},{1,9},{2,10},{3,11},{4,12},{5,13},{6,14},{7,15},{8,0},{9,1},... | collective-permute-start | bytes 1544 | tf_op jit(solution)/shard_map/ppermute | solution.py:147
  13.0 6.2 %collective-permute-start.6 = (s32[4,32]{1,0:T(4,128)S(1)}, s32[4,32]{1,0:T(4,128)S(1)}, u32[]{:S(2)}, u32[]{:S(2)}) collective-permute-start(s32[4,32]{1,0:T(4,128)S(1)} %pad_add_fusion.1.list0_ref), channel_id=1, source_target_pairs={{0,12},{1,13},{2,14},{3,15},{4,8},{5,9},{6,10},{7,11},{8,4},{9,5},... | collective-permute-start | bytes 1544 | tf_op jit(solution)/shard_map/ppermute | solution.py:147
  23.5 1.8 %collective-permute-start.9 = (f32[4,200,128]{2,1,0:T(8,128)S(1)}, f32[4,200,128]{2,1,0:T(8,128)S(1)}, u32[]{:S(2)}, u32[]{:S(2)}) collective-permute-start(f32[4,200,128]{2,1,0:T(8,128)S(1)} %get-tuple-element.41), channel_id=1, source_target_pairs={{0,1},{1,0},{2,3},{3,2},{4,5},{5,4},{6,7},{7,6},{8,9},{9,8},{10,11... | collective-permute-start | bytes 1228808 | tf_op jit(solution)/shard_map/ppermute | solution.py:147
  23.6 4.4 %collective-permute-start.8 = (f32[4,200,128]{2,1,0:T(8,128)S(1)}, f32[4,200,128]{2,1,0:T(8,128)S(1)}, u32[]{:S(2)}, u32[]{:S(2)}) collective-permute-start(f32[4,200,128]{2,1,0:T(8,128)S(1)} %get-tuple-element.39), channel_id=1, source_target_pairs={{0,1},{1,0},{2,3},{3,2},{4,5},{5,4},{6,7},{7,6},{8,9},{9,8},{10,11... | collective-permute-start | bytes 1228808 | tf_op jit(solution)/shard_map/ppermute | solution.py:147
  25.3 11.6 %collective-permute-start.10 = (f32[4,200,128]{2,1,0:T(8,128)S(1)}, f32[4,200,128]{2,1,0:T(8,128)S(1)}, u32[]{:S(2)}, u32[]{:S(2)}) collective-permute-start(f32[4,200,128]{2,1,0:T(8,128)S(1)} %add.125), channel_id=1, source_target_pairs={{0,2},{1,3},{2,0},{3,1},{4,6},{5,7},{6,4},{7,5},{8,10},{9,11},{10,... | collective-permute-start | bytes 1228808 | tf_op jit(solution)/shard_map/ppermute | solution.py:147
  26.9 10.1 %collective-permute-start.11 = (bf16[2,2,208,128]{3,2,1,0:T(8,128)(2,1)S(1)}, bf16[2,2,208,128]{3,2,1,0:T(8,128)(2,1)S(1)}, u32[]{:S(2)}, u32[]{:S(2)}) collective-permute-start(bf16[2,2,208,128]{3,2,1,0:T(8,128)(2,1)S(1)} %pad_maximum_fusion.1), channel_id=1, source_target_pairs={{0,4},{1,5},{2,6},{3,7},{4,0},{5,1},{6,2},{7,3},{8,12},{9,13},{10,... | collective-permute-start | bytes 638984 | tf_op jit(solution)/shard_map/ppermute | solution.py:147
  37.0 5.5 %collective-permute-start.12 = (f32[200,128]{1,0:T(8,128)S(1)}, f32[200,128]{1,0:T(8,128)S(1)}, u32[]{:S(2)}, u32[]{:S(2)}) collective-permute-start(f32[200,128]{1,0:T(8,128)S(1)} %get-tuple-element.43), channel_id=1, source_target_pairs={{0,4},{1,5},{2,6},{3,7},{4,0},{5,1},{6,2},{7,3},{8,12},{9,13},{10,... | collective-permute-start | bytes 307208 | tf_op jit(solution)/shard_map/ppermute | solution.py:147
  37.7 10.2 %collective-permute-start.13 = (f32[200,128]{1,0:T(8,128)S(1)}, f32[200,128]{1,0:T(8,128)S(1)}, u32[]{:S(2)}, u32[]{:S(2)}) collective-permute-start(f32[200,128]{1,0:T(8,128)S(1)} %get-tuple-element.48), channel_id=1, source_target_pairs={{0,8},{1,9},{2,10},{3,11},{4,12},{5,13},{6,14},{7,15},{8,0},{9,1},... | collective-permute-start | bytes 307208 | tf_op jit(solution)/shard_map/ppermute | solution.py:147
  39.3 8.6 %collective-permute-start.14 = (f32[200,128]{1,0:T(8,128)S(1)}, f32[200,128]{1,0:T(8,128)S(1)}, u32[]{:S(2)}, u32[]{:S(2)}) collective-permute-start(f32[200,128]{1,0:T(8,128)S(1)} %get-tuple-element.49), channel_id=1, source_target_pairs={{0,12},{1,13},{2,14},{3,15},{4,8},{5,9},{6,10},{7,11},{8,4},{9,5},... | collective-permute-start | bytes 307208 | tf_op jit(solution)/shard_map/ppermute | solution.py:147
  42.4 14.4 %collective-permute-start.16 = (bf16[4,2,208,128]{3,2,1,0:T(8,128)(2,1)S(1)}, bf16[4,2,208,128]{3,2,1,0:T(8,128)(2,1)S(1)}, u32[]{:S(2)}, u32[]{:S(2)}) collective-permute-start(bf16[4,2,208,128]{3,2,1,0:T(8,128)(2,1)S(1)} %pad_maximum_fusion.near_ref), channel_id=1, source_target_pairs={{0,2},{1,3},{2,0},{3,1},{4,6},{5,7},{6,4},{7,5},{8,10},{9,11},{10,... | collective-permute-start | bytes 1277960 | tf_op jit(solution)/shard_map/ppermute | solution.py:147
  47.9 8.9 %collective-permute-start.15 = (bf16[200,128]{1,0:T(8,128)(2,1)S(1)}, bf16[200,128]{1,0:T(8,128)(2,1)S(1)}, u32[]{:S(2)}, u32[]{:S(2)}) collective-permute-start(bf16[200,128]{1,0:T(8,128)(2,1)S(1)} %add_convert_fusion.refs_0_), channel_id=1, source_target_pairs={{0,12},{1,13},{2,14},{3,15},{4,8},{5,9},{6,10},{7,11},{8,4},{9,5},... | collective-permute-start | bytes 153608 | tf_op jit(solution)/shard_map/ppermute | solution.py:147
  49.4 4.9 %collective-permute-start.18 = (bf16[200,128]{1,0:T(8,128)(2,1)S(1)}, bf16[200,128]{1,0:T(8,128)(2,1)S(1)}, u32[]{:S(2)}, u32[]{:S(2)}) collective-permute-start(bf16[200,128]{1,0:T(8,128)(2,1)S(1)} %add_convert_fusion.refs_0_), channel_id=1, source_target_pairs={{0,4},{1,5},{2,6},{3,7},{4,0},{5,1},{6,2},{7,3},{8,12},{9,13},{10,... | collective-permute-start | bytes 153608 | tf_op jit(solution)/shard_map/ppermute | solution.py:147
  50.3 5.3 %collective-permute-start.20 = (bf16[200,128]{1,0:T(8,128)(2,1)S(1)}, bf16[200,128]{1,0:T(8,128)(2,1)S(1)}, u32[]{:S(2)}, u32[]{:S(2)}) collective-permute-start(bf16[200,128]{1,0:T(8,128)(2,1)S(1)} %add_convert_fusion.refs_0_), channel_id=1, source_target_pairs={{0,8},{1,9},{2,10},{3,11},{4,12},{5,13},{6,14},{7,15},{8,0},{9,1},... | collective-permute-start | bytes 153608 | tf_op jit(solution)/shard_map/ppermute | solution.py:147
  52.7 6.4 %collective-permute-start.17 = (bf16[200,128]{1,0:T(8,128)(2,1)S(1)}, bf16[200,128]{1,0:T(8,128)(2,1)S(1)}, u32[]{:S(2)}, u32[]{:S(2)}) collective-permute-start(bf16[200,128]{1,0:T(8,128)(2,1)S(1)} %add_convert_fusion.refs_0_), channel_id=1, source_target_pairs={{0,2},{1,3},{2,0},{3,1},{4,6},{5,7},{6,4},{7,5},{8,10},{9,11},{10,... | collective-permute-start | bytes 153608 | tf_op jit(solution)/shard_map/ppermute | solution.py:147
  54.3 4.8 %collective-permute-start.19 = (bf16[200,128]{1,0:T(8,128)(2,1)S(1)}, bf16[200,128]{1,0:T(8,128)(2,1)S(1)}, u32[]{:S(2)}, u32[]{:S(2)}) collective-permute-start(bf16[200,128]{1,0:T(8,128)(2,1)S(1)} %collective-permute-done.18.refs_2_), channel_id=1, source_target_pairs={{0,2},{1,3},{2,0},{3,1},{4,6},{5,7},{6,4},{7,5},{8,10},{9,11},{10,... | collective-permute-start | bytes 153608 | tf_op jit(solution)/shard_map/ppermute | solution.py:147
  55.6 4.1 %collective-permute-start.21 = (bf16[200,128]{1,0:T(8,128)(2,1)S(1)}, bf16[200,128]{1,0:T(8,128)(2,1)S(1)}, u32[]{:S(2)}, u32[]{:S(2)}) collective-permute-start(bf16[200,128]{1,0:T(8,128)(2,1)S(1)} %collective-permute-done.20.refs_4_), channel_id=1, source_target_pairs={{0,2},{1,3},{2,0},{3,1},{4,6},{5,7},{6,4},{7,5},{8,10},{9,11},{10,... | collective-permute-start | bytes 153608 | tf_op jit(solution)/shard_map/ppermute | solution.py:147
  56.8 4.1 %collective-permute-start.22 = (bf16[200,128]{1,0:T(8,128)(2,1)S(1)}, bf16[200,128]{1,0:T(8,128)(2,1)S(1)}, u32[]{:S(2)}, u32[]{:S(2)}) collective-permute-start(bf16[200,128]{1,0:T(8,128)(2,1)S(1)} %collective-permute-done.15.refs_6_), channel_id=1, source_target_pairs={{0,2},{1,3},{2,0},{3,1},{4,6},{5,7},{6,4},{7,5},{8,10},{9,11},{10,... | collective-permute-start | bytes 153608 | tf_op jit(solution)/shard_map/ppermute | solution.py:147
  62.8 1.8 %collective-permute-start.23 = (f32[208,512]{1,0:T(8,128)S(1)}, f32[208,512]{1,0:T(8,128)S(1)}, u32[]{:S(2)}, u32[]{:S(2)}) collective-permute-start(f32[208,512]{1,0:T(8,128)S(1)} %gram_and_cross.1.mine_ref), channel_id=1, source_target_pairs={{0,1},{1,0},{2,3},{3,2},{4,5},{5,4},{6,7},{7,6},{8,9},{9,8},{10,11... | collective-permute-start | bytes 1277960 | tf_op jit(solution)/shard_map/ppermute | solution.py:147
